TPU v7x, 768 devices: a whole 4x8x12 slice. The times are simulated.
768 devices in a mesh: gx: 96 (over z, x, core), gy: 8 (over y).
Axes of the slice: x: 4, y: 8, z: 12, core: 2. Of those that a mesh axis runs over, the one named last changes fastest.
Arguments:
- blocks: float32 [6144, 64, 448], P(('gx', 'gy')), may hold values from -0.75 to 0.75
- neighbors: int32 [6144, 7], P(('gx', 'gy')), may hold values from 0 to 6143, as said below
- aggregate: int32 [6144], P(('gx', 'gy')), may hold values from 0 to 1535, as said below
- tentative: float32 [64, 393216], P(None, ('gx', 'gy')), may hold values from -0.75 to 0.75
- inv_diagonal: float32 [64, 393216], P(None, ('gx', 'gy')), may hold values from -0.75 to 0.75
- target: int32 [1536], P(('gx', 'gy')), may hold values from 0 to 7, as said below
Outputs:
- repart: float32 [393216, 640], P(('gx', 'gy'))
- anchor: int32 [6144], P(('gx', 'gy'))
Inputs may be any that keep to these rules, and one draw needn't show every extreme that they name: `neighbors`: row i lists i first, then 7 - 1 block columns j with 1 <= |j - i| <= 4 (repeats may occur next to the ends of the grid); the distance 4 occurs. Each block row belongs to an aggregate of its own device: i // 8 == aggregate[i] // 2; every aggregate holds one block row or more. `target`: the 2 coarse rows of one device name distinct positions; in each group of 8 consecutive devices one position is named by every device of the group.
All inputs are finite; a program needn't handle non-finite values.
Results may differ from a plain program's by a relative error of at most 0.0003.
Values sent between devices are 32-bit elements; how exact they have to be, the bound alone decides.
No kernel may reach another device: no remote copies, remote signals or barrier semaphores. Data moves between devices by JAX's collectives and lax.ppermute only.
A program may use at most 64 MiB of HBM per device.

v0:
```python
import jax
import jax.numpy as jnp
from jax import lax
from jax.sharding import PartitionSpec as P

BS = 64
K = 7
RB = 8
NA = 2
REACH = 4
AW = 640


OMEGA = 2.0 / 3.0
HIGHEST = lax.Precision.HIGHEST


def padded(shard, sides, width):
    for axis, dim in sides:
        devices, length = (lax.axis_size(axis), shard.shape[dim])
        up = [(i, (i + 1) % devices) for i in range(devices - 1)]
        down = [(j, i) for i, j in up]
        last = lax.slice_in_dim(shard, length - width, length, axis=dim)
        initial = lax.slice_in_dim(shard, 0, width, axis=dim)
        before = lax.ppermute(last, axis, up)
        after = lax.ppermute(initial, axis, down)
        shard = jnp.concatenate([before, shard, after], axis=dim)
    return shard


def smooth_rows(
    matrix, dinv_rows, tent_own, agg_own, near_index, tent_near, agg_near, agg_base, windows
):
    row_total = matrix.shape[0]
    block_size = matrix.shape[1]
    near_tent = tent_near[near_index]
    product = jnp.einsum("irkc,ikcs->ikrs", matrix, near_tent, precision=HIGHEST)
    columns = jnp.arange(windows, dtype=jnp.int32)
    placed = ((agg_near[near_index] - agg_base)[:, :, None] == columns[None, None, :]).astype(
        jnp.float32
    )
    summed = jnp.einsum("ikw,ikrs->irws", placed, product, precision=HIGHEST).reshape(
        row_total, block_size, windows * block_size
    )
    smoothed = jnp.einsum("irc,icp->irp", dinv_rows, summed, precision=HIGHEST)
    initial_hot = ((agg_own - agg_base)[:, None] == columns[None, :]).astype(jnp.float32)
    initial = jnp.einsum("iw,irs->irws", initial_hot, tent_own, precision=HIGHEST).reshape(
        row_total, block_size, windows * block_size
    )
    return initial - OMEGA * smoothed


def left_factors(matrix, near_index, own_prolong, frame_rows):
    slots = jnp.arange(frame_rows, dtype=jnp.int32)
    hits = (near_index[:, :, None] == slots[None, None, :]).astype(jnp.float32)
    placed_blocks = jnp.einsum("ikj,irks->ijrs", hits, matrix, precision=HIGHEST)
    return jnp.einsum("irp,ijrs->jps", own_prolong, placed_blocks, precision=HIGHEST)


def body(blocks, neighbors, aggregate, tentative, inv_diagonal, target):
    agg_cols = NA * BS
    device = lax.axis_index(("gx", "gy"))
    first_row = device * RB
    frame_rows = RB + 2 * REACH
    matrix = blocks.reshape(RB, BS, K, BS)
    own_tent = tentative.reshape(BS, RB, BS).transpose(1, 0, 2)
    own_dinv = inv_diagonal.reshape(BS, RB, BS).transpose(1, 0, 2)
    near_index = neighbors - first_row + REACH
    tent_ext = padded(tentative, ((("gx", "gy"), 1),), REACH * BS)
    agg_near = padded(aggregate, ((("gx", "gy"), 0),), REACH)
    tent_rows = tent_ext.reshape(BS, frame_rows, BS).transpose(1, 0, 2)
    own_prolong = smooth_rows(
        matrix,
        own_dinv,
        own_tent,
        aggregate,
        near_index,
        tent_rows,
        agg_near,
        (device - 1) * NA,
        3 * NA,
    )
    prolong_near = padded(own_prolong, ((("gx", "gy"), 0),), REACH)
    left = left_factors(matrix, near_index, own_prolong, frame_rows)
    lower_part = jnp.einsum("jps,jsq->pq", left[:REACH], prolong_near[:REACH], precision=HIGHEST)
    own_part = jnp.einsum("jps,jsq->pq", left[REACH : REACH + RB], own_prolong, precision=HIGHEST)
    upper_part = jnp.einsum(
        "jps,jsq->pq", left[REACH + RB :], prolong_near[REACH + RB :], precision=HIGHEST
    )
    coarse_part = (
        jnp.pad(lower_part, ((0, 0), (0, 2 * agg_cols)))
        + jnp.pad(own_part, ((0, 0), (agg_cols, agg_cols)))
        + jnp.pad(upper_part, ((0, 0), (2 * agg_cols, 0)))
    )
    edge_rows = jnp.concatenate([coarse_part[:agg_cols], coarse_part[2 * agg_cols :]], 0)
    arrived = padded(edge_rows, ((("gx", "gy"), 0),), agg_cols)
    from_lower = jnp.pad(arrived[:agg_cols, agg_cols:], ((0, 0), (0, agg_cols)))
    from_upper = jnp.pad(arrived[3 * agg_cols :, : 4 * agg_cols], ((0, 0), (agg_cols, 0)))
    coarse_band = coarse_part[agg_cols : 2 * agg_cols] + from_lower + from_upper
    group_size = lax.axis_size("gy")
    chosen = target[:, None] == jnp.arange(group_size, dtype=jnp.int32)[None, :]
    send_rows = jnp.einsum(
        "ug,ubq->gbq",
        chosen.astype(jnp.float32),
        coarse_band.reshape(NA, BS, AW),
        precision=HIGHEST,
    )
    coarse_ids = device * NA + jnp.arange(NA, dtype=jnp.int32) + 1
    send_ids = jnp.sum(chosen.astype(jnp.int32) * coarse_ids[:, None], axis=0) - 1
    got_rows, got_ids = (
        lax.all_to_all(send_rows, "gy", split_axis=0, concat_axis=0, tiled=True),
        lax.all_to_all(send_ids, "gy", split_axis=0, concat_axis=0, tiled=True),
    )
    return (got_rows.reshape(group_size * BS, AW), got_ids)


def solution(mesh):
    placed = (
        P(("gx", "gy"), None, None),
        P(("gx", "gy"), None),
        P(("gx", "gy")),
        P(None, ("gx", "gy")),
        P(None, ("gx", "gy")),
        P(("gx", "gy")),
    )
    return jax.shard_map(
        body,
        mesh=mesh,
        in_specs=placed,
        out_specs=(P(("gx", "gy"), None), P(("gx", "gy"))),
        check_vma=False,
    )
```

profile of v0, /device:TPU:7, one launch (start us, length us, event | category | flops | bytes accessed | tf_op | source)
XLA Modules:
  0.0 129.9 jit_solution(16381886931582539595)
XLA Ops:
  1.4 3.2 %collective-permute-start.2 = (s32[4]{0:T(128)S(1)}, s32[4]{0:T(128)S(1)}, u32[]{:S(2)}, u32[]{:S(2)}) collective-permute-start(s32[4]{0:T(128)S(1)} %get-tuple-element.10), channel_id=1, source_target_pairs={{0,1},{1,2},{2,3},{3,4},{4,5},{5,6},{6,7},{7,8},{8,9},{9,10},{10,1... | collective-permute-start | bytes 56 | tf_op jit(solution)/shard_map/ppermute | solution.py:25
  4.6 4.4 %collective-permute-start.3 = (s32[4]{0:T(128)S(1)}, s32[4]{0:T(128)S(1)}, u32[]{:S(2)}, u32[]{:S(2)}) collective-permute-start(s32[4]{0:T(128)S(1)} %get-tuple-element.11), channel_id=1, source_target_pairs={{1,0},{2,1},{3,2},{4,3},{5,4},{6,5},{7,6},{8,7},{9,8},{10,9},{11,1... | collective-permute-start | bytes 56 | tf_op jit(solution)/shard_map/ppermute | solution.py:26
  9.9 1.9 %collective-permute-start = (f32[64,256]{1,0:T(8,128)S(1)}, f32[64,256]{1,0:T(8,128)S(1)}, u32[]{:S(2)}, u32[]{:S(2)}) collective-permute-start(f32[64,256]{1,0:T(8,128)S(1)} %get-tuple-element.6), channel_id=1, source_target_pairs={{0,1},{1,2},{2,3},{3,4},{4,5},{5,6},{6,7},{7,8},{8,9},{9,10},{10,1... | collective-permute-start | bytes 196616 | tf_op jit(solution)/shard_map/ppermute | solution.py:25
  11.8 4.9 %collective-permute-start.1 = (f32[64,256]{1,0:T(8,128)S(1)}, f32[64,256]{1,0:T(8,128)S(1)}, u32[]{:S(2)}, u32[]{:S(2)}) collective-permute-start(f32[64,256]{1,0:T(8,128)S(1)} %get-tuple-element.7), channel_id=1, source_target_pairs={{1,0},{2,1},{3,2},{4,3},{5,4},{6,5},{7,6},{8,7},{9,8},{10,9},{11,1... | collective-permute-start | bytes 196616 | tf_op jit(solution)/shard_map/ppermute | solution.py:26
  18.5 1.6 %reshape.50 = f32[8,64,7,64]{3,2,1,0:T(8,128)S(1)} reshape(f32[8,64,448]{2,1,0:T(8,128)} %param.6) | data formatting | bytes 1835008 | tf_op jit(solution)/shard_map/reshape | solution.py:65
  20.3 1.6 %multiply_bitcast_fusion = f32[8,64,6,64]{3,2,1,0:T(8,128)} fusion(f32[8,64,64]{2,1,0:T(8,128)S(1)} %copy.34, f32[8,6]{1,0:T(8,128)S(1)} %fusion.37), kind=kLoop, calls=%fused_computation.4 | loop fusion | flops 196608 | bytes 917696 | tf_op jit(solution)/shard_map/iw,irs->irws/transpose | solution.py:47
  21.9 2.0 %reshape.52 = f32[8,64,384]{2,1,0:T(8,128)S(1)} reshape(f32[8,64,6,64]{3,2,1,0:T(8,128)} %multiply_bitcast_fusion) | data formatting | bytes 1572864 | tf_op jit(solution)/shard_map/reshape | solution.py:47
  24.7 4.1 %fusion.31 = f32[8,16,64,64]{3,1,2,0:T(8,128)} fusion(f32[8,64,7,64]{3,2,1,0:T(8,128)S(1)} %reshape.50, s32[8,7]{1,0:T(8,128)S(1)} %get-tuple-element.8), kind=kOutput, calls=%fused_computation.34 | convolution fusion | flops 44041088 | bytes 3014880 | tf_op jit(solution)/shard_map/ikj,irks->ijrs/dot_general | solution.py:56
  31.9 1.9 %gather_fusion = f32[56,64,64]{2,1,0:T(8,128)} fusion(f32[16,64,64]{2,1,0:T(8,128)S(1)} %bitcast.67, s32[1024]{0:T(1024)S(1)} %pad_clamp_fusion), kind=kCustom, calls=%fused_computation | custom fusion | bytes 1835232 | tf_op jit(solution)/shard_map/gather | solution.py:36
  33.8 6.0 %fusion.10 = f32[8,7,64,64]{2,3,1,0:T(8,128)} fusion(f32[8,7,64,64]{3,2,1,0:T(8,128)} %bitcast.68, f32[8,64,7,64]{3,2,1,0:T(8,128)S(1)} %reshape.50), kind=kOutput, calls=%fused_computation.14 | convolution fusion | flops 176160768 | bytes 2752512 | tf_op jit(solution)/shard_map/irkc,ikcs->ikrs/dot_general | solution.py:37
  39.8 2.9 %copy.38 = f32[8,7,64,64]{3,1,2,0:T(8,128)} copy(f32[8,7,64,64]{2,3,1,0:T(8,128)} %fusion.10) | data formatting | bytes 1835008 | tf_op jit(solution)/shard_map/irkc,ikcs->ikrs/dot_general | solution.py:37
  42.7 2.7 %convolution_bitcast_fusion = f32[8,64,6,64]{3,2,1,0:T(8,128)S(1)} fusion(f32[8,7,64,64]{3,1,2,0:T(8,128)} %copy.38, s32[8,7]{1,0:T(8,128)S(1)} %reshape.79), kind=kOutput, calls=%fused_computation.7 | convolution fusion | flops 16515408 | bytes 1704160 | tf_op jit(solution)/shard_map/ikw,ikrs->irws/dot_general | solution.py:42
  45.4 1.4 %reshape.54 = f32[8,64,384]{2,1,0:T(8,128)} reshape(f32[8,64,6,64]{3,2,1,0:T(8,128)S(1)} %convolution_bitcast_fusion) | data formatting | bytes 1572864 | tf_op jit(solution)/shard_map/reshape | solution.py:42
  46.8 2.1 %fusion.14 = f32[8,64,384]{2,1,0:T(8,128)S(1)} fusion(f32[8,64,384]{2,1,0:T(8,128)S(1)} %reshape.52, f32[8,64,384]{2,1,0:T(8,128)} %reshape.54, f32[64,8,64]{2,1,0:T(8,128)S(1)} %copy-done.2), kind=kOutput, calls=%fused_computation.17 | convolution fusion | flops 151388160 | bytes 2490368 | tf_op jit(solution)/shard_map/irc,icp->irp/dot_general | solution.py:45
  49.0 1.9 %collective-permute-start.4 = (f32[4,64,384]{2,1,0:T(8,128)S(1)}, f32[4,64,384]{2,1,0:T(8,128)S(1)}, u32[]{:S(2)}, u32[]{:S(2)}) collective-permute-start(f32[4,64,384]{2,1,0:T(8,128)S(1)} %get-tuple-element.4), channel_id=1, source_target_pairs={{0,1},{1,2},{2,3},{3,4},{4,5},{5,6},{6,7},{7,8},{8,9},{9,10},{10,1... | collective-permute-start | bytes 1179656 | tf_op jit(solution)/shard_map/ppermute | solution.py:25
  50.9 5.0 %collective-permute-start.5 = (f32[4,64,384]{2,1,0:T(8,128)S(1)}, f32[4,64,384]{2,1,0:T(8,128)S(1)}, u32[]{:S(2)}, u32[]{:S(2)}) collective-permute-start(f32[4,64,384]{2,1,0:T(8,128)S(1)} %get-tuple-element.5), channel_id=1, source_target_pairs={{1,0},{2,1},{3,2},{4,3},{5,4},{6,5},{7,6},{8,7},{9,8},{10,9},{11,1... | collective-permute-start | bytes 1179656 | tf_op jit(solution)/shard_map/ppermute | solution.py:26
  55.9 7.6 %fusion = f32[16,64,384,1]{2,1,3,0:T(8,128)S(1)} fusion(f32[8,16,64,64]{3,1,2,0:T(8,128)S(1)} %copy-done, f32[8,64,384]{2,1,0:T(8,128)S(1)} %fusion.14), kind=kOutput, calls=%fused_computation.2 | convolution fusion | flops 2415919104 | bytes 4456448 | tf_op jit(solution)/shard_map/irp,ijrs->jps/dot_general | solution.py:57
  63.5 1.5 %fusion.18 = f32[384,384]{1,0:T(8,128)S(1)} fusion(f32[8,64,384]{2,1,0:T(8,128)S(1)} %fusion.14, f32[16,64,384,1]{2,1,3,0:T(8,128)S(1)} %fusion), kind=kOutput, calls=%fused_computation.19 | convolution fusion | flops 905969664 | bytes 2949120 | tf_op jit(solution)/shard_map/jps,jsq->pq/dot_general | solution.py:86
  66.9 1.9 %collective-permute-start.6 = (f32[128,640]{1,0:T(8,128)S(1)}, f32[128,640]{1,0:T(8,128)S(1)}, u32[]{:S(2)}, u32[]{:S(2)}) collective-permute-start(f32[128,640]{1,0:T(8,128)S(1)} %get-tuple-element.2), channel_id=1, source_target_pairs={{0,1},{1,2},{2,3},{3,4},{4,5},{5,6},{6,7},{7,8},{8,9},{9,10},{10,1... | collective-permute-start | bytes 983048 | tf_op jit(solution)/shard_map/ppermute | solution.py:25
  68.8 4.9 %collective-permute-start.7 = (f32[128,640]{1,0:T(8,128)S(1)}, f32[128,640]{1,0:T(8,128)S(1)}, u32[]{:S(2)}, u32[]{:S(2)}) collective-permute-start(f32[128,640]{1,0:T(8,128)S(1)} %get-tuple-element.3), channel_id=1, source_target_pairs={{1,0},{2,1},{3,2},{4,3},{5,4},{6,5},{7,6},{8,7},{9,8},{10,9},{11,1... | collective-permute-start | bytes 983048 | tf_op jit(solution)/shard_map/ppermute | solution.py:26
  74.4 11.5 %all-to-all-start.1 = ((s32[8,1,1]{2,1,0:T(1,128)}), s32[8,1,1]{2,1,0:T(1,128)S(1)}, u32[]{:S(2)}, u32[]{:S(2)}) async-start(s32[8,1,1]{2,1,0:T(1,128)} %copy.43), calls=%async_computation.1 | async-start | bytes 8192 | tf_op jit(solution)/shard_map/all_to_all | solution.py:112
  88.4 4.0 %all-to-all-done.1 = s32[8,1,1]{2,1,0:T(1,128)S(1)} async-done(((s32[8,1,1]{2,1,0:T(1,128)}), s32[8,1,1]{2,1,0:T(1,128)S(1)}, u32[]{:S(2)}, u32[]{:S(2)}) %all-to-all-start.1) | async-done | bytes 64 | tf_op jit(solution)/shard_map/all_to_all | solution.py:112
  92.5 5.9 %all-to-all-start = ((f32[8,64,640]{2,1,0:T(8,128)}), f32[8,64,640]{2,1,0:T(8,128)S(1)}, u32[]{:S(2)}, u32[]{:S(2)}) async-start(f32[8,64,640]{2,1,0:T(8,128)} %copy.42), calls=%async_computation | async-start | bytes 2621440 | tf_op jit(solution)/shard_map/all_to_all | solution.py:111
  99.1 29.7 %all-to-all-done = f32[8,64,640]{2,1,0:T(8,128)S(1)} async-done(((f32[8,64,640]{2,1,0:T(8,128)}), f32[8,64,640]{2,1,0:T(8,128)S(1)}, u32[]{:S(2)}, u32[]{:S(2)}) %all-to-all-start) | async-done | bytes 1310752 | tf_op jit(solution)/shard_map/all_to_all | solution.py:111
  (53 shorter events, 14.5 us)
Async XLA Ops:
  1.4 27.3 %collective-permute-start.2 = (s32[4]{0:T(128)S(1)}, s32[4]{0:T(128)S(1)}, u32[]{:S(2)}, u32[]{:S(2)}) collective-permute-start(s32[4]{0:T(128)S(1)} %get-tuple-element.10), channel_id=1, source_target_pairs={{0,1},{1,2},{2,3},{3,4},{4,5},{5,6},{6,7},{7,8},{8,9},{9,10},{10,1... | collective-permute-start | bytes 56 | tf_op jit(solution)/shard_map/ppermute | solution.py:25
  4.6 24.1 %collective-permute-start.3 = (s32[4]{0:T(128)S(1)}, s32[4]{0:T(128)S(1)}, u32[]{:S(2)}, u32[]{:S(2)}) collective-permute-start(s32[4]{0:T(128)S(1)} %get-tuple-element.11), channel_id=1, source_target_pairs={{1,0},{2,1},{3,2},{4,3},{5,4},{6,5},{7,6},{8,7},{9,8},{10,9},{11,1... | collective-permute-start | bytes 56 | tf_op jit(solution)/shard_map/ppermute | solution.py:26
  9.9 10.3 %copy-start.4 = (s32[8]{0:T(128)S(1)}, s32[8]{0:T(128)}, u32[]{:S(2)}) copy-start(s32[8]{0:T(128)} %param.8) | copy-start | bytes 100
  9.9 19.8 %collective-permute-start = (f32[64,256]{1,0:T(8,128)S(1)}, f32[64,256]{1,0:T(8,128)S(1)}, u32[]{:S(2)}, u32[]{:S(2)}) collective-permute-start(f32[64,256]{1,0:T(8,128)S(1)} %get-tuple-element.6), channel_id=1, source_target_pairs={{0,1},{1,2},{2,3},{3,4},{4,5},{5,6},{6,7},{7,8},{8,9},{9,10},{10,1... | collective-permute-start | bytes 196616 | tf_op jit(solution)/shard_map/ppermute | solution.py:25
  11.8 17.9 %collective-permute-start.1 = (f32[64,256]{1,0:T(8,128)S(1)}, f32[64,256]{1,0:T(8,128)S(1)}, u32[]{:S(2)}, u32[]{:S(2)}) collective-permute-start(f32[64,256]{1,0:T(8,128)S(1)} %get-tuple-element.7), channel_id=1, source_target_pairs={{1,0},{2,1},{3,2},{4,3},{5,4},{6,5},{7,6},{8,7},{9,8},{10,9},{11,1... | collective-permute-start | bytes 196616 | tf_op jit(solution)/shard_map/ppermute | solution.py:26
  21.9 2.0 %copy-start.3 = (f32[64,512]{1,0:T(8,128)S(1)}, f32[64,512]{1,0:T(8,128)}, u32[]{:S(2)}) copy-start(f32[64,512]{1,0:T(8,128)} %param.10) | copy-start | bytes 393220
  28.8 0.9 copy-start.1
  45.4 1.4 %copy-start.2 = (f32[64,8,64]{2,1,0:T(8,128)S(1)}, f32[64,8,64]{2,1,0:T(8,128)}, u32[]{:S(2)}) copy-start(f32[64,8,64]{2,1,0:T(8,128)} %reshape.55) | copy-start | bytes 393220
  46.8 9.2 %copy-start = (f32[8,16,64,64]{3,1,2,0:T(8,128)S(1)}, f32[8,16,64,64]{3,1,2,0:T(8,128)}, u32[]{:S(2)}) copy-start(f32[8,16,64,64]{3,1,2,0:T(8,128)} %fusion.31) | copy-start | bytes 6291460
  49.0 16.0 %collective-permute-start.4 = (f32[4,64,384]{2,1,0:T(8,128)S(1)}, f32[4,64,384]{2,1,0:T(8,128)S(1)}, u32[]{:S(2)}, u32[]{:S(2)}) collective-permute-start(f32[4,64,384]{2,1,0:T(8,128)S(1)} %get-tuple-element.4), channel_id=1, source_target_pairs={{0,1},{1,2},{2,3},{3,4},{4,5},{5,6},{6,7},{7,8},{8,9},{9,10},{10,1... | collective-permute-start | bytes 1179656 | tf_op jit(solution)/shard_map/ppermute | solution.py:25
  50.9 15.0 %collective-permute-start.5 = (f32[4,64,384]{2,1,0:T(8,128)S(1)}, f32[4,64,384]{2,1,0:T(8,128)S(1)}, u32[]{:S(2)}, u32[]{:S(2)}) collective-permute-start(f32[4,64,384]{2,1,0:T(8,128)S(1)} %get-tuple-element.5), channel_id=1, source_target_pairs={{1,0},{2,1},{3,2},{4,3},{5,4},{6,5},{7,6},{8,7},{9,8},{10,9},{11,1... | collective-permute-start | bytes 1179656 | tf_op jit(solution)/shard_map/ppermute | solution.py:26
  66.7 7.0 %copy-start.5 = (s32[2]{0:T(128)S(1)}, s32[2]{0:T(128)}, u32[]{:S(2)}) copy-start(s32[2]{0:T(128)} %param.11) | copy-start | bytes 28
  66.9 19.1 %collective-permute-start.6 = (f32[128,640]{1,0:T(8,128)S(1)}, f32[128,640]{1,0:T(8,128)S(1)}, u32[]{:S(2)}, u32[]{:S(2)}) collective-permute-start(f32[128,640]{1,0:T(8,128)S(1)} %get-tuple-element.2), channel_id=1, source_target_pairs={{0,1},{1,2},{2,3},{3,4},{4,5},{5,6},{6,7},{7,8},{8,9},{9,10},{10,1... | collective-permute-start | bytes 983048 | tf_op jit(solution)/shard_map/ppermute | solution.py:25
  68.8 17.2 %collective-permute-start.7 = (f32[128,640]{1,0:T(8,128)S(1)}, f32[128,640]{1,0:T(8,128)S(1)}, u32[]{:S(2)}, u32[]{:S(2)}) collective-permute-start(f32[128,640]{1,0:T(8,128)S(1)} %get-tuple-element.3), channel_id=1, source_target_pairs={{1,0},{2,1},{3,2},{4,3},{5,4},{6,5},{7,6},{8,7},{9,8},{10,9},{11,1... | collective-permute-start | bytes 983048 | tf_op jit(solution)/shard_map/ppermute | solution.py:26
  74.4 18.0 %all-to-all-start.1 = ((s32[8,1,1]{2,1,0:T(1,128)}), s32[8,1,1]{2,1,0:T(1,128)S(1)}, u32[]{:S(2)}, u32[]{:S(2)}) async-start(s32[8,1,1]{2,1,0:T(1,128)} %copy.43), calls=%async_computation.1 | async-start | bytes 8192 | tf_op jit(solution)/shard_map/all_to_all | solution.py:112
  92.5 36.4 %all-to-all-start = ((f32[8,64,640]{2,1,0:T(8,128)}), f32[8,64,640]{2,1,0:T(8,128)S(1)}, u32[]{:S(2)}, u32[]{:S(2)}) async-start(f32[8,64,640]{2,1,0:T(8,128)} %copy.42), calls=%async_computation | async-start | bytes 2621440 | tf_op jit(solution)/shard_map/all_to_all | solution.py:111
where the time goes:
time: 131 us; the launch traced here: 130 us
  starting transfers between devices  45.5 us (35%)
  waiting for transfers between devices  33.8 us (26%)
  matrix products  26.6 us (20%)
  local copies, waits for them, and re-layouts  19.6 us (15%)
  other arithmetic  3.44 us (3%)
    all_to_all x1, waiting for transfers between devices, body(): lax.all_to_all(send_rows, 'gy', split_axis=0, concat_axis=0, tiled=True)  29.7 us
    ppermute x4, starting transfers between devices, padded(): after = lax.ppermute(initial, axis, down)  19.1 us
    all_to_all x1, starting transfers between devices, body(): lax.all_to_all(send_ids, 'gy', split_axis=0, concat_axis=0, tiled=True)  11.5 us
    ppermute x4, starting transfers between devices, padded(): before = lax.ppermute(last, axis, up)  8.95 us
    dot_general x1, matrix products, left_factors(): jnp.einsum('irp,ijrs->jps', own_prolong, placed_blocks, precision=HIGHEST)  7.57 us
    dot_general x1, matrix products, smooth_rows(): jnp.einsum('irkc,ikcs->ikrs', matrix, near_tent, precision=HIGHEST)  5.95 us
    all_to_all x1, starting transfers between devices, body(): lax.all_to_all(send_rows, 'gy', split_axis=0, concat_axis=0, tiled=True)  5.92 us
    dot_general x1, matrix products, left_factors(): jnp.einsum('ikj,irks->ijrs', hits, matrix, precision=HIGHEST)  4.08 us
  transfers between devices with their start and end apart: 10, of which 2 were waited for; matrix products, arithmetic and copies ran while one was open for 21% of the time, Pallas kernels for 0%

commit v1 on v0

v1 whole, which is shorter than its diff:
```python
import jax
import jax.numpy as jnp
from jax import lax
from jax.experimental import pallas as pl
from jax.experimental.pallas import tpu as pltpu
from jax.sharding import PartitionSpec as P

BS = 64
K = 7
RB = 8
NA = 2
AW = 640
HALF = 256
AGG = NA * BS
EDGE = 9 * BS + 8
SLOT = 5 * BS + 8
OMEGA = 2.0 / 3.0
F32 = jnp.float32
BF16 = jnp.bfloat16


def split(x):
    high = x.astype(BF16)
    return high, (x - high.astype(F32)).astype(BF16)


def dot3(a, b, side=1):
    def dot(x, y):
        return lax.dot_general(x, y, (((side,), (0,)), ((), ())), preferred_element_type=F32)

    return dot(a[0], b[0]) + (dot(a[0], b[1]) + dot(a[1], b[0]))


def lane_half(rows):
    return lax.broadcasted_iota(jnp.int32, (rows, 2 * BS), 1) // BS


def doubled(pair):
    low = lane_half(BS) == 0
    other = pltpu.roll(pair, BS, 1)
    return jnp.where(low, pair, other), jnp.where(low, other, pair)


def place(pairs, members):
    half = lane_half(BS)
    rows = []
    for p, pair in enumerate(pairs):
        for q, block in enumerate(doubled(pair)):
            rows.append(jnp.where(half == members[2 * p + q], block, 0.0))
    return jnp.concatenate(rows, 0)


def block_diagonal(low, high):
    tall = jnp.concatenate([jnp.concatenate([low, high], 1)] * 4, 0)
    row = lax.broadcasted_iota(jnp.int32, tall.shape, 0) // BS
    column = lax.broadcasted_iota(jnp.int32, tall.shape, 1) // BS
    return jnp.where(row == column, tall, 0.0)


def piece(ref, c):
    return ref[c * BS : (c + 1) * BS]


def received_members(ref):
    return [ref[9 * BS + m : 9 * BS + m + 1].astype(jnp.int32) for m in range(4)]


def received_place(ref):
    return place([piece(ref, 0), piece(ref, 1)], received_members(ref))


def frame_columns(frame, first, columns):
    return jnp.concatenate([frame[first : first + 4, c].reshape(HALF, 2 * BS) for c in columns], 1)


def frame_kernel(nbr, agg, blocks, tent, dinv, frame, up, down):
    first = nbr[0, 0]
    half = lane_half(BS)
    for i in range(RB):
        origin = first - 4 if i < 4 else first
        mine = i + 4 if i < 4 else i
        copies = []
        for p in range(3):
            copies.extend(doubled(blocks[i, :, 2 * p * BS : 2 * (p + 1) * BS]))
        last = blocks[i, :, 6 * BS : 7 * BS]
        copies.append(jnp.concatenate([last, last], 1))
        for c in range(6):
            if c == mine // 2:
                frame[i, c] = jnp.where(half == mine % 2, copies[0], 0.0)
            else:
                frame[i, c] = jnp.zeros((BS, 2 * BS), F32)
        for k in range(1, K):
            at = nbr[i, k] - origin
            column = at >> 1
            frame[i, column] = frame[i, column] + jnp.where(half == (at & 1), copies[k], 0.0)

    def send(out, pieces, members):
        for c, value in enumerate(pieces):
            out[c * BS : (c + 1) * BS] = value
        row = lax.broadcasted_iota(jnp.int32, (8, 2 * BS), 0)
        value = jnp.zeros((8, 2 * BS), F32)
        for m, member in enumerate(members):
            value = jnp.where(row == m, member.astype(F32), value)
        out[9 * BS :] = value

    owner = first // 4
    low = half == 0
    send(
        up,
        [tent[:, 256:384], tent[:, 384:512], dinv[:, 256:384], dinv[:, 384:512]]
        + [frame[7, 4], frame[7, 5], frame[6, 4]]
        + [jnp.where(low, frame[6, 5], pltpu.roll(frame[4, 4], BS, 1)), frame[5, 4]],
        [agg[4 + m] - owner for m in range(4)],
    )
    send(
        down,
        [tent[:, 0:128], tent[:, 128:256], dinv[:, 0:128], dinv[:, 128:256]]
        + [frame[0, 0], frame[0, 1]]
        + [jnp.where(low, pltpu.roll(frame[3, 1], BS, 1), frame[1, 0]), frame[1, 1], frame[2, 1]],
        [agg[m] - owner for m in range(4)],
    )


def own_kernel(nbr, agg, frame, tent, dinv, a_high, a_low, near, factors, own, image):
    owner = nbr[0, 0] // 4
    a = split(
        jnp.concatenate(
            [frame_columns(frame, 0, range(2, 6)), frame_columns(frame, 4, range(0, 4))], 0
        )
    )
    a_high[...], a_low[...] = a
    placed = place(
        [tent[:, 2 * p * BS : 2 * (p + 1) * BS] for p in range(4)],
        [agg[j] - owner for j in range(RB)],
    )
    near[...] = placed
    summed = dot3(a, split(placed))
    parts = []
    for s, columns in ((0, (0, 1)), (1, (4, 5))):
        rows = slice(s * HALF, (s + 1) * HALF)
        inverse = split(
            block_diagonal(
                dinv[:, s * HALF : s * HALF + 128], dinv[:, s * HALF + 128 : (s + 1) * HALF]
            )
        )
        parts.append(placed[rows] - OMEGA * dot3(inverse, split(summed[rows])))
        factors[s] = -OMEGA * dot3(inverse, split(frame_columns(frame, 4 * s, columns)))
    prolong = jnp.concatenate(parts, 0)
    own[...] = prolong
    image[...] = dot3(a, split(prolong))


def edge_kernel(a_high, a_low, factors, own, image, below, above, side, left, right, up, down):
    b_low = dot3(split(factors[0]), split(received_place(below)))
    b_high = dot3(split(factors[1]), split(received_place(above)))
    side[:HALF] = b_low
    side[HALF:] = b_high
    b_low, b_high = split(b_low), split(b_high)
    image_left = dot3((a_high[:, :HALF], a_low[:, :HALF]), b_low)
    image_right = dot3((a_high[:, HALF:], a_low[:, HALF:]), b_high)
    left[...] = image_left
    right[...] = image_right
    for out, factor, rows in ((down, b_low, slice(0, HALF)), (up, b_high, slice(HALF, 2 * HALF))):
        terms = dot3(
            factor,
            split(jnp.concatenate([image_left[rows], image[rows], image_right[rows]], 1)),
            0,
        )
        for c in range(3):
            out[c * AGG : (c + 1) * AGG] = terms[:, c * AGG : (c + 1) * AGG]
        out[3 * AGG :] = own[rows]


def middle_kernel(frame, near, own, image, side, left, right, below, above, part, lo, hi):
    own_low, own_high = own[:HALF], own[HALF:]
    c_low, c_high = split(own_low), split(own_high)
    middle = dot3(
        split(own[...]), split(jnp.concatenate([left[...], image[...], right[...]], 1)), 0
    )
    low = lane_half(BS) == 0
    none = jnp.zeros((BS, 2 * BS), F32)

    def square(rows):
        return split(jnp.concatenate([jnp.concatenate(row, 1) for row in rows], 0))

    seven = piece(below, 7)
    a_below = square(
        [
            [jnp.where(low, pltpu.roll(seven, BS, 1), 0.0), none],
            [piece(below, 8), none],
            [piece(below, 6), jnp.where(low, seven, 0.0)],
            [piece(below, 4), piece(below, 5)],
        ]
    )
    six = piece(above, 6)
    a_above = square(
        [
            [piece(above, 4), piece(above, 5)],
            [jnp.where(low, 0.0, six), piece(above, 7)],
            [none, piece(above, 8)],
            [none, jnp.where(low, 0.0, pltpu.roll(six, BS, 1))],
        ]
    )
    inverse = split(block_diagonal(piece(below, 2), piece(below, 3)))
    b_below = split(
        -OMEGA * dot3(inverse, split(dot3(a_below, split(near[:HALF]))))
    )
    inverse = split(block_diagonal(piece(above, 2), piece(above, 3)))
    b_above = split(
        -OMEGA * dot3(inverse, split(dot3(a_above, split(near[HALF:]))))
    )
    x_low = dot3(
        b_below, split(dot3(a_below, split(jnp.concatenate([side[:HALF], own_low], 1)))), 0
    )
    x_high = dot3(
        b_above, split(dot3(a_above, split(jnp.concatenate([own_high, side[HALF:]], 1)))), 0
    )
    t_low = dot3(c_low, split(frame_columns(frame, 0, (0, 1))), 0)
    t_high = dot3(c_high, split(frame_columns(frame, 4, (4, 5))), 0)
    lo[...] = t_low
    hi[...] = t_high
    part[:, :AGG] = middle[:, :AGG] + x_low[:, :AGG]
    part[:, AGG : 2 * AGG] = (
        middle[:, AGG : 2 * AGG]
        + (x_low[:, AGG:] + dot3(split(t_low), b_below))
        + (x_high[:, :AGG] + dot3(split(t_high), b_above))
    )
    part[:, 2 * AGG :] = middle[:, 2 * AGG :] + x_high[:, AGG:]


def finish_kernel(nbr, target, part, lo, hi, below, above, out):
    first_id = nbr[0, 0] // 4
    band = [
        below[:AGG],
        part[:, :AGG]
        + below[AGG : 2 * AGG]
        + dot3(split(lo[...]), split(below[3 * AGG :])),
        part[:, AGG : 2 * AGG] + below[2 * AGG : 3 * AGG] + above[:AGG],
        part[:, 2 * AGG :]
        + above[AGG : 2 * AGG]
        + dot3(split(hi[...]), split(above[3 * AGG :])),
        above[2 * AGG : 3 * AGG],
    ]
    for g in range(RB):
        out[g] = jnp.zeros((SLOT, 2 * BS), F32)
    for u in range(NA):
        g = target[u]
        for c in range(5):
            out[g, c * BS : (c + 1) * BS] = band[c][u * BS : (u + 1) * BS]
        out[g, 5 * BS :] = jnp.full((8, 2 * BS), first_id + (u + 1), jnp.int32).astype(F32)


def unpack_kernel(got, rows, ids):
    lane = lax.broadcasted_iota(jnp.int32, (1, 2 * BS), 1)
    found = jnp.zeros((1, 2 * BS), F32)
    for s in range(RB):
        for c in range(5):
            rows[s * BS : (s + 1) * BS, c * 128 : (c + 1) * 128] = got[s, c * BS : (c + 1) * BS]
        found = jnp.where(lane == s, got[s, 5 * BS : 5 * BS + 1], found)
    ids[...] = found.astype(jnp.int32) - 1


VMEM = pl.BlockSpec(memory_space=pltpu.VMEM)
SMEM = pl.BlockSpec(memory_space=pltpu.SMEM)


def call(kernel, scalars, arrays, outs):
    return pl.pallas_call(
        kernel,
        in_specs=[SMEM] * len(scalars) + [VMEM] * len(arrays),
        out_specs=[VMEM] * len(outs),
        out_shape=[jax.ShapeDtypeStruct(shape, dtype) for shape, dtype in outs],
        compiler_params=pltpu.CompilerParams(vmem_limit_bytes=32 * 1024 * 1024),
        name=kernel.__name__,
    )(*scalars, *arrays)


def body(blocks, neighbors, aggregate, tentative, inv_diagonal, target):
    axes = ("gx", "gy")
    devices = lax.axis_size(axes)
    upward = [(i, i + 1) for i in range(devices - 1)]
    downward = [(j, i) for i, j in upward]
    frame, up, down = call(
        frame_kernel,
        [neighbors, aggregate],
        [blocks, tentative, inv_diagonal],
        [((RB, 6, BS, 2 * BS), F32), ((EDGE, 2 * BS), F32), ((EDGE, 2 * BS), F32)],
    )
    below = lax.ppermute(up, axes, upward)
    above = lax.ppermute(down, axes, downward)
    a_high, a_low, near, factors, own, image = call(
        own_kernel,
        [neighbors, aggregate],
        [frame, tentative, inv_diagonal],
        [
            ((2 * HALF, 2 * HALF), BF16),
            ((2 * HALF, 2 * HALF), BF16),
            ((2 * HALF, AGG), F32),
            ((2, HALF, HALF), F32),
            ((2 * HALF, AGG), F32),
            ((2 * HALF, AGG), F32),
        ],
    )
    side, left, right, up, down = call(
        edge_kernel,
        [],
        [a_high, a_low, factors, own, image, below, above],
        [((2 * HALF, AGG), F32)] * 3 + [((5 * AGG, AGG), F32)] * 2,
    )
    below_terms = lax.ppermute(up, axes, upward)
    above_terms = lax.ppermute(down, axes, downward)
    part, lo, hi = call(
        middle_kernel,
        [],
        [frame, near, own, image, side, left, right, below, above],
        [((AGG, 3 * AGG), F32), ((AGG, HALF), F32), ((AGG, HALF), F32)],
    )
    (slots,) = call(
        finish_kernel,
        [neighbors, target],
        [part, lo, hi, below_terms, above_terms],
        [((RB, SLOT, 2 * BS), F32)],
    )
    got = lax.all_to_all(slots, "gy", split_axis=0, concat_axis=0, tiled=True)
    rows, ids = call(
        unpack_kernel,
        [],
        [got],
        [((RB * BS, AW), F32), ((1, 2 * BS), jnp.int32)],
    )
    return rows, ids[0, :RB]


def solution(mesh):
    placed = (
        P(("gx", "gy"), None, None),
        P(("gx", "gy"), None),
        P(("gx", "gy")),
        P(None, ("gx", "gy")),
        P(None, ("gx", "gy")),
        P(("gx", "gy")),
    )
    return jax.shard_map(
        body,
        mesh=mesh,
        in_specs=placed,
        out_specs=(P(("gx", "gy"), None), P(("gx", "gy"))),
        check_vma=False,
    )
```

time: 131 us -> 81.1 us (0.62)
  the two profiles are of different devices: /device:TPU:7 before, /device:TPU:199 now
where the time goes in v1:
time: 81.1 us; the launch traced here: 80.7 us
  blocking collectives  43.1 us (53%)
  starting transfers between devices  15.1 us (19%)
  Pallas kernels  9.63 us (12%)
  waiting for transfers between devices  7.32 us (9%)
  local copies, waits for them, and re-layouts  4.88 us (6%)
    all_to_all x1, blocking collectives, body(): got = lax.all_to_all(slots, 'gy', split_axis=0, concat_axis=0, tiled=True)  43.1 us
    pallas_call x6, Pallas kernels, call(): pl.pallas_call(kernel, in_specs=[SMEM] * len(scalars) + [VMEM] * len(arra...  9.63 us
    ppermute x1, starting transfers between devices, body(): above_terms = lax.ppermute(down, axes, downward)  5.11 us
    unnamed x12, local copies, waits for them, and re-layouts  4.37 us
    ppermute x1, starting transfers between devices, body(): above = lax.ppermute(down, axes, downward)  4.37 us
    ppermute x1, waiting for transfers between devices, body(): below_terms = lax.ppermute(up, axes, upward)  4.3 us
    ppermute x1, starting transfers between devices, body(): below = lax.ppermute(up, axes, upward)  3.21 us
    ppermute x1, waiting for transfers between devices, body(): below = lax.ppermute(up, axes, upward)  2.98 us
  transfers between devices with their start and end apart: 4, of which 2 were waited for; matrix products, arithmetic and copies ran while one was open for 0% of the time, Pallas kernels for 6%

profile of v1, /device:TPU:199, one launch (start us, length us, event | category | flops | bytes accessed | tf_op | source)
XLA Modules:
  0.0 80.7 jit_solution(18425007462560611971)
XLA Ops:
  0.6 0.0 copy-start
  0.6 1.2 %copy-done = f32[8,64,448]{2,1,0:T(8,128)S(1)} copy-done((f32[8,64,448]{2,1,0:T(8,128)S(1)}, f32[8,64,448]{2,1,0:T(8,128)}, u32[]{:S(2)}) %copy-start) | copy-done | bytes 917528
  1.9 0.9 %copy-done.1 = f32[64,512]{1,0:T(8,128)S(1)} copy-done((f32[64,512]{1,0:T(8,128)S(1)}, f32[64,512]{1,0:T(8,128)}, u32[]{:S(2)}) %copy-start.1) | copy-done | bytes 131096
  2.8 0.9 %copy-done.2 = f32[64,512]{1,0:T(8,128)S(1)} copy-done((f32[64,512]{1,0:T(8,128)S(1)}, f32[64,512]{1,0:T(8,128)}, u32[]{:S(2)}) %copy-start.2) | copy-done | bytes 131096
  3.7 0.7 copy-done.3
  4.4 0.7 copy-done.4
  5.0 1.2 %frame_kernel.1 = (f32[8,6,64,128]{3,2,1,0:T(8,128)S(1)}, f32[584,128]{1,0:T(8,128)S(1)}, f32[584,128]{1,0:T(8,128)S(1)}) custom-call(s32[8,7]{1,0:T(8,128)S(1)} %copy-done.3, s32[8]{0:T(128)S(1)} %copy-done.4, f32[8,64,448]{2,1,0:T(8,128)S(1)} %copy-done, f32[64,512]{1,0:T(8,128)S(1)} %copy-done.1, f32[64,512]{1,0:T(8,128)S(1)} %copy-done.2), custom_call_target="tpu_custom_call" | custom-call | tf_op jit(solution)/shard_map/frame_kernel/pallas_call | solution.py:268
  6.2 3.2 %collective-permute-start = (f32[584,128]{1,0:T(8,128)S(1)}, f32[584,128]{1,0:T(8,128)S(1)}, u32[]{:S(2)}, u32[]{:S(2)}) collective-permute-start(f32[584,128]{1,0:T(8,128)S(1)} %get-tuple-element.28), channel_id=1, source_target_pairs={{0,1},{1,2},{2,3},{3,4},{4,5},{5,6},{6,7},{7,8},{8,9},{9,10},{10,1... | collective-permute-start | bytes 897032 | tf_op jit(solution)/shard_map/ppermute | solution.py:289
  9.4 4.4 %collective-permute-start.1 = (f32[584,128]{1,0:T(8,128)S(1)}, f32[584,128]{1,0:T(8,128)S(1)}, u32[]{:S(2)}, u32[]{:S(2)}) collective-permute-start(f32[584,128]{1,0:T(8,128)S(1)} %get-tuple-element.29), channel_id=1, source_target_pairs={{1,0},{2,1},{3,2},{4,3},{5,4},{6,5},{7,6},{8,7},{9,8},{10,9},{11,1... | collective-permute-start | bytes 897032 | tf_op jit(solution)/shard_map/ppermute | solution.py:290
  13.8 2.9 %own_kernel.1 = (bf16[512,512]{1,0:T(8,128)(2,1)S(1)}, bf16[512,512]{1,0:T(8,128)(2,1)S(1)}, f32[512,128]{1,0:T(8,128)S(1)}, f32[2,256,256]{2,1,0:T(8,128)S(1)},...) custom-call(s32[8,7]{1,0:T(8,128)S(1)} %copy-done.3, s32[8]{0:T(128)S(1)} %copy-done.4, ...), custom_call_target="tpu_custom_call" | custom-call | tf_op jit(solution)/shard_map/own_kernel/pallas_call | solution.py:268
  16.7 3.0 %collective-permute-done.below = f32[584,128]{1,0:T(8,128)S(1)} collective-permute-done((f32[584,128]{1,0:T(8,128)S(1)}, f32[584,128]{1,0:T(8,128)S(1)}, u32[]{:S(2)}, u32[]{:S(2)}) %collective-permute-start) | collective-permute-done | bytes 299040 | tf_op jit(solution)/shard_map/ppermute | solution.py:289
  19.7 0.0 collective-permute-done.1.above
  19.7 1.2 %edge_kernel.1 = (f32[512,128]{1,0:T(8,128)S(1)}, f32[512,128]{1,0:T(8,128)S(1)}, f32[512,128]{1,0:T(8,128)S(1)}, f32[640,128]{1,0:T(8,128)S(1)}, f32[640,128]{1,0:T(8,128)S(1)}) custom-call(bf16[512,512]{1,0:T(8,128)(2,1)S(1)} %get-tuple-element.25.a_high, bf16[512,512]{1,0:T(8,128)(2,1)S(1)} %get-tuple-element.26.a_low, ...), custom_call_target="tpu_custom_call" | custom-call | tf_op jit(solution)/shard_map/edge_kernel/pallas_call | solution.py:268
  21.0 2.4 %collective-permute-start.2 = (f32[640,128]{1,0:T(8,128)S(1)}, f32[640,128]{1,0:T(8,128)S(1)}, u32[]{:S(2)}, u32[]{:S(2)}) collective-permute-start(f32[640,128]{1,0:T(8,128)S(1)} %get-tuple-element.36), channel_id=1, source_target_pairs={{0,1},{1,2},{2,3},{3,4},{4,5},{5,6},{6,7},{7,8},{8,9},{9,10},{10,1... | collective-permute-start | bytes 983048 | tf_op jit(solution)/shard_map/ppermute | solution.py:310
  23.4 5.1 %collective-permute-start.3 = (f32[640,128]{1,0:T(8,128)S(1)}, f32[640,128]{1,0:T(8,128)S(1)}, u32[]{:S(2)}, u32[]{:S(2)}) collective-permute-start(f32[640,128]{1,0:T(8,128)S(1)} %get-tuple-element.37), channel_id=1, source_target_pairs={{1,0},{2,1},{3,2},{4,3},{5,4},{6,5},{7,6},{8,7},{9,8},{10,9},{11,1... | collective-permute-start | bytes 983048 | tf_op jit(solution)/shard_map/ppermute | solution.py:311
  28.5 0.0 copy-start.5
  28.5 2.3 %middle_kernel.1 = (f32[128,384]{1,0:T(8,128)S(1)}, f32[128,256]{1,0:T(8,128)S(1)}, f32[128,256]{1,0:T(8,128)S(1)}) custom-call(f32[8,6,64,128]{3,2,1,0:T(8,128)S(1)} %get-tuple-element.21.frame, f32[512,128]{1,0:T(8,128)S(1)} %get-tuple-element.22.near, f32[512,128]{1,0:T(8,128)S(1)} %get-tuple-element.23.own, f32[512,128]{1,0:T(8,128)S(1)} %get-tuple-element.24.image, ...), custom_call_target="tpu_custom_call" | custom-call | tf_op jit(solution)/shard_map/middle_kernel/pallas_call | solution.py:268
  30.8 4.3 %collective-permute-done.2.below = f32[640,128]{1,0:T(8,128)S(1)} collective-permute-done((f32[640,128]{1,0:T(8,128)S(1)}, f32[640,128]{1,0:T(8,128)S(1)}, u32[]{:S(2)}, u32[]{:S(2)}) %collective-permute-start.2) | collective-permute-done | bytes 327712 | tf_op jit(solution)/shard_map/ppermute | solution.py:310
  35.1 0.0 collective-permute-done.3.above
  35.1 0.0 copy-done.5
  35.1 0.9 %finish_kernel.1 = f32[8,328,128]{2,1,0:T(8,128)S(1)} custom-call(s32[8,7]{1,0:T(8,128)S(1)} %copy-done.3, s32[2]{0:T(128)S(1)} %copy-done.5, f32[128,384]{1,0:T(8,128)S(1)} %get-tuple-element.33.part, f32[128,256]{1,0:T(8,128)S(1)} %get-tuple-element.34.lo, f32[128,256]{1,0:T(8,128)S(1)} %get-tuple-element.35.hi, ...), custom_call_target="tpu_custom_call" | custom-call | tf_op jit(solution)/shard_map/finish_kernel/pallas_call | solution.py:268
  36.0 43.1 %all_to_all.5.got = f32[8,328,128]{2,1,0:T(8,128)S(1)} all-to-all(f32[8,328,128]{2,1,0:T(8,128)S(1)} %finish_kernel.1), channel_id=1, replica_groups=mesh['gx'=96,'gy'=8] {'gy'}, dimensions={0} | all-to-all | bytes 2686976 | tf_op jit(solution)/shard_map/all_to_all | solution.py:324
  79.1 1.1 %unpack_kernel.1 = (f32[512,640]{1,0:T(8,128)}, s32[1,128]{1,0:T(1,128)S(1)}) custom-call(f32[8,328,128]{2,1,0:T(8,128)S(1)} %all_to_all.5.got), custom_call_target="tpu_custom_call" | custom-call | tf_op jit(solution)/shard_map/unpack_kernel/pallas_call | solution.py:268
  80.2 0.5 slice_bitcast_fusion
  (4 shorter events, 0.0 us)
Async XLA Ops:
  0.6 1.2 %copy-start = (f32[8,64,448]{2,1,0:T(8,128)S(1)}, f32[8,64,448]{2,1,0:T(8,128)}, u32[]{:S(2)}) copy-start(f32[8,64,448]{2,1,0:T(8,128)} %blocks.1) | copy-start | bytes 2752516
  1.9 0.9 %copy-start.1 = (f32[64,512]{1,0:T(8,128)S(1)}, f32[64,512]{1,0:T(8,128)}, u32[]{:S(2)}) copy-start(f32[64,512]{1,0:T(8,128)} %tent.3) | copy-start | bytes 393220
  2.8 0.9 %copy-start.2 = (f32[64,512]{1,0:T(8,128)S(1)}, f32[64,512]{1,0:T(8,128)}, u32[]{:S(2)}) copy-start(f32[64,512]{1,0:T(8,128)} %dinv.3) | copy-start | bytes 393220
  3.7 0.7 copy-start.3
  4.4 0.7 copy-start.4
  6.2 13.5 %collective-permute-start = (f32[584,128]{1,0:T(8,128)S(1)}, f32[584,128]{1,0:T(8,128)S(1)}, u32[]{:S(2)}, u32[]{:S(2)}) collective-permute-start(f32[584,128]{1,0:T(8,128)S(1)} %get-tuple-element.28), channel_id=1, source_target_pairs={{0,1},{1,2},{2,3},{3,4},{4,5},{5,6},{6,7},{7,8},{8,9},{9,10},{10,1... | collective-permute-start | bytes 897032 | tf_op jit(solution)/shard_map/ppermute | solution.py:289
  9.4 10.3 %collective-permute-start.1 = (f32[584,128]{1,0:T(8,128)S(1)}, f32[584,128]{1,0:T(8,128)S(1)}, u32[]{:S(2)}, u32[]{:S(2)}) collective-permute-start(f32[584,128]{1,0:T(8,128)S(1)} %get-tuple-element.29), channel_id=1, source_target_pairs={{1,0},{2,1},{3,2},{4,3},{5,4},{6,5},{7,6},{8,7},{9,8},{10,9},{11,1... | collective-permute-start | bytes 897032 | tf_op jit(solution)/shard_map/ppermute | solution.py:290
  21.0 14.2 %collective-permute-start.2 = (f32[640,128]{1,0:T(8,128)S(1)}, f32[640,128]{1,0:T(8,128)S(1)}, u32[]{:S(2)}, u32[]{:S(2)}) collective-permute-start(f32[640,128]{1,0:T(8,128)S(1)} %get-tuple-element.36), channel_id=1, source_target_pairs={{0,1},{1,2},{2,3},{3,4},{4,5},{5,6},{6,7},{7,8},{8,9},{9,10},{10,1... | collective-permute-start | bytes 983048 | tf_op jit(solution)/shard_map/ppermute | solution.py:310
  23.4 11.7 %collective-permute-start.3 = (f32[640,128]{1,0:T(8,128)S(1)}, f32[640,128]{1,0:T(8,128)S(1)}, u32[]{:S(2)}, u32[]{:S(2)}) collective-permute-start(f32[640,128]{1,0:T(8,128)S(1)} %get-tuple-element.37), channel_id=1, source_target_pairs={{1,0},{2,1},{3,2},{4,3},{5,4},{6,5},{7,6},{8,7},{9,8},{10,9},{11,1... | collective-permute-start | bytes 983048 | tf_op jit(solution)/shard_map/ppermute | solution.py:311
  28.5 6.6 %copy-start.5 = (s32[2]{0:T(128)S(1)}, s32[2]{0:T(128)}, u32[]{:S(2)}) copy-start(s32[2]{0:T(128)} %target.1) | copy-start | bytes 28

commit v2 on v1

--- a/solution.py
+++ b/solution.py
@@ -73,10 +73,42 @@
     return jnp.concatenate([frame[first : first + 4, c].reshape(HALF, 2 * BS) for c in columns], 1)
 
 
-def frame_kernel(nbr, agg, blocks, tent, dinv, frame, up, down):
-    first = nbr[0, 0]
+def frame_kernel(
+    nbr_in,
+    agg_in,
+    blocks_in,
+    tent_in,
+    dinv_in,
+    frame,
+    tent,
+    dinv,
+    up,
+    down,
+    nbr,
+    agg,
+    blocks,
+    sems,
+):
+    small = [
+        pltpu.make_async_copy(nbr_in, nbr, sems.at[0]),
+        pltpu.make_async_copy(agg_in, agg, sems.at[1]),
+    ]
+    rows = [pltpu.make_async_copy(blocks_in.at[i], blocks.at[i], sems.at[2 + i]) for i in range(RB)]
+    others = [
+        pltpu.make_async_copy(tent_in, tent, sems.at[2 + RB]),
+        pltpu.make_async_copy(dinv_in, dinv, sems.at[3 + RB]),
+    ]
+    for copy in small + rows + others:
+        copy.start()
     half = lane_half(BS)
     for i in range(RB):
+        for c in range(6):
+            frame[i, c] = jnp.zeros((BS, 2 * BS), F32)
+    for copy in small:
+        copy.wait()
+    first = nbr[0, 0]
+    for i in range(RB):
+        rows[i].wait()
         origin = first - 4 if i < 4 else first
         mine = i + 4 if i < 4 else i
         copies = []
@@ -84,15 +116,13 @@
             copies.extend(doubled(blocks[i, :, 2 * p * BS : 2 * (p + 1) * BS]))
         last = blocks[i, :, 6 * BS : 7 * BS]
         copies.append(jnp.concatenate([last, last], 1))
-        for c in range(6):
-            if c == mine // 2:
-                frame[i, c] = jnp.where(half == mine % 2, copies[0], 0.0)
-            else:
-                frame[i, c] = jnp.zeros((BS, 2 * BS), F32)
+        frame[i, mine // 2] = jnp.where(half == mine % 2, copies[0], 0.0)
         for k in range(1, K):
             at = nbr[i, k] - origin
             column = at >> 1
             frame[i, column] = frame[i, column] + jnp.where(half == (at & 1), copies[k], 0.0)
+    for copy in others:
+        copy.wait()
 
     def send(out, pieces, members):
         for c, value in enumerate(pieces):
@@ -121,8 +151,7 @@
     )
 
 
-def own_kernel(nbr, agg, frame, tent, dinv, a_high, a_low, near, factors, own, image):
-    owner = nbr[0, 0] // 4
+def own_kernel(frame, tent, dinv, up, down, a_high, a_low, near, factors, own, image):
     a = split(
         jnp.concatenate(
             [frame_columns(frame, 0, range(2, 6)), frame_columns(frame, 4, range(0, 4))], 0
@@ -131,7 +160,7 @@
     a_high[...], a_low[...] = a
     placed = place(
         [tent[:, 2 * p * BS : 2 * (p + 1) * BS] for p in range(4)],
-        [agg[j] - owner for j in range(RB)],
+        received_members(down) + received_members(up),
     )
     near[...] = placed
     summed = dot3(a, split(placed))
@@ -171,7 +200,7 @@
         out[3 * AGG :] = own[rows]
 
 
-def middle_kernel(frame, near, own, image, side, left, right, below, above, part, lo, hi):
+def middle_kernel(frame, near, own, image, side, left, right, below, above, part, lo, hi, slots):
     own_low, own_high = own[:HALF], own[HALF:]
     c_low, c_high = split(own_low), split(own_high)
     middle = dot3(
@@ -226,9 +255,12 @@
         + (x_high[:, :AGG] + dot3(split(t_high), b_above))
     )
     part[:, 2 * AGG :] = middle[:, 2 * AGG :] + x_high[:, AGG:]
-
-
-def finish_kernel(nbr, target, part, lo, hi, below, above, out):
+    for g in range(RB):
+        slots[g] = jnp.zeros((SLOT, 2 * BS), F32)
+
+
+def finish_kernel(nbr, target, part, lo, hi, below, above, empty, out):
+    del empty
     first_id = nbr[0, 0] // 4
     band = [
         below[:AGG],
@@ -241,8 +273,6 @@
         + dot3(split(hi[...]), split(above[3 * AGG :])),
         above[2 * AGG : 3 * AGG],
     ]
-    for g in range(RB):
-        out[g] = jnp.zeros((SLOT, 2 * BS), F32)
     for u in range(NA):
         g = target[u]
         for c in range(5):
@@ -250,29 +280,44 @@
         out[g, 5 * BS :] = jnp.full((8, 2 * BS), first_id + (u + 1), jnp.int32).astype(F32)
 
 
-def unpack_kernel(got, rows, ids):
+def unpack_kernel(got, rows, ids, sems):
+    copies = [
+        pltpu.make_async_copy(
+            got.at[:, c * BS : (c + 1) * BS], rows.at[:, :, c * 128 : (c + 1) * 128], sems.at[c]
+        )
+        for c in range(5)
+    ]
+    for copy in copies:
+        copy.start()
     lane = lax.broadcasted_iota(jnp.int32, (1, 2 * BS), 1)
     found = jnp.zeros((1, 2 * BS), F32)
     for s in range(RB):
-        for c in range(5):
-            rows[s * BS : (s + 1) * BS, c * 128 : (c + 1) * 128] = got[s, c * BS : (c + 1) * BS]
         found = jnp.where(lane == s, got[s, 5 * BS : 5 * BS + 1], found)
-    ids[...] = found.astype(jnp.int32) - 1
+    ids[...] = (found.astype(jnp.int32) - 1)[0, :RB]
+    for copy in copies:
+        copy.wait()
 
 
 VMEM = pl.BlockSpec(memory_space=pltpu.VMEM)
 SMEM = pl.BlockSpec(memory_space=pltpu.SMEM)
-
-
-def call(kernel, scalars, arrays, outs):
+HBM = pl.BlockSpec(memory_space=pltpu.HBM)
+
+
+def call(kernel, ins, outs, scratch=(), aliases=None):
     return pl.pallas_call(
         kernel,
-        in_specs=[SMEM] * len(scalars) + [VMEM] * len(arrays),
-        out_specs=[VMEM] * len(outs),
-        out_shape=[jax.ShapeDtypeStruct(shape, dtype) for shape, dtype in outs],
+        in_specs=[memory for memory, _ in ins],
+        out_specs=[memory for memory, _, _ in outs],
+        out_shape=[jax.ShapeDtypeStruct(shape, dtype) for _, shape, dtype in outs],
+        scratch_shapes=list(scratch),
+        input_output_aliases=aliases or {},
         compiler_params=pltpu.CompilerParams(vmem_limit_bytes=32 * 1024 * 1024),
         name=kernel.__name__,
-    )(*scalars, *arrays)
+    )(*[array for _, array in ins])
+
+
+def on_chip(*arrays):
+    return [(VMEM, array) for array in arrays]
 
 
 def body(blocks, neighbors, aggregate, tentative, inv_diagonal, target):
@@ -280,55 +325,71 @@
     devices = lax.axis_size(axes)
     upward = [(i, i + 1) for i in range(devices - 1)]
     downward = [(j, i) for i, j in upward]
-    frame, up, down = call(
+    frame, tent, dinv, up, down = call(
         frame_kernel,
-        [neighbors, aggregate],
-        [blocks, tentative, inv_diagonal],
-        [((RB, 6, BS, 2 * BS), F32), ((EDGE, 2 * BS), F32), ((EDGE, 2 * BS), F32)],
+        [(HBM, pltpu.with_memory_space_constraint(x, pltpu.HBM)) for x in (neighbors, aggregate, blocks, tentative, inv_diagonal)],
+        [
+            (VMEM, (RB, 6, BS, 2 * BS), F32),
+            (VMEM, (BS, RB * BS), F32),
+            (VMEM, (BS, RB * BS), F32),
+            (VMEM, (EDGE, 2 * BS), F32),
+            (VMEM, (EDGE, 2 * BS), F32),
+        ],
+        [
+            pltpu.SMEM((RB, K), jnp.int32),
+            pltpu.SMEM((RB,), jnp.int32),
+            pltpu.VMEM((RB, BS, K * BS), F32),
+            pltpu.SemaphoreType.DMA((4 + RB,)),
+        ],
     )
     below = lax.ppermute(up, axes, upward)
     above = lax.ppermute(down, axes, downward)
+    tall = (VMEM, (2 * HALF, AGG), F32)
     a_high, a_low, near, factors, own, image = call(
         own_kernel,
-        [neighbors, aggregate],
-        [frame, tentative, inv_diagonal],
-        [
-            ((2 * HALF, 2 * HALF), BF16),
-            ((2 * HALF, 2 * HALF), BF16),
-            ((2 * HALF, AGG), F32),
-            ((2, HALF, HALF), F32),
-            ((2 * HALF, AGG), F32),
-            ((2 * HALF, AGG), F32),
+        on_chip(frame, tent, dinv, up, down),
+        [
+            (VMEM, (2 * HALF, 2 * HALF), BF16),
+            (VMEM, (2 * HALF, 2 * HALF), BF16),
+            tall,
+            (VMEM, (2, HALF, HALF), F32),
+            tall,
+            tall,
         ],
     )
     side, left, right, up, down = call(
         edge_kernel,
-        [],
-        [a_high, a_low, factors, own, image, below, above],
-        [((2 * HALF, AGG), F32)] * 3 + [((5 * AGG, AGG), F32)] * 2,
+        on_chip(a_high, a_low, factors, own, image, below, above),
+        [tall] * 3 + [(VMEM, (5 * AGG, AGG), F32)] * 2,
     )
     below_terms = lax.ppermute(up, axes, upward)
     above_terms = lax.ppermute(down, axes, downward)
-    part, lo, hi = call(
+    slots_out = (VMEM, (RB, SLOT, 2 * BS), F32)
+    part, lo, hi, slots = call(
         middle_kernel,
-        [],
-        [frame, near, own, image, side, left, right, below, above],
-        [((AGG, 3 * AGG), F32), ((AGG, HALF), F32), ((AGG, HALF), F32)],
+        on_chip(frame, near, own, image, side, left, right, below, above),
+        [
+            (VMEM, (AGG, 3 * AGG), F32),
+            (VMEM, (AGG, HALF), F32),
+            (VMEM, (AGG, HALF), F32),
+            slots_out,
+        ],
     )
     (slots,) = call(
         finish_kernel,
-        [neighbors, target],
-        [part, lo, hi, below_terms, above_terms],
-        [((RB, SLOT, 2 * BS), F32)],
+        [(SMEM, neighbors), (SMEM, target)]
+        + on_chip(part, lo, hi, below_terms, above_terms, slots),
+        [slots_out],
+        aliases={7: 0},
     )
     got = lax.all_to_all(slots, "gy", split_axis=0, concat_axis=0, tiled=True)
     rows, ids = call(
         unpack_kernel,
-        [],
-        [got],
-        [((RB * BS, AW), F32), ((1, 2 * BS), jnp.int32)],
-    )
-    return rows, ids[0, :RB]
+        on_chip(got),
+        [(HBM, (RB, BS, AW), F32), (VMEM, (RB,), jnp.int32)],
+        [pltpu.SemaphoreType.DMA((5,))],
+    )
+    return rows.reshape(RB * BS, AW), ids
 
 
 def solution(mesh):

time: 81.1 us -> 77.5 us (0.956)
  local copies, waits for them, and re-layouts: 4.88 us -> 0.01 us
    unnamed x12 -> x4, local copies, waits for them, and re-layouts: 4.37 us -> 0.01 us
where the time goes in v2:
time: 77.5 us; the launch traced here: 77.2 us
  blocking collectives  43.1 us (56%)
  starting transfers between devices  15.1 us (19%)
  Pallas kernels  10.4 us (13%)
  waiting for transfers between devices  7.86 us (10%)
    all_to_all x1, blocking collectives, body(): got = lax.all_to_all(slots, 'gy', split_axis=0, concat_axis=0, tiled=True)  43.1 us
    pallas_call x6, Pallas kernels, call(): pl.pallas_call(kernel, in_specs=[memory for memory, _ in ins], out_specs=...  10.4 us
    ppermute x1, starting transfers between devices, body(): above_terms = lax.ppermute(down, axes, downward)  5.11 us
    ppermute x1, starting transfers between devices, body(): above = lax.ppermute(down, axes, downward)  4.38 us
    ppermute x1, waiting for transfers between devices, body(): below_terms = lax.ppermute(up, axes, upward)  4.24 us
    ppermute x1, waiting for transfers between devices, body(): below = lax.ppermute(up, axes, upward)  3.59 us
    ppermute x1, starting transfers between devices, body(): below = lax.ppermute(up, axes, upward)  3.2 us
    ppermute x1, starting transfers between devices, body(): below_terms = lax.ppermute(up, axes, upward)  2.41 us
  transfers between devices with their start and end apart: 4, of which 2 were waited for; matrix products, arithmetic and copies ran while one was open for 0% of the time, Pallas kernels for 6%

profile of v2, /device:TPU:199, one launch (start us, length us, event | category | flops | bytes accessed | tf_op | source)
XLA Modules:
  0.0 77.2 jit_solution(14267973315475332239)
XLA Ops:
  0.6 2.0 %frame_kernel.1 = (f32[8,6,64,128]{3,2,1,0:T(8,128)S(1)}, f32[64,512]{1,0:T(8,128)S(1)}, f32[64,512]{1,0:T(8,128)S(1)}, f32[584,128]{1,0:T(8,128)S(1)}, f32[584,128]{1,0:T(8,128)S(1)}) custom-call(s32[8,7]{1,0:T(8,128)} %nbr.1, s32[8]{0:T(128)} %agg_in.1, f32[8,64,448]{2,1,0:T(8,128)} %blocks_in.1, f32[64,512]{1,0:T(8,128)} %tent_in.1, f32[64,512]{1,0:T(8,128)} %dinv_in.1), custom_call_target="tpu_custom_call" | custom-call | tf_op jit(solution)/shard_map/frame_kernel/pallas_call | solution.py:307
  2.7 3.2 %collective-permute-start = (f32[584,128]{1,0:T(8,128)S(1)}, f32[584,128]{1,0:T(8,128)S(1)}, u32[]{:S(2)}, u32[]{:S(2)}) collective-permute-start(f32[584,128]{1,0:T(8,128)S(1)} %get-tuple-element.27.up), channel_id=1, source_target_pairs={{0,1},{1,2},{2,3},{3,4},{4,5},{5,6},{6,7},{7,8},{8,9},{9,10},{10,1... | collective-permute-start | bytes 897032 | tf_op jit(solution)/shard_map/ppermute | solution.py:345
  5.9 4.4 %collective-permute-start.1 = (f32[584,128]{1,0:T(8,128)S(1)}, f32[584,128]{1,0:T(8,128)S(1)}, u32[]{:S(2)}, u32[]{:S(2)}) collective-permute-start(f32[584,128]{1,0:T(8,128)S(1)} %get-tuple-element.28.down), channel_id=1, source_target_pairs={{1,0},{2,1},{3,2},{4,3},{5,4},{6,5},{7,6},{8,7},{9,8},{10,9},{11,1... | collective-permute-start | bytes 897032 | tf_op jit(solution)/shard_map/ppermute | solution.py:346
  10.3 2.3 %own_kernel.1 = (bf16[512,512]{1,0:T(8,128)(2,1)S(1)}, bf16[512,512]{1,0:T(8,128)(2,1)S(1)}, f32[512,128]{1,0:T(8,128)S(1)}, f32[2,256,256]{2,1,0:T(8,128)S(1)},...) custom-call(f32[8,6,64,128]{3,2,1,0:T(8,128)S(1)} %get-tuple-element.24.frame, f32[64,512]{1,0:T(8,128)S(1)} %get-tuple-element.25.tent, ...), custom_call_target="tpu_custom_call" | custom-call | tf_op jit(solution)/shard_map/own_kernel/pallas_call | solution.py:307
  12.6 3.6 %collective-permute-done.below = f32[584,128]{1,0:T(8,128)S(1)} collective-permute-done((f32[584,128]{1,0:T(8,128)S(1)}, f32[584,128]{1,0:T(8,128)S(1)}, u32[]{:S(2)}, u32[]{:S(2)}) %collective-permute-start) | collective-permute-done | bytes 299040 | tf_op jit(solution)/shard_map/ppermute | solution.py:345
  16.2 0.0 collective-permute-done.1.above
  16.2 1.2 %edge_kernel.1 = (f32[512,128]{1,0:T(8,128)S(1)}, f32[512,128]{1,0:T(8,128)S(1)}, f32[512,128]{1,0:T(8,128)S(1)}, f32[640,128]{1,0:T(8,128)S(1)}, f32[640,128]{1,0:T(8,128)S(1)}) custom-call(bf16[512,512]{1,0:T(8,128)(2,1)S(1)} %get-tuple-element.32.a_high, bf16[512,512]{1,0:T(8,128)(2,1)S(1)} %get-tuple-element.33.a_low, ...), custom_call_target="tpu_custom_call" | custom-call | tf_op jit(solution)/shard_map/edge_kernel/pallas_call | solution.py:307
  17.4 2.4 %collective-permute-start.2 = (f32[640,128]{1,0:T(8,128)S(1)}, f32[640,128]{1,0:T(8,128)S(1)}, u32[]{:S(2)}, u32[]{:S(2)}) collective-permute-start(f32[640,128]{1,0:T(8,128)S(1)} %get-tuple-element.41), channel_id=1, source_target_pairs={{0,1},{1,2},{2,3},{3,4},{4,5},{5,6},{6,7},{7,8},{8,9},{9,10},{10,1... | collective-permute-start | bytes 983048 | tf_op jit(solution)/shard_map/ppermute | solution.py:365
  19.9 5.1 %collective-permute-start.3 = (f32[640,128]{1,0:T(8,128)S(1)}, f32[640,128]{1,0:T(8,128)S(1)}, u32[]{:S(2)}, u32[]{:S(2)}) collective-permute-start(f32[640,128]{1,0:T(8,128)S(1)} %get-tuple-element.42), channel_id=1, source_target_pairs={{1,0},{2,1},{3,2},{4,3},{5,4},{6,5},{7,6},{8,7},{9,8},{10,9},{11,1... | collective-permute-start | bytes 983048 | tf_op jit(solution)/shard_map/ppermute | solution.py:366
  25.0 0.0 copy-start
  25.0 0.0 copy-start.1
  25.0 2.4 %middle_kernel.1 = (f32[128,384]{1,0:T(8,128)S(1)}, f32[128,256]{1,0:T(8,128)S(1)}, f32[128,256]{1,0:T(8,128)S(1)}, f32[8,328,128]{2,1,0:T(8,128)S(1)}) custom-call(f32[8,6,64,128]{3,2,1,0:T(8,128)S(1)} %get-tuple-element.24.frame, f32[512,128]{1,0:T(8,128)S(1)} %get-tuple-element.29.near, f32[512,128]{1,0:T(8,128)S(1)} %get-tuple-element.30.own, ...), custom_call_target="tpu_custom_call" | custom-call | tf_op jit(solution)/shard_map/middle_kernel/pallas_call | solution.py:307
  27.4 4.2 %collective-permute-done.2.below = f32[640,128]{1,0:T(8,128)S(1)} collective-permute-done((f32[640,128]{1,0:T(8,128)S(1)}, f32[640,128]{1,0:T(8,128)S(1)}, u32[]{:S(2)}, u32[]{:S(2)}) %collective-permute-start.2) | collective-permute-done | bytes 327712 | tf_op jit(solution)/shard_map/ppermute | solution.py:365
  31.6 0.0 collective-permute-done.3.above
  31.6 0.0 copy-done
  31.6 0.0 copy-done.1
  31.6 0.9 %finish_kernel.1 = f32[8,328,128]{2,1,0:T(8,128)S(1)} custom-call(s32[8,7]{1,0:T(8,128)S(1)} %copy-done, s32[2]{0:T(128)S(1)} %copy-done.1, f32[128,384]{1,0:T(8,128)S(1)} %get-tuple-element.38.part, f32[128,256]{1,0:T(8,128)S(1)} %get-tuple-element.39.lo, f32[128,256]{1,0:T(8,128)S(1)} %get-tuple-element.40.hi, ...), custom_call_target="tpu_custom_call", output_to_operand_aliasing={{}: (7, {})} | custom-call | tf_op jit(solution)/shard_map/finish_kernel/pallas_call | solution.py:307
  32.5 43.1 %all_to_all.5.got = f32[8,328,128]{2,1,0:T(8,128)S(1)} all-to-all(f32[8,328,128]{2,1,0:T(8,128)S(1)} %finish_kernel.1), channel_id=1, replica_groups=mesh['gx'=96,'gy'=8] {'gy'}, dimensions={0} | all-to-all | bytes 2686976 | tf_op jit(solution)/shard_map/all_to_all | solution.py:385
  75.6 1.6 %unpack_kernel.1 = (f32[8,64,640]{2,1,0:T(8,128)}, s32[8]{0:T(128)}) custom-call(f32[8,328,128]{2,1,0:T(8,128)S(1)} %all_to_all.5.got), custom_call_target="tpu_custom_call" | custom-call | tf_op jit(solution)/shard_map/unpack_kernel/pallas_call | solution.py:307
Async XLA Ops:
  2.7 13.5 %collective-permute-start = (f32[584,128]{1,0:T(8,128)S(1)}, f32[584,128]{1,0:T(8,128)S(1)}, u32[]{:S(2)}, u32[]{:S(2)}) collective-permute-start(f32[584,128]{1,0:T(8,128)S(1)} %get-tuple-element.27.up), channel_id=1, source_target_pairs={{0,1},{1,2},{2,3},{3,4},{4,5},{5,6},{6,7},{7,8},{8,9},{9,10},{10,1... | collective-permute-start | bytes 897032 | tf_op jit(solution)/shard_map/ppermute | solution.py:345
  5.9 10.3 %collective-permute-start.1 = (f32[584,128]{1,0:T(8,128)S(1)}, f32[584,128]{1,0:T(8,128)S(1)}, u32[]{:S(2)}, u32[]{:S(2)}) collective-permute-start(f32[584,128]{1,0:T(8,128)S(1)} %get-tuple-element.28.down), channel_id=1, source_target_pairs={{1,0},{2,1},{3,2},{4,3},{5,4},{6,5},{7,6},{8,7},{9,8},{10,9},{11,1... | collective-permute-start | bytes 897032 | tf_op jit(solution)/shard_map/ppermute | solution.py:346
  17.4 14.2 %collective-permute-start.2 = (f32[640,128]{1,0:T(8,128)S(1)}, f32[640,128]{1,0:T(8,128)S(1)}, u32[]{:S(2)}, u32[]{:S(2)}) collective-permute-start(f32[640,128]{1,0:T(8,128)S(1)} %get-tuple-element.41), channel_id=1, source_target_pairs={{0,1},{1,2},{2,3},{3,4},{4,5},{5,6},{6,7},{7,8},{8,9},{9,10},{10,1... | collective-permute-start | bytes 983048 | tf_op jit(solution)/shard_map/ppermute | solution.py:365
  19.9 11.7 %collective-permute-start.3 = (f32[640,128]{1,0:T(8,128)S(1)}, f32[640,128]{1,0:T(8,128)S(1)}, u32[]{:S(2)}, u32[]{:S(2)}) collective-permute-start(f32[640,128]{1,0:T(8,128)S(1)} %get-tuple-element.42), channel_id=1, source_target_pairs={{1,0},{2,1},{3,2},{4,3},{5,4},{6,5},{7,6},{8,7},{9,8},{10,9},{11,1... | collective-permute-start | bytes 983048 | tf_op jit(solution)/shard_map/ppermute | solution.py:366
  25.0 6.6 %copy-start = (s32[8,7]{1,0:T(8,128)S(1)}, s32[8,7]{1,0:T(8,128)}, u32[]{:S(2)}) copy-start(s32[8,7]{1,0:T(8,128)} %nbr.1) | copy-start | bytes 676
  25.0 6.6 %copy-start.1 = (s32[2]{0:T(128)S(1)}, s32[2]{0:T(128)}, u32[]{:S(2)}) copy-start(s32[2]{0:T(128)} %target.1) | copy-start | bytes 28

commit v3 on v2

v3 whole, which is shorter than its diff:
```python
import jax
import jax.numpy as jnp
from jax import lax
from jax.experimental import pallas as pl
from jax.experimental.pallas import tpu as pltpu
from jax.sharding import PartitionSpec as P

BS = 64
K = 7
RB = 8
NA = 2
AW = 640
HALF = 256
AGG = NA * BS
UP = 9 * BS + 8 + HALF
DOWN = 2 * BS + 8
SLOT = 5 * BS // 8 + 1
OMEGA = 2.0 / 3.0
F32 = jnp.float32
BF16 = jnp.bfloat16


def split(x):
    high = x.astype(BF16)
    return high, (x - high.astype(F32)).astype(BF16)


def dot3(a, b, side=1):
    def dot(x, y):
        return lax.dot_general(x, y, (((side,), (0,)), ((), ())), preferred_element_type=F32)

    return dot(a[0], b[0]) + (dot(a[0], b[1]) + dot(a[1], b[0]))


def lane_half(rows):
    return lax.broadcasted_iota(jnp.int32, (rows, 2 * BS), 1) // BS


def doubled(pair):
    low = lane_half(BS) == 0
    other = pltpu.roll(pair, BS, 1)
    return jnp.where(low, pair, other), jnp.where(low, other, pair)


def place(pairs, members):
    half = lane_half(BS)
    rows = []
    for p, pair in enumerate(pairs):
        for q, block in enumerate(doubled(pair)):
            rows.append(jnp.where(half == members[2 * p + q], block, 0.0))
    return jnp.concatenate(rows, 0)


def block_diagonal(low, high):
    tall = jnp.concatenate([jnp.concatenate([low, high], 1)] * 4, 0)
    row = lax.broadcasted_iota(jnp.int32, tall.shape, 0) // BS
    column = lax.broadcasted_iota(jnp.int32, tall.shape, 1) // BS
    return jnp.where(row == column, tall, 0.0)


def piece(ref, c):
    return ref[c * BS : (c + 1) * BS]


def received_place(ref, members):
    rows = [ref[members + m : members + m + 1].astype(jnp.int32) for m in range(4)]
    return place([piece(ref, 0), piece(ref, 1)], rows)


def frame_columns(frame, first, columns):
    return jnp.concatenate([frame[first : first + 4, c].reshape(HALF, 2 * BS) for c in columns], 1)


def doubled_row(blocks, i):
    copies = []
    for p in range(3):
        copies.extend(doubled(blocks[i, :, 2 * p * BS : 2 * (p + 1) * BS]))
    last = blocks[i, :, 6 * BS : 7 * BS]
    return copies + [jnp.concatenate([last, last], 1)]


def own_prolong(own_rows, near, inverse, rows):
    summed = dot3(own_rows, split(near))
    return near[rows] - OMEGA * dot3(inverse, split(summed))


def frame_kernel(
    nbr_in, agg_in, blocks_in, tent_in, dinv_in, frame, dinv, near, odd, up, down, nbr, agg, blocks, tent, sems
):
    small = [
        pltpu.make_async_copy(nbr_in, nbr, sems.at[0]),
        pltpu.make_async_copy(agg_in, agg, sems.at[1]),
    ]
    rows = [pltpu.make_async_copy(blocks_in.at[i], blocks.at[i], sems.at[2 + i]) for i in range(RB)]
    others = [
        pltpu.make_async_copy(tent_in, tent, sems.at[2 + RB]),
        pltpu.make_async_copy(dinv_in, dinv, sems.at[3 + RB]),
    ]
    for copy in small + others + rows:
        copy.start()
    half = lane_half(BS)
    for i in range(RB):
        for c in range(6):
            frame[i, c] = jnp.zeros((BS, 2 * BS), F32)
    for copy in small + others:
        copy.wait()
    first = nbr[0, 0]
    owner = first // 4
    odd[...] = jnp.full((8, 2 * BS), (first // RB) & 1, jnp.int32)
    near[...] = place(
        [tent[:, 2 * p * BS : 2 * (p + 1) * BS] for p in range(4)],
        [agg[j] - owner for j in range(RB)],
    )
    for i in range(RB):
        rows[i].wait()
        origin = first - 4 if i < 4 else first
        mine = i + 4 if i < 4 else i
        copies = doubled_row(blocks, i)
        frame[i, mine // 2] = jnp.where(half == mine % 2, copies[0], 0.0)
        for k in range(1, K):
            at = nbr[i, k] - origin
            column = at >> 1
            frame[i, column] = frame[i, column] + jnp.where(half == (at & 1), copies[k], 0.0)

    def send(out, pieces, members):
        for c, value in enumerate(pieces):
            out[c * BS : (c + 1) * BS] = value
        row = lax.broadcasted_iota(jnp.int32, (8, 2 * BS), 0)
        value = jnp.zeros((8, 2 * BS), F32)
        for m, member in enumerate(members):
            value = jnp.where(row == m, member.astype(F32), value)
        out[len(pieces) * BS : len(pieces) * BS + 8] = value

    low = half == 0
    send(
        up,
        [tent[:, 256:384], tent[:, 384:512], dinv[:, 256:384], dinv[:, 384:512]]
        + [frame[7, 4], frame[7, 5], frame[6, 4]]
        + [jnp.where(low, frame[6, 5], pltpu.roll(frame[4, 4], BS, 1)), frame[5, 4]],
        [agg[4 + m] - owner for m in range(4)],
    )
    send(down, [tent[:, 0:128], tent[:, 128:256]], [agg[m] - owner for m in range(4)])
    up[UP - HALF :] = own_prolong(
        split(frame_columns(frame, 4, range(0, 4))),
        near[...],
        split(block_diagonal(dinv[:, 256:384], dinv[:, 384:512])),
        slice(HALF, 2 * HALF),
    )


def own_kernel(
    frame, dinv, near, up, a_high, a_low, factors, inner, outer, cross, crossed, own, image
):
    lower = split(frame_columns(frame, 0, range(2, 6)))
    upper = split(frame_columns(frame, 4, range(0, 4)))
    a = [jnp.concatenate([x, y], 0) for x, y in zip(lower, upper)]
    a_high[...], a_low[...] = a
    inverse = [
        split(block_diagonal(dinv[:, s * HALF : s * HALF + 128], dinv[:, s * HALF + 128 : (s + 1) * HALF]))
        for s in range(2)
    ]
    c_low = own_prolong(lower, near[...], inverse[0], slice(0, HALF))
    edge = [split(frame_columns(frame, 0, (0, 1))), split(frame_columns(frame, 4, (4, 5)))]
    both = []
    for s in range(2):
        factor = -OMEGA * dot3(inverse[s], edge[s])
        factors[s] = factor
        both.append(split(factor))
    prolong = jnp.concatenate([c_low, up[UP - HALF :]], 0)
    own[...] = prolong
    applied = dot3(a, split(prolong))
    image[...] = applied
    for t in range(2):
        columns = slice(t * HALF, (t + 1) * HALF)
        moved = dot3((a[0][:, columns], a[1][:, columns]), both[t])
        for s in range(2):
            inner[s, t] = dot3(both[s], split(moved[s * HALF : (s + 1) * HALF]), 0)
    for s in range(2):
        outer[s] = dot3(both[s], split(applied[s * HALF : (s + 1) * HALF]), 0)
    cross[...] = dot3(both[0], edge[0], 0)
    crossed[...] = dot3(split(c_low), edge[0], 0)


def edge_kernel(
    odd, inner, outer, cross, factors, near, own, below, above, side, far, moved, early, late
):
    placed = [split(received_place(below, 9 * BS)), split(received_place(above, 2 * BS))]
    low = lane_half(BS) == 0
    none = jnp.zeros((BS, 2 * BS), F32)
    seven = piece(below, 7)
    a_below = split(
        jnp.concatenate(
            [
                jnp.concatenate(row, 1)
                for row in [
                    [jnp.where(low, pltpu.roll(seven, BS, 1), 0.0), none],
                    [piece(below, 8), none],
                    [piece(below, 6), jnp.where(low, seven, 0.0)],
                    [piece(below, 4), piece(below, 5)],
                ]
            ],
            0,
        )
    )
    inverse = split(block_diagonal(piece(below, 2), piece(below, 3)))
    b_below = -OMEGA * dot3(inverse, split(dot3(a_below, split(near[:HALF]))))
    b_low = dot3(split(factors[0]), placed[0])
    image_low = dot3(a_below, split(jnp.concatenate([b_low, own[:HALF]], 1)))
    c_below = below[UP - HALF :]
    far_rows = jnp.concatenate([c_below, b_below], 1)
    side[...] = b_low
    far[...] = far_rows
    moved[...] = image_low
    across = dot3(split(cross[...]), split(far_rows))
    terms = []
    for s in range(2):
        left, right = [dot3(split(inner[s, t]), placed[t]) for t in range(2)]
        middle = outer[s]
        if s == 0:
            left = left + across[:, :AGG]
            middle = middle + across[:, AGG:]
        terms.append(dot3(placed[s], split(jnp.concatenate([left, middle, right], 1)), 0))
    lower_terms = dot3(split(c_below), split(image_low), 0)
    upward = odd[:1] == 1
    for c in range(3):
        columns = slice(c * AGG, (c + 1) * AGG)
        down, up = terms[0][:, columns], terms[1][:, columns]
        if c < 2:
            down = down + lower_terms[:, columns]
        early[columns] = jnp.where(upward, up, down)
        late[columns] = jnp.where(upward, down, up)


def middle_kernel(
    a_high, a_low, factors, crossed, own, image, above, side, far, moved, part, slots
):
    b_high = dot3(split(factors[1]), split(received_place(above, 2 * BS)))
    left = dot3((a_high[:, :HALF], a_low[:, :HALF]), split(side[...]))
    right = dot3((a_high[:, HALF:], a_low[:, HALF:]), split(b_high))
    middle = dot3(split(own[...]), split(jnp.concatenate([left, image[...], right], 1)), 0)
    lower = dot3(split(far[:, AGG:]), split(moved[...]), 0) + dot3(
        split(crossed[...]), split(far[...])
    )
    part[:, : 2 * AGG] = middle[:, : 2 * AGG] + lower
    part[:, 2 * AGG :] = middle[:, 2 * AGG :]
    for g in range(RB):
        slots[g] = jnp.zeros((SLOT, 8, 2 * BS), F32)


def finish_kernel(nbr, target, odd, part, early, late, empty, out):
    del empty
    first_id = nbr[0, 0] // 4
    upward = odd[:1] == 1
    below = [
        jnp.where(upward, late[c * AGG : (c + 1) * AGG], early[c * AGG : (c + 1) * AGG])
        for c in range(3)
    ]
    above = [
        jnp.where(upward, early[c * AGG : (c + 1) * AGG], late[c * AGG : (c + 1) * AGG])
        for c in range(3)
    ]
    band = [
        below[0],
        part[:, :AGG] + below[1],
        part[:, AGG : 2 * AGG] + below[2] + above[0],
        part[:, 2 * AGG :] + above[1],
        above[2],
    ]
    for u in range(NA):
        g = target[u]
        for r in range(8):
            for c in range(5):
                out[g, 5 * r + c] = band[c][u * BS + 8 * r : u * BS + 8 * (r + 1)]
        out[g, SLOT - 1] = jnp.full((8, 2 * BS), first_id + (u + 1), jnp.int32).astype(F32)


def unpack_kernel(got, rows, ids, sem):
    copy = pltpu.make_async_copy(got.at[:, : SLOT - 1], rows, sem)
    copy.start()
    lane = lax.broadcasted_iota(jnp.int32, (1, 2 * BS), 1)
    found = jnp.zeros((1, 2 * BS), F32)
    for s in range(RB):
        found = jnp.where(lane == s, got[s, SLOT - 1, :1], found)
    ids[...] = (found.astype(jnp.int32) - 1)[0, :RB]
    copy.wait()


VMEM = pl.BlockSpec(memory_space=pltpu.VMEM)
SMEM = pl.BlockSpec(memory_space=pltpu.SMEM)
HBM = pl.BlockSpec(memory_space=pltpu.HBM)


def call(kernel, ins, outs, scratch=(), aliases=None):
    return pl.pallas_call(
        kernel,
        in_specs=[memory for memory, _ in ins],
        out_specs=[memory for memory, _, _ in outs],
        out_shape=[jax.ShapeDtypeStruct(shape, dtype) for _, shape, dtype in outs],
        scratch_shapes=list(scratch),
        input_output_aliases=aliases or {},
        compiler_params=pltpu.CompilerParams(vmem_limit_bytes=32 * 1024 * 1024),
        name=kernel.__name__,
    )(*[array for _, array in ins])


def on_chip(*arrays):
    return [(VMEM, array) for array in arrays]


def body(blocks, neighbors, aggregate, tentative, inv_diagonal, target):
    axes = ("gx", "gy")
    devices = lax.axis_size(axes)
    upward = [(i, i + 1) for i in range(devices - 1)]
    downward = [(j, i) for i, j in upward]
    tall = (VMEM, (2 * HALF, AGG), F32)
    square = (VMEM, (HALF, HALF), F32)
    frame, dinv, near, odd, up, down = call(
        frame_kernel,
        [
            (HBM, pltpu.with_memory_space_constraint(x, pltpu.HBM))
            for x in (neighbors, aggregate, blocks, tentative, inv_diagonal)
        ],
        [
            (VMEM, (RB, 6, BS, 2 * BS), F32),
            (VMEM, (BS, RB * BS), F32),
            tall,
            (VMEM, (8, 2 * BS), jnp.int32),
            (VMEM, (UP, 2 * BS), F32),
            (VMEM, (DOWN, 2 * BS), F32),
        ],
        [
            pltpu.SMEM((RB, K), jnp.int32),
            pltpu.SMEM((RB,), jnp.int32),
            pltpu.VMEM((RB, BS, K * BS), F32),
            pltpu.VMEM((BS, RB * BS), F32),
            pltpu.SemaphoreType.DMA((4 + RB,)),
        ],
    )
    below = lax.ppermute(up, axes, upward)
    above = lax.ppermute(down, axes, downward)
    a_high, a_low, factors, inner, outer, cross, crossed, own, image = call(
        own_kernel,
        on_chip(frame, dinv, near, up),
        [
            (VMEM, (2 * HALF, 2 * HALF), BF16),
            (VMEM, (2 * HALF, 2 * HALF), BF16),
            (VMEM, (2, HALF, HALF), F32),
            (VMEM, (2, 2, HALF, HALF), F32),
            (VMEM, (2, HALF, AGG), F32),
            square,
            (VMEM, (AGG, HALF), F32),
            tall,
            tall,
        ],
    )
    side, far, moved, early, late = call(
        edge_kernel,
        on_chip(odd, inner, outer, cross, factors, near, own, below, above),
        [(VMEM, (HALF, AGG), F32), square, square] + [(VMEM, (3 * AGG, AGG), F32)] * 2,
    )
    odd_pairs = [(i, i + 1 if i % 2 else i - 1) for i in range(1, devices - 1)]
    even_pairs = [(i, i ^ 1) for i in range(devices)]
    early = lax.ppermute(early, axes, odd_pairs)
    late = lax.ppermute(late, axes, even_pairs)
    slots_out = (VMEM, (RB, SLOT, 8, 2 * BS), F32)
    part, slots = call(
        middle_kernel,
        on_chip(a_high, a_low, factors, crossed, own, image, above, side, far, moved),
        [(VMEM, (AGG, 3 * AGG), F32), slots_out],
    )
    (slots,) = call(
        finish_kernel,
        [(SMEM, neighbors), (SMEM, target)] + on_chip(odd, part, early, late, slots),
        [slots_out],
        aliases={6: 0},
    )
    got = lax.all_to_all(slots, "gy", split_axis=0, concat_axis=0, tiled=True)
    tiles, ids = call(
        unpack_kernel,
        on_chip(got),
        [(HBM, (RB, SLOT - 1, 8, 2 * BS), F32), (VMEM, (RB,), jnp.int32)],
        [pltpu.SemaphoreType.DMA(())],
    )
    rows = tiles.reshape(RB * BS // 8, AW // 128, 8, 128).transpose(0, 2, 1, 3)
    return rows.reshape(RB * BS, AW), ids


def solution(mesh):
    placed = (
        P(("gx", "gy"), None, None),
        P(("gx", "gy"), None),
        P(("gx", "gy")),
        P(None, ("gx", "gy")),
        P(None, ("gx", "gy")),
        P(("gx", "gy")),
    )
    return jax.shard_map(
        body,
        mesh=mesh,
        in_specs=placed,
        out_specs=(P(("gx", "gy"), None), P(("gx", "gy"))),
        check_vma=False,
    )
```

time: 77.5 us -> 76.2 us (0.983)
  waiting for transfers between devices: 7.86 us -> 11.1 us
  starting transfers between devices: 15.1 us -> 12.4 us
  blocking collectives: 43.1 us -> 40.5 us
  Pallas kernels: 10.4 us -> 11.3 us
    ppermute x2, starting transfers between devices: 7.52 us -> 4.81 us  [the longest x1 2.89 us: body(): early = lax.ppermute(early, axes, odd_pairs)]
    all_to_all x1, blocking collectives: 43.1 us -> 40.5 us  [body(): got = lax.all_to_all(slots, 'gy', split_axis=0, concat_axis=0, tiled=True)]
    ppermute x1, waiting for transfers between devices: 3.59 us -> 5.86 us  [body(): below = lax.ppermute(up, axes, upward)]
    ppermute x2, waiting for transfers between devices: 4.24 us -> 5.24 us  [the longest x1 2.68 us: body(): early = lax.ppermute(early, axes, odd_pairs)]
    pallas_call x6, Pallas kernels: 10.4 us -> 11.3 us  [call(): pl.pallas_call(kernel, in_specs=[memory for memory, _ in ins], out_specs=...]
  transfers between devices with their start and end apart: 4 -> 4, of which waited for: 2 -> 3; matrix products, arithmetic and copies ran while one was open for 0% -> 0% of each run, Pallas kernels for 6% -> 6%
where the time goes in v3:
time: 76.2 us; the launch traced here: 76 us
  blocking collectives  40.5 us (53%)
  starting transfers between devices  12.4 us (16%)
  Pallas kernels  11.3 us (15%)
  waiting for transfers between devices  11.1 us (15%)
    all_to_all x1, blocking collectives, body(): got = lax.all_to_all(slots, 'gy', split_axis=0, concat_axis=0, tiled=True)  40.5 us
    pallas_call x6, Pallas kernels, call(): pl.pallas_call(kernel, in_specs=[memory for memory, _ in ins], out_specs=...  11.3 us
    ppermute x1, waiting for transfers between devices, body(): below = lax.ppermute(up, axes, upward)  5.86 us
    ppermute x1, starting transfers between devices, body(): above = lax.ppermute(down, axes, downward)  4.38 us
    ppermute x1, starting transfers between devices, body(): below = lax.ppermute(up, axes, upward)  3.21 us
    ppermute x1, starting transfers between devices, body(): early = lax.ppermute(early, axes, odd_pairs)  2.89 us
    ppermute x1, waiting for transfers between devices, body(): early = lax.ppermute(early, axes, odd_pairs)  2.68 us
    ppermute x1, waiting for transfers between devices, body(): late = lax.ppermute(late, axes, even_pairs)  2.56 us
  transfers between devices with their start and end apart: 4, of which 3 were waited for; matrix products, arithmetic and copies ran while one was open for 0% of the time, Pallas kernels for 6%

profile of v3, /device:TPU:199, one launch (start us, length us, event | category | flops | bytes accessed | tf_op | source)
XLA Modules:
  0.0 76.0 jit_solution(4780719123333802175)
XLA Ops:
  0.6 2.8 %frame_kernel.1 = (f32[8,6,64,128]{3,2,1,0:T(8,128)S(1)}, f32[64,512]{1,0:T(8,128)S(1)}, f32[512,128]{1,0:T(8,128)S(1)}, s32[8,128]{1,0:T(8,128)S(1)}, f32[840,128]{1,0:T(8,128)S(1)}, /*index=5*/f32[136,128]{1,0:T(8,128)S(1)}) custom-call(s32[8,7]{1,0:T(8,128)} %nbr.1, s32[8]{0:T(128)} %agg_in.1, f32[8,64,448]{2,1,0:T(8,128)} %blocks_in.1, ...), custom_call_target="tpu_custom_call" | custom-call | tf_op jit(solution)/shard_map/frame_kernel/pallas_call | solution.py:294
  3.4 3.2 %collective-permute-start.1 = (f32[840,128]{1,0:T(8,128)S(1)}, f32[840,128]{1,0:T(8,128)S(1)}, u32[]{:S(2)}, u32[]{:S(2)}) collective-permute-start(f32[840,128]{1,0:T(8,128)S(1)} %get-tuple-element.30.up), channel_id=1, source_target_pairs={{0,1},{1,2},{2,3},{3,4},{4,5},{5,6},{6,7},{7,8},{8,9},{9,10},{10,1... | collective-permute-start | bytes 1290248 | tf_op jit(solution)/shard_map/ppermute | solution.py:339
  6.6 4.4 %collective-permute-start = (f32[136,128]{1,0:T(8,128)S(1)}, f32[136,128]{1,0:T(8,128)S(1)}, u32[]{:S(2)}, u32[]{:S(2)}) collective-permute-start(f32[136,128]{1,0:T(8,128)S(1)} %get-tuple-element.37), channel_id=1, source_target_pairs={{1,0},{2,1},{3,2},{4,3},{5,4},{6,5},{7,6},{8,7},{9,8},{10,9},{11,1... | collective-permute-start | bytes 208904 | tf_op jit(solution)/shard_map/ppermute | solution.py:340
  11.0 2.8 %own_kernel.1 = (bf16[512,512]{1,0:T(8,128)(2,1)S(1)}, bf16[512,512]{1,0:T(8,128)(2,1)S(1)}, f32[2,256,256]{2,1,0:T(8,128)S(1)}, f32[2,2,256,256]{3,2,1,0:T(8,12...) custom-call(f32[8,6,64,128]{3,2,1,0:T(8,128)S(1)} %get-tuple-element, ...), custom_call_target="tpu_custom_call" | custom-call | tf_op jit(solution)/shard_map/own_kernel/pallas_call | solution.py:294
  13.8 0.0 collective-permute-done.above
  13.9 5.9 %collective-permute-done.1.below = f32[840,128]{1,0:T(8,128)S(1)} collective-permute-done((f32[840,128]{1,0:T(8,128)S(1)}, f32[840,128]{1,0:T(8,128)S(1)}, u32[]{:S(2)}, u32[]{:S(2)}) %collective-permute-start.1) | collective-permute-done | bytes 430112 | tf_op jit(solution)/shard_map/ppermute | solution.py:339
  19.7 2.0 %edge_kernel.1 = (f32[256,128]{1,0:T(8,128)S(1)}, f32[256,256]{1,0:T(8,128)S(1)}, f32[256,256]{1,0:T(8,128)S(1)}, f32[384,128]{1,0:T(8,128)S(1)}, f32[384,128]{1,0:T(8,128)S(1)}) custom-call(s32[8,128]{1,0:T(8,128)S(1)} %get-tuple-element.26.odd, f32[2,2,256,256]{3,2,1,0:T(8,128)S(1)} %get-tuple-element.38.inner, ...), custom_call_target="tpu_custom_call" | custom-call | tf_op jit(solution)/shard_map/edge_kernel/pallas_call | solution.py:294
  21.8 2.9 %collective-permute-start.2 = (f32[384,128]{1,0:T(8,128)S(1)}, f32[384,128]{1,0:T(8,128)S(1)}, u32[]{:S(2)}, u32[]{:S(2)}) collective-permute-start(f32[384,128]{1,0:T(8,128)S(1)} %get-tuple-element.45), channel_id=1, source_target_pairs={{1,2},{2,1},{3,4},{4,3},{5,6},{6,5},{7,8},{8,7},{9,10},{10,9},{11,... | collective-permute-start | bytes 589832 | tf_op jit(solution)/shard_map/ppermute | solution.py:363
  24.7 1.9 %collective-permute-start.3 = (f32[384,128]{1,0:T(8,128)S(1)}, f32[384,128]{1,0:T(8,128)S(1)}, u32[]{:S(2)}, u32[]{:S(2)}) collective-permute-start(f32[384,128]{1,0:T(8,128)S(1)} %get-tuple-element.46), channel_id=1, source_target_pairs={{0,1},{1,0},{2,3},{3,2},{4,5},{5,4},{6,7},{7,6},{8,9},{9,8},{10,11... | collective-permute-start | bytes 589832 | tf_op jit(solution)/shard_map/ppermute | solution.py:364
  26.6 0.0 copy-start
  26.6 0.0 copy-start.1
  26.6 1.4 %middle_kernel.1 = (f32[128,384]{1,0:T(8,128)S(1)}, f32[8,41,8,128]{3,2,1,0:T(8,128)S(1)}) custom-call(bf16[512,512]{1,0:T(8,128)(2,1)S(1)} %get-tuple-element.31.a_high, bf16[512,512]{1,0:T(8,128)(2,1)S(1)} %get-tuple-element.32.a_low, f32[2,256,256]{2,1,0:T(8,128)S(1)} %get-tuple-element.33.factors, f32[128,256]{1,0:T(8,128)S(1)} %get-tuple-element.34.crossed, ...), custom_call_target="tpu_custom_call" | custom-call | tf_op jit(solution)/shard_map/middle_kernel/pallas_call | solution.py:294
  28.0 2.7 %collective-permute-done.2.early = f32[384,128]{1,0:T(8,128)S(1)} collective-permute-done((f32[384,128]{1,0:T(8,128)S(1)}, f32[384,128]{1,0:T(8,128)S(1)}, u32[]{:S(2)}, u32[]{:S(2)}) %collective-permute-start.2) | collective-permute-done | bytes 196640 | tf_op jit(solution)/shard_map/ppermute | solution.py:363
  30.7 2.6 %collective-permute-done.3.late = f32[384,128]{1,0:T(8,128)S(1)} collective-permute-done((f32[384,128]{1,0:T(8,128)S(1)}, f32[384,128]{1,0:T(8,128)S(1)}, u32[]{:S(2)}, u32[]{:S(2)}) %collective-permute-start.3) | collective-permute-done | bytes 196640 | tf_op jit(solution)/shard_map/ppermute | solution.py:364
  33.3 0.0 copy-done
  33.3 0.0 copy-done.1
  33.3 0.6 finish_kernel.1
  33.9 40.5 %all_to_all.5.got = f32[8,41,8,128]{3,2,1,0:T(8,128)S(1)} all-to-all(f32[8,41,8,128]{3,2,1,0:T(8,128)S(1)} %finish_kernel.1), channel_id=1, replica_groups=mesh['gx'=96,'gy'=8] {'gy'}, dimensions={0} | all-to-all | bytes 2686976 | tf_op jit(solution)/shard_map/all_to_all | solution.py:377
  74.4 1.6 %unpack_kernel.1 = (f32[8,40,8,128]{3,2,1,0:T(8,128)}, s32[8]{0:T(128)}) custom-call(f32[8,41,8,128]{3,2,1,0:T(8,128)S(1)} %all_to_all.5.got), custom_call_target="tpu_custom_call" | custom-call | tf_op jit(solution)/shard_map/unpack_kernel/pallas_call | solution.py:294
Async XLA Ops:
  3.4 16.3 %collective-permute-start.1 = (f32[840,128]{1,0:T(8,128)S(1)}, f32[840,128]{1,0:T(8,128)S(1)}, u32[]{:S(2)}, u32[]{:S(2)}) collective-permute-start(f32[840,128]{1,0:T(8,128)S(1)} %get-tuple-element.30.up), channel_id=1, source_target_pairs={{0,1},{1,2},{2,3},{3,4},{4,5},{5,6},{6,7},{7,8},{8,9},{9,10},{10,1... | collective-permute-start | bytes 1290248 | tf_op jit(solution)/shard_map/ppermute | solution.py:339
  6.6 7.2 %collective-permute-start = (f32[136,128]{1,0:T(8,128)S(1)}, f32[136,128]{1,0:T(8,128)S(1)}, u32[]{:S(2)}, u32[]{:S(2)}) collective-permute-start(f32[136,128]{1,0:T(8,128)S(1)} %get-tuple-element.37), channel_id=1, source_target_pairs={{1,0},{2,1},{3,2},{4,3},{5,4},{6,5},{7,6},{8,7},{9,8},{10,9},{11,1... | collective-permute-start | bytes 208904 | tf_op jit(solution)/shard_map/ppermute | solution.py:340
  21.8 8.9 %collective-permute-start.2 = (f32[384,128]{1,0:T(8,128)S(1)}, f32[384,128]{1,0:T(8,128)S(1)}, u32[]{:S(2)}, u32[]{:S(2)}) collective-permute-start(f32[384,128]{1,0:T(8,128)S(1)} %get-tuple-element.45), channel_id=1, source_target_pairs={{1,2},{2,1},{3,4},{4,3},{5,6},{6,5},{7,8},{8,7},{9,10},{10,9},{11,... | collective-permute-start | bytes 589832 | tf_op jit(solution)/shard_map/ppermute | solution.py:363
  24.7 8.6 %collective-permute-start.3 = (f32[384,128]{1,0:T(8,128)S(1)}, f32[384,128]{1,0:T(8,128)S(1)}, u32[]{:S(2)}, u32[]{:S(2)}) collective-permute-start(f32[384,128]{1,0:T(8,128)S(1)} %get-tuple-element.46), channel_id=1, source_target_pairs={{0,1},{1,0},{2,3},{3,2},{4,5},{5,4},{6,7},{7,6},{8,9},{9,8},{10,11... | collective-permute-start | bytes 589832 | tf_op jit(solution)/shard_map/ppermute | solution.py:364
  26.6 6.7 %copy-start = (s32[8,7]{1,0:T(8,128)S(1)}, s32[8,7]{1,0:T(8,128)}, u32[]{:S(2)}) copy-start(s32[8,7]{1,0:T(8,128)} %nbr.1) | copy-start | bytes 676
  26.6 6.7 %copy-start.1 = (s32[2]{0:T(128)S(1)}, s32[2]{0:T(128)}, u32[]{:S(2)}) copy-start(s32[2]{0:T(128)} %target.1) | copy-start | bytes 28

commit v4 on v3

--- a/solution.py
+++ b/solution.py
@@ -67,8 +67,8 @@
     return place([piece(ref, 0), piece(ref, 1)], rows)
 
 
-def frame_columns(frame, first, columns):
-    return jnp.concatenate([frame[first : first + 4, c].reshape(HALF, 2 * BS) for c in columns], 1)
+def frame_columns(frame, columns):
+    return jnp.concatenate([frame[:, c].reshape(HALF, 2 * BS) for c in columns], 1)
 
 
 def doubled_row(blocks, i):
@@ -84,83 +84,116 @@
     return near[rows] - OMEGA * dot3(inverse, split(summed))
 
 
+def spread(nbr, blocks, frame, i, origin):
+    half = lane_half(BS)
+    row, mine = i % 4, i + 4 if i < 4 else i
+    copies = doubled_row(blocks, row)
+    for c in range(6):
+        frame[row, c] = jnp.zeros((BS, 2 * BS), F32)
+    frame[row, mine // 2] = jnp.where(half == mine % 2, copies[0], 0.0)
+    for k in range(1, K):
+        at = nbr[i, k] - origin
+        column = at >> 1
+        frame[row, column] = frame[row, column] + jnp.where(half == (at & 1), copies[k], 0.0)
+
+
 def frame_kernel(
-    nbr_in, agg_in, blocks_in, tent_in, dinv_in, frame, dinv, near, odd, up, down, nbr, agg, blocks, tent, sems
+    nbr_in, agg_in, blocks_in, tent_in, dinv_in, frame, near, odd, up, down, nbr, agg, blocks, sems
 ):
+    def pieces(source, first, out, at, sem):
+        return [
+            pltpu.make_async_copy(
+                source.at[:, first + c * 128 : first + (c + 1) * 128],
+                out.at[at + c * BS : at + (c + 1) * BS],
+                sems.at[sem + c],
+            )
+            for c in range(2)
+        ]
+
     small = [
         pltpu.make_async_copy(nbr_in, nbr, sems.at[0]),
         pltpu.make_async_copy(agg_in, agg, sems.at[1]),
     ]
-    rows = [pltpu.make_async_copy(blocks_in.at[i], blocks.at[i], sems.at[2 + i]) for i in range(RB)]
-    others = [
-        pltpu.make_async_copy(tent_in, tent, sems.at[2 + RB]),
-        pltpu.make_async_copy(dinv_in, dinv, sems.at[3 + RB]),
-    ]
-    for copy in small + others + rows:
+    tents = pieces(tent_in, 0, down, 0, 2) + pieces(tent_in, HALF, up, 0, 4)
+    dinvs = pieces(dinv_in, HALF, up, 2 * BS, 6)
+    rows = [
+        pltpu.make_async_copy(blocks_in.at[4 + i], blocks.at[i], sems.at[8 + i]) for i in range(4)
+    ]
+    for copy in small + tents + rows + dinvs:
         copy.start()
-    half = lane_half(BS)
-    for i in range(RB):
-        for c in range(6):
-            frame[i, c] = jnp.zeros((BS, 2 * BS), F32)
-    for copy in small + others:
+    for copy in small + tents:
         copy.wait()
     first = nbr[0, 0]
-    owner = first // 4
+    members = [agg[j] - first // 4 for j in range(RB)]
     odd[...] = jnp.full((8, 2 * BS), (first // RB) & 1, jnp.int32)
-    near[...] = place(
-        [tent[:, 2 * p * BS : 2 * (p + 1) * BS] for p in range(4)],
-        [agg[j] - owner for j in range(RB)],
-    )
-    for i in range(RB):
+    near[...] = place([piece(ref, c) for ref in (down, up) for c in range(2)], members)
+    row = lax.broadcasted_iota(jnp.int32, (8, 2 * BS), 0)
+    for out, at, mine in ((down, 2 * BS, members[:4]), (up, 9 * BS, members[4:])):
+        value = jnp.zeros((8, 2 * BS), F32)
+        for m, member in enumerate(mine):
+            value = jnp.where(row == m, member.astype(F32), value)
+        out[at : at + 8] = value
+    for i in range(4):
         rows[i].wait()
-        origin = first - 4 if i < 4 else first
-        mine = i + 4 if i < 4 else i
-        copies = doubled_row(blocks, i)
-        frame[i, mine // 2] = jnp.where(half == mine % 2, copies[0], 0.0)
-        for k in range(1, K):
-            at = nbr[i, k] - origin
-            column = at >> 1
-            frame[i, column] = frame[i, column] + jnp.where(half == (at & 1), copies[k], 0.0)
-
-    def send(out, pieces, members):
-        for c, value in enumerate(pieces):
-            out[c * BS : (c + 1) * BS] = value
-        row = lax.broadcasted_iota(jnp.int32, (8, 2 * BS), 0)
-        value = jnp.zeros((8, 2 * BS), F32)
-        for m, member in enumerate(members):
-            value = jnp.where(row == m, member.astype(F32), value)
-        out[len(pieces) * BS : len(pieces) * BS + 8] = value
-
-    low = half == 0
-    send(
-        up,
-        [tent[:, 256:384], tent[:, 384:512], dinv[:, 256:384], dinv[:, 384:512]]
-        + [frame[7, 4], frame[7, 5], frame[6, 4]]
-        + [jnp.where(low, frame[6, 5], pltpu.roll(frame[4, 4], BS, 1)), frame[5, 4]],
-        [agg[4 + m] - owner for m in range(4)],
-    )
-    send(down, [tent[:, 0:128], tent[:, 128:256]], [agg[m] - owner for m in range(4)])
+        spread(nbr, blocks, frame, 4 + i, first)
+    for copy in dinvs:
+        copy.wait()
+    low = lane_half(BS) == 0
+    for c, value in enumerate(
+        [frame[3, 4], frame[3, 5], frame[2, 4]]
+        + [jnp.where(low, frame[2, 5], pltpu.roll(frame[0, 4], BS, 1)), frame[1, 4]]
+    ):
+        up[(4 + c) * BS : (5 + c) * BS] = value
     up[UP - HALF :] = own_prolong(
-        split(frame_columns(frame, 4, range(0, 4))),
+        split(frame_columns(frame, range(0, 4))),
         near[...],
-        split(block_diagonal(dinv[:, 256:384], dinv[:, 384:512])),
+        split(block_diagonal(piece(up, 2), piece(up, 3))),
         slice(HALF, 2 * HALF),
     )
 
 
 def own_kernel(
-    frame, dinv, near, up, a_high, a_low, factors, inner, outer, cross, crossed, own, image
+    nbr_in,
+    blocks_in,
+    dinv_in,
+    frame,
+    near,
+    up,
+    a_high,
+    a_low,
+    factors,
+    inner,
+    outer,
+    cross,
+    crossed,
+    own,
+    image,
+    nbr,
+    blocks,
+    dinv,
+    low_frame,
+    sems,
 ):
-    lower = split(frame_columns(frame, 0, range(2, 6)))
-    upper = split(frame_columns(frame, 4, range(0, 4)))
+    copies = [
+        pltpu.make_async_copy(nbr_in, nbr, sems.at[0]),
+        pltpu.make_async_copy(blocks_in.at[:4], blocks, sems.at[1]),
+        pltpu.make_async_copy(dinv_in.at[:, :HALF], dinv, sems.at[2]),
+    ]
+    for copy in copies:
+        copy.start()
+    upper = split(frame_columns(frame, range(0, 4)))
+    inverse = [None, split(block_diagonal(piece(up, 2), piece(up, 3)))]
+    edge = [None, split(frame_columns(frame, (4, 5)))]
+    for copy in copies:
+        copy.wait()
+    for i in range(4):
+        spread(nbr, blocks, low_frame, i, nbr[0, 0] - 4)
+    lower = split(frame_columns(low_frame, range(2, 6)))
+    inverse[0] = split(block_diagonal(dinv[:, :128], dinv[:, 128:]))
+    edge[0] = split(frame_columns(low_frame, (0, 1)))
     a = [jnp.concatenate([x, y], 0) for x, y in zip(lower, upper)]
     a_high[...], a_low[...] = a
-    inverse = [
-        split(block_diagonal(dinv[:, s * HALF : s * HALF + 128], dinv[:, s * HALF + 128 : (s + 1) * HALF]))
-        for s in range(2)
-    ]
     c_low = own_prolong(lower, near[...], inverse[0], slice(0, HALF))
-    edge = [split(frame_columns(frame, 0, (0, 1))), split(frame_columns(frame, 4, (4, 5)))]
     both = []
     for s in range(2):
         factor = -OMEGA * dot3(inverse[s], edge[s])
@@ -232,7 +265,7 @@
 
 
 def middle_kernel(
-    a_high, a_low, factors, crossed, own, image, above, side, far, moved, part, slots
+    a_high, a_low, factors, crossed, own, image, above, side, far, moved, part
 ):
     b_high = dot3(split(factors[1]), split(received_place(above, 2 * BS)))
     left = dot3((a_high[:, :HALF], a_low[:, :HALF]), split(side[...]))
@@ -243,13 +276,11 @@
     )
     part[:, : 2 * AGG] = middle[:, : 2 * AGG] + lower
     part[:, 2 * AGG :] = middle[:, 2 * AGG :]
-    for g in range(RB):
-        slots[g] = jnp.zeros((SLOT, 8, 2 * BS), F32)
-
-
-def finish_kernel(nbr, target, odd, part, early, late, empty, out):
-    del empty
+
+
+def finish_kernel(nbr, target, odd, part, early, late, *outs):
     first_id = nbr[0, 0] // 4
+    here = (nbr[0, 0] // RB) % RB
     upward = odd[:1] == 1
     below = [
         jnp.where(upward, late[c * AGG : (c + 1) * AGG], early[c * AGG : (c + 1) * AGG])
@@ -266,23 +297,57 @@
         part[:, 2 * AGG :] + above[1],
         above[2],
     ]
-    for u in range(NA):
-        g = target[u]
+    numbers = [jnp.full((8, 2 * BS), first_id + (u + 1), jnp.int32).astype(F32) for u in range(NA)]
+    shifts = [(target[u] - here) & (RB - 1) for u in range(NA)]
+    for shift, out in enumerate(outs):
+        used = [jnp.full((8, 2 * BS), shifts[u], jnp.int32) == shift for u in range(NA)]
+
+        def chosen(first, second):
+            return jnp.where(used[0], first, jnp.where(used[1], second, 0.0))
+
         for r in range(8):
             for c in range(5):
-                out[g, 5 * r + c] = band[c][u * BS + 8 * r : u * BS + 8 * (r + 1)]
-        out[g, SLOT - 1] = jnp.full((8, 2 * BS), first_id + (u + 1), jnp.int32).astype(F32)
-
-
-def unpack_kernel(got, rows, ids, sem):
-    copy = pltpu.make_async_copy(got.at[:, : SLOT - 1], rows, sem)
-    copy.start()
+                out[5 * r + c] = chosen(
+                    *[band[c][u * BS + 8 * r : u * BS + 8 * (r + 1)] for u in range(NA)]
+                )
+        out[SLOT - 1] = chosen(*numbers)
+
+
+def unpack(got, shifts, rows, sems, found):
+    here = lax.axis_index("gy")
+    copies = []
+    sources = [(here - shift) & (RB - 1) for shift in shifts]
+    for k, (source, ref) in enumerate(zip(sources, got)):
+        copies.append(pltpu.make_async_copy(ref.at[: SLOT - 1], rows.at[source], sems.at[k]))
+        copies[-1].start()
     lane = lax.broadcasted_iota(jnp.int32, (1, 2 * BS), 1)
-    found = jnp.zeros((1, 2 * BS), F32)
-    for s in range(RB):
-        found = jnp.where(lane == s, got[s, SLOT - 1, :1], found)
-    ids[...] = (found.astype(jnp.int32) - 1)[0, :RB]
-    copy.wait()
+    for source, ref in zip(sources, got):
+        found = jnp.where(lane == source, ref[SLOT - 1, :1], found)
+    return copies, found
+
+
+def unpack_first_kernel(*refs):
+    got, (rows, found, sems) = refs[: len(EARLY)], refs[len(EARLY) :]
+    copies, numbers = unpack(got, EARLY, rows, sems, jnp.zeros((1, 2 * BS), F32))
+    found[...] = numbers
+    for copy in copies:
+        copy.wait()
+
+
+def unpack_second_kernel(begun, found, *refs):
+    del begun
+    got, (rows, ids, numbers, sems) = refs[: len(LATE)], refs[len(LATE) :]
+    copies, held = unpack(got, LATE, rows, sems, found[...])
+    numbers[...] = (held.astype(jnp.int32) - 1)[0, :RB]
+    copies.append(pltpu.make_async_copy(numbers, ids, sems.at[len(LATE)]))
+    copies[-1].start()
+    for copy in copies:
+        copy.wait()
+
+
+SHIFTS = (4, 3, 5, 2, 6, 1, 7)
+EARLY = (0,) + SHIFTS[:5]
+LATE = SHIFTS[5:]
 
 
 VMEM = pl.BlockSpec(memory_space=pltpu.VMEM)
@@ -314,15 +379,15 @@
     downward = [(j, i) for i, j in upward]
     tall = (VMEM, (2 * HALF, AGG), F32)
     square = (VMEM, (HALF, HALF), F32)
-    frame, dinv, near, odd, up, down = call(
+    pinned = [
+        (HBM, pltpu.with_memory_space_constraint(x, pltpu.HBM))
+        for x in (neighbors, aggregate, blocks, tentative, inv_diagonal)
+    ]
+    frame, near, odd, up, down = call(
         frame_kernel,
+        pinned,
         [
-            (HBM, pltpu.with_memory_space_constraint(x, pltpu.HBM))
-            for x in (neighbors, aggregate, blocks, tentative, inv_diagonal)
-        ],
-        [
-            (VMEM, (RB, 6, BS, 2 * BS), F32),
-            (VMEM, (BS, RB * BS), F32),
+            (VMEM, (4, 6, BS, 2 * BS), F32),
             tall,
             (VMEM, (8, 2 * BS), jnp.int32),
             (VMEM, (UP, 2 * BS), F32),
@@ -331,16 +396,15 @@
         [
             pltpu.SMEM((RB, K), jnp.int32),
             pltpu.SMEM((RB,), jnp.int32),
-            pltpu.VMEM((RB, BS, K * BS), F32),
-            pltpu.VMEM((BS, RB * BS), F32),
-            pltpu.SemaphoreType.DMA((4 + RB,)),
+            pltpu.VMEM((4, BS, K * BS), F32),
+            pltpu.SemaphoreType.DMA((12,)),
         ],
     )
     below = lax.ppermute(up, axes, upward)
     above = lax.ppermute(down, axes, downward)
     a_high, a_low, factors, inner, outer, cross, crossed, own, image = call(
         own_kernel,
-        on_chip(frame, dinv, near, up),
+        [pinned[0], pinned[2], pinned[4]] + on_chip(frame, near, up),
         [
             (VMEM, (2 * HALF, 2 * HALF), BF16),
             (VMEM, (2 * HALF, 2 * HALF), BF16),
@@ -352,6 +416,13 @@
             tall,
             tall,
         ],
+        [
+            pltpu.SMEM((RB, K), jnp.int32),
+            pltpu.VMEM((4, BS, K * BS), F32),
+            pltpu.VMEM((BS, HALF), F32),
+            pltpu.VMEM((4, 6, BS, 2 * BS), F32),
+            pltpu.SemaphoreType.DMA((3,)),
+        ],
     )
     side, far, moved, early, late = call(
         edge_kernel,
@@ -362,24 +433,34 @@
     even_pairs = [(i, i ^ 1) for i in range(devices)]
     early = lax.ppermute(early, axes, odd_pairs)
     late = lax.ppermute(late, axes, even_pairs)
-    slots_out = (VMEM, (RB, SLOT, 8, 2 * BS), F32)
-    part, slots = call(
+    (part,) = call(
         middle_kernel,
         on_chip(a_high, a_low, factors, crossed, own, image, above, side, far, moved),
-        [(VMEM, (AGG, 3 * AGG), F32), slots_out],
-    )
-    (slots,) = call(
+        [(VMEM, (AGG, 3 * AGG), F32)],
+    )
+    slots = call(
         finish_kernel,
-        [(SMEM, neighbors), (SMEM, target)] + on_chip(odd, part, early, late, slots),
-        [slots_out],
-        aliases={6: 0},
-    )
-    got = lax.all_to_all(slots, "gy", split_axis=0, concat_axis=0, tiled=True)
+        [(SMEM, neighbors), (SMEM, target)] + on_chip(odd, part, early, late),
+        [(VMEM, (SLOT, 8, 2 * BS), F32)] * RB,
+    )
+    got = {0: slots[0]}
+    for shift in SHIFTS:
+        pairs = [(i, (i + shift) % RB) for i in range(RB)]
+        got[shift] = lax.ppermute(slots[shift], "gy", pairs)
+    rows_out = (HBM, (RB, SLOT - 1, 8, 2 * BS), F32)
+    begun, found = call(
+        unpack_first_kernel,
+        on_chip(*[got[shift] for shift in EARLY]),
+        [rows_out, (VMEM, (1, 2 * BS), F32)],
+        [pltpu.SemaphoreType.DMA((len(EARLY),))],
+    )
     tiles, ids = call(
-        unpack_kernel,
-        on_chip(got),
-        [(HBM, (RB, SLOT - 1, 8, 2 * BS), F32), (VMEM, (RB,), jnp.int32)],
-        [pltpu.SemaphoreType.DMA(())],
+        unpack_second_kernel,
+        [(HBM, pltpu.with_memory_space_constraint(begun, pltpu.HBM))]
+        + on_chip(found, *[got[shift] for shift in LATE]),
+        [rows_out, (HBM, (RB,), jnp.int32)],
+        [pltpu.VMEM((RB,), jnp.int32), pltpu.SemaphoreType.DMA((len(LATE) + 1,))],
+        aliases={0: 0},
     )
     rows = tiles.reshape(RB * BS // 8, AW // 128, 8, 128).transpose(0, 2, 1, 3)
     return rows.reshape(RB * BS, AW), ids

time: 76.2 us -> 72.6 us (0.953)
  the two profiles are of different devices: /device:TPU:199 before, /device:TPU:1 now
where the time goes in v4:
time: 72.6 us; the launch traced here: 72.1 us
  starting transfers between devices  36.5 us (50%)
  waiting for transfers between devices  22.5 us (31%)
  Pallas kernels  12.4 us (17%)
  between operations  0.81 us (1%)
    ppermute x7, starting transfers between devices, body(): got[shift] = lax.ppermute(slots[shift], 'gy', pairs)  23 us
    ppermute x7, waiting for transfers between devices, body(): got[shift] = lax.ppermute(slots[shift], 'gy', pairs)  13.1 us
    pallas_call x7, Pallas kernels, call(): pl.pallas_call(kernel, in_specs=[memory for memory, _ in ins], out_specs=...  12.4 us
    ppermute x1, starting transfers between devices, body(): above = lax.ppermute(down, axes, downward)  4.37 us
    ppermute x1, waiting for transfers between devices, body(): below = lax.ppermute(up, axes, upward)  4.19 us
    ppermute x1, starting transfers between devices, body(): below = lax.ppermute(up, axes, upward)  4.04 us
    ppermute x1, starting transfers between devices, body(): early = lax.ppermute(early, axes, odd_pairs)  3.21 us
    ppermute x1, waiting for transfers between devices, body(): early = lax.ppermute(early, axes, odd_pairs)  2.72 us
  transfers between devices with their start and end apart: 11, of which 7 were waited for; matrix products, arithmetic and copies ran while one was open for 0% of the time, Pallas kernels for 9%

profile of v4, /device:TPU:1, one launch (start us, length us, event | category | flops | bytes accessed | tf_op | source)
XLA Modules:
  0.0 72.1 jit_solution(17989254055773892967)
XLA Ops:
  0.6 2.2 %frame_kernel.1 = (f32[4,6,64,128]{3,2,1,0:T(8,128)S(1)}, f32[512,128]{1,0:T(8,128)S(1)}, s32[8,128]{1,0:T(8,128)S(1)}, f32[840,128]{1,0:T(8,128)S(1)}, f32[136,128]{1,0:T(8,128)S(1)}) custom-call(s32[8,7]{1,0:T(8,128)} %nbr.1, s32[8]{0:T(128)} %agg_in.1, f32[8,64,448]{2,1,0:T(8,128)} %blocks_in.3, f32[64,512]{1,0:T(8,128)} %tent_in.1, f32[64,512]{1,0:T(8,128)} %dinv_in.3), custom_call_target="tpu_custom_call" | custom-call | tf_op jit(solution)/shard_map/frame_kernel/pallas_call | solution.py:359
  2.9 4.0 %collective-permute-start.1 = (f32[840,128]{1,0:T(8,128)S(1)}, f32[840,128]{1,0:T(8,128)S(1)}, u32[]{:S(2)}, u32[]{:S(2)}) collective-permute-start(f32[840,128]{1,0:T(8,128)S(1)} %get-tuple-element.36.up), channel_id=1, source_target_pairs={{0,1},{1,2},{2,3},{3,4},{4,5},{5,6},{6,7},{7,8},{8,9},{9,10},{10,1... | collective-permute-start | bytes 1290248 | tf_op jit(solution)/shard_map/ppermute | solution.py:403
  6.9 4.4 %collective-permute-start = (f32[136,128]{1,0:T(8,128)S(1)}, f32[136,128]{1,0:T(8,128)S(1)}, u32[]{:S(2)}, u32[]{:S(2)}) collective-permute-start(f32[136,128]{1,0:T(8,128)S(1)} %get-tuple-element.43), channel_id=1, source_target_pairs={{1,0},{2,1},{3,2},{4,3},{5,4},{6,5},{7,6},{8,7},{9,8},{10,9},{11,1... | collective-permute-start | bytes 208904 | tf_op jit(solution)/shard_map/ppermute | solution.py:404
  11.3 4.2 %own_kernel.1 = (bf16[512,512]{1,0:T(8,128)(2,1)S(1)}, bf16[512,512]{1,0:T(8,128)(2,1)S(1)}, f32[2,256,256]{2,1,0:T(8,128)S(1)}, f32[2,2,256,256]{3,2,1,0:T(8,12...) custom-call(s32[8,7]{1,0:T(8,128)} %nbr.1, ...), custom_call_target="tpu_custom_call" | custom-call | tf_op jit(solution)/shard_map/own_kernel/pallas_call | solution.py:359
  15.5 4.2 %collective-permute-done.1.below = f32[840,128]{1,0:T(8,128)S(1)} collective-permute-done((f32[840,128]{1,0:T(8,128)S(1)}, f32[840,128]{1,0:T(8,128)S(1)}, u32[]{:S(2)}, u32[]{:S(2)}) %collective-permute-start.1) | collective-permute-done | bytes 430112 | tf_op jit(solution)/shard_map/ppermute | solution.py:403
  19.7 2.1 %edge_kernel.1 = (f32[256,128]{1,0:T(8,128)S(1)}, f32[256,256]{1,0:T(8,128)S(1)}, f32[256,256]{1,0:T(8,128)S(1)}, f32[384,128]{1,0:T(8,128)S(1)}, f32[384,128]{1,0:T(8,128)S(1)}) custom-call(s32[8,128]{1,0:T(8,128)S(1)} %get-tuple-element.33.odd, f32[2,2,256,256]{3,2,1,0:T(8,128)S(1)} %get-tuple-element.44.inner, ...), custom_call_target="tpu_custom_call" | custom-call | tf_op jit(solution)/shard_map/edge_kernel/pallas_call | solution.py:359
  21.8 3.2 %collective-permute-start.2 = (f32[384,128]{1,0:T(8,128)S(1)}, f32[384,128]{1,0:T(8,128)S(1)}, u32[]{:S(2)}, u32[]{:S(2)}) collective-permute-start(f32[384,128]{1,0:T(8,128)S(1)} %get-tuple-element.50), channel_id=1, source_target_pairs={{1,2},{2,1},{3,4},{4,3},{5,6},{6,5},{7,8},{8,7},{9,10},{10,9},{11,... | collective-permute-start | bytes 589832 | tf_op jit(solution)/shard_map/ppermute | solution.py:434
  25.0 1.9 %collective-permute-start.3 = (f32[384,128]{1,0:T(8,128)S(1)}, f32[384,128]{1,0:T(8,128)S(1)}, u32[]{:S(2)}, u32[]{:S(2)}) collective-permute-start(f32[384,128]{1,0:T(8,128)S(1)} %get-tuple-element.51), channel_id=1, source_target_pairs={{0,1},{1,0},{2,3},{3,2},{4,5},{5,4},{6,7},{7,6},{8,9},{9,8},{10,11... | collective-permute-start | bytes 589832 | tf_op jit(solution)/shard_map/ppermute | solution.py:435
  26.9 1.4 %middle_kernel.1.part = f32[128,384]{1,0:T(8,128)S(1)} custom-call(bf16[512,512]{1,0:T(8,128)(2,1)S(1)} %get-tuple-element.37.a_high, bf16[512,512]{1,0:T(8,128)(2,1)S(1)} %get-tuple-element.38.a_low, f32[2,256,256]{2,1,0:T(8,128)S(1)} %get-tuple-element.39.factors, f32[128,256]{1,0:T(8,128)S(1)} %get-tuple-element.40.crossed, ...), custom_call_target="tpu_custom_call" | custom-call | tf_op jit(solution)/shard_map/middle_kernel/pallas_call | solution.py:359
  28.3 2.7 %collective-permute-done.2.early = f32[384,128]{1,0:T(8,128)S(1)} collective-permute-done((f32[384,128]{1,0:T(8,128)S(1)}, f32[384,128]{1,0:T(8,128)S(1)}, u32[]{:S(2)}, u32[]{:S(2)}) %collective-permute-start.2) | collective-permute-done | bytes 196640 | tf_op jit(solution)/shard_map/ppermute | solution.py:434
  31.0 2.4 %collective-permute-done.3.late = f32[384,128]{1,0:T(8,128)S(1)} collective-permute-done((f32[384,128]{1,0:T(8,128)S(1)}, f32[384,128]{1,0:T(8,128)S(1)}, u32[]{:S(2)}, u32[]{:S(2)}) %collective-permute-start.3) | collective-permute-done | bytes 196640 | tf_op jit(solution)/shard_map/ppermute | solution.py:435
  34.2 2.3 %collective-permute-start.4 = (f32[41,8,128]{2,1,0:T(8,128)S(1)}, f32[41,8,128]{2,1,0:T(8,128)S(1)}, u32[]{:S(2)}, u32[]{:S(2)}) collective-permute-start(f32[41,8,128]{2,1,0:T(8,128)S(1)} %get-tuple-element.53), channel_id=1, source_target_pairs={{0,4},{1,5},{2,6},{3,7},{4,0},{5,1},{6,2},{7,3},{8,12},{9,13},{10,... | collective-permute-start | bytes 503816 | tf_op jit(solution)/shard_map/ppermute | solution.py:449
  36.5 6.8 %collective-permute-start.5 = (f32[41,8,128]{2,1,0:T(8,128)S(1)}, f32[41,8,128]{2,1,0:T(8,128)S(1)}, u32[]{:S(2)}, u32[]{:S(2)}) collective-permute-start(f32[41,8,128]{2,1,0:T(8,128)S(1)} %get-tuple-element.54), channel_id=1, source_target_pairs={{0,3},{1,4},{2,5},{3,6},{4,7},{5,0},{6,1},{7,2},{8,11},{9,12},{10,... | collective-permute-start | bytes 503816 | tf_op jit(solution)/shard_map/ppermute | solution.py:449
  43.3 1.9 %collective-permute-start.6 = (f32[41,8,128]{2,1,0:T(8,128)S(1)}, f32[41,8,128]{2,1,0:T(8,128)S(1)}, u32[]{:S(2)}, u32[]{:S(2)}) collective-permute-start(f32[41,8,128]{2,1,0:T(8,128)S(1)} %get-tuple-element.55), channel_id=1, source_target_pairs={{0,5},{1,6},{2,7},{3,0},{4,1},{5,2},{6,3},{7,4},{8,13},{9,14},{10,... | collective-permute-start | bytes 503816 | tf_op jit(solution)/shard_map/ppermute | solution.py:449
  45.2 6.2 %collective-permute-start.7 = (f32[41,8,128]{2,1,0:T(8,128)S(1)}, f32[41,8,128]{2,1,0:T(8,128)S(1)}, u32[]{:S(2)}, u32[]{:S(2)}) collective-permute-start(f32[41,8,128]{2,1,0:T(8,128)S(1)} %get-tuple-element.56), channel_id=1, source_target_pairs={{0,2},{1,3},{2,4},{3,5},{4,6},{5,7},{6,0},{7,1},{8,10},{9,11},{10,... | collective-permute-start | bytes 503816 | tf_op jit(solution)/shard_map/ppermute | solution.py:449
  51.4 1.9 %collective-permute-start.8 = (f32[41,8,128]{2,1,0:T(8,128)S(1)}, f32[41,8,128]{2,1,0:T(8,128)S(1)}, u32[]{:S(2)}, u32[]{:S(2)}) collective-permute-start(f32[41,8,128]{2,1,0:T(8,128)S(1)} %get-tuple-element.57), channel_id=1, source_target_pairs={{0,6},{1,7},{2,0},{3,1},{4,2},{5,3},{6,4},{7,5},{8,14},{9,15},{10,... | collective-permute-start | bytes 503816 | tf_op jit(solution)/shard_map/ppermute | solution.py:449
  53.4 1.9 %collective-permute-start.9 = (f32[41,8,128]{2,1,0:T(8,128)S(1)}, f32[41,8,128]{2,1,0:T(8,128)S(1)}, u32[]{:S(2)}, u32[]{:S(2)}) collective-permute-start(f32[41,8,128]{2,1,0:T(8,128)S(1)} %get-tuple-element.60), channel_id=1, source_target_pairs={{0,1},{1,2},{2,3},{3,4},{4,5},{5,6},{6,7},{7,0},{8,9},{9,10},{10,1... | collective-permute-start | bytes 503816 | tf_op jit(solution)/shard_map/ppermute | solution.py:449
  55.3 5.9 %collective-permute-done.5.refs_2_ = f32[41,8,128]{2,1,0:T(8,128)S(1)} collective-permute-done((f32[41,8,128]{2,1,0:T(8,128)S(1)}, f32[41,8,128]{2,1,0:T(8,128)S(1)}, u32[]{:S(2)}, u32[]{:S(2)}) %collective-permute-start.5) | collective-permute-done | bytes 167968 | tf_op jit(solution)/shard_map/ppermute | solution.py:449
  61.2 1.9 %collective-permute-start.10 = (f32[41,8,128]{2,1,0:T(8,128)S(1)}, f32[41,8,128]{2,1,0:T(8,128)S(1)}, u32[]{:S(2)}, u32[]{:S(2)}) collective-permute-start(f32[41,8,128]{2,1,0:T(8,128)S(1)} %get-tuple-element.61), channel_id=1, source_target_pairs={{0,7},{1,0},{2,1},{3,2},{4,3},{5,4},{6,5},{7,6},{8,15},{9,8},{10,9... | collective-permute-start | bytes 503816 | tf_op jit(solution)/shard_map/ppermute | solution.py:449
  63.1 4.5 %collective-permute-done.8.refs_5_ = f32[41,8,128]{2,1,0:T(8,128)S(1)} collective-permute-done((f32[41,8,128]{2,1,0:T(8,128)S(1)}, f32[41,8,128]{2,1,0:T(8,128)S(1)}, u32[]{:S(2)}, u32[]{:S(2)}) %collective-permute-start.8) | collective-permute-done | bytes 167968 | tf_op jit(solution)/shard_map/ppermute | solution.py:449
  67.7 1.0 %unpack_first_kernel.1 = (f32[8,40,8,128]{3,2,1,0:T(8,128)}, f32[1,128]{1,0:T(1,128)S(1)}) custom-call(f32[41,8,128]{2,1,0:T(8,128)S(1)} %get-tuple-element.52.refs_0_, f32[41,8,128]{2,1,0:T(8,128)S(1)} %collective-permute-done.4.refs_1_, f32[41,8,128]{2,1,0:T(8,128)S(1)} %collective-permute-done.5.refs_2_, ...), custom_call_target="tpu_custom_call" | custom-call | tf_op jit(solution)/shard_map/unpack_first_kernel/pallas_call | solution.py:359
  68.7 1.1 %collective-permute-done.9.refs_0_ = f32[41,8,128]{2,1,0:T(8,128)S(1)} collective-permute-done((f32[41,8,128]{2,1,0:T(8,128)S(1)}, f32[41,8,128]{2,1,0:T(8,128)S(1)}, u32[]{:S(2)}, u32[]{:S(2)}) %collective-permute-start.9) | collective-permute-done | bytes 167968 | tf_op jit(solution)/shard_map/ppermute | solution.py:449
  69.7 1.6 %collective-permute-done.10.refs_1_ = f32[41,8,128]{2,1,0:T(8,128)S(1)} collective-permute-done((f32[41,8,128]{2,1,0:T(8,128)S(1)}, f32[41,8,128]{2,1,0:T(8,128)S(1)}, u32[]{:S(2)}, u32[]{:S(2)}) %collective-permute-start.10) | collective-permute-done | bytes 167968 | tf_op jit(solution)/shard_map/ppermute | solution.py:449
  71.4 0.8 %unpack_second_kernel.1 = (f32[8,40,8,128]{3,2,1,0:T(8,128)}, s32[8]{0:T(128)}) custom-call(f32[8,40,8,128]{3,2,1,0:T(8,128)} %get-tuple-element.58.begun, f32[1,128]{1,0:T(1,128)S(1)} %get-tuple-element.59.found, f32[41,8,128]{2,1,0:T(8,128)S(1)} %collective-permute-done.9.refs_0_, ...), custom_call_target="tpu_custom_call", output_to_operand_aliasing={{0}: (0, {})} | custom-call | tf_op jit(solution)/shard_map/unpack_second_kernel/pallas_call | solution.py:359
  (9 shorter events, 0.8 us)
Async XLA Ops:
  2.9 16.8 %collective-permute-start.1 = (f32[840,128]{1,0:T(8,128)S(1)}, f32[840,128]{1,0:T(8,128)S(1)}, u32[]{:S(2)}, u32[]{:S(2)}) collective-permute-start(f32[840,128]{1,0:T(8,128)S(1)} %get-tuple-element.36.up), channel_id=1, source_target_pairs={{0,1},{1,2},{2,3},{3,4},{4,5},{5,6},{6,7},{7,8},{8,9},{9,10},{10,1... | collective-permute-start | bytes 1290248 | tf_op jit(solution)/shard_map/ppermute | solution.py:403
  6.9 8.6 %collective-permute-start = (f32[136,128]{1,0:T(8,128)S(1)}, f32[136,128]{1,0:T(8,128)S(1)}, u32[]{:S(2)}, u32[]{:S(2)}) collective-permute-start(f32[136,128]{1,0:T(8,128)S(1)} %get-tuple-element.43), channel_id=1, source_target_pairs={{1,0},{2,1},{3,2},{4,3},{5,4},{6,5},{7,6},{8,7},{9,8},{10,9},{11,1... | collective-permute-start | bytes 208904 | tf_op jit(solution)/shard_map/ppermute | solution.py:404
  21.8 9.3 %collective-permute-start.2 = (f32[384,128]{1,0:T(8,128)S(1)}, f32[384,128]{1,0:T(8,128)S(1)}, u32[]{:S(2)}, u32[]{:S(2)}) collective-permute-start(f32[384,128]{1,0:T(8,128)S(1)} %get-tuple-element.50), channel_id=1, source_target_pairs={{1,2},{2,1},{3,4},{4,3},{5,6},{6,5},{7,8},{8,7},{9,10},{10,9},{11,... | collective-permute-start | bytes 589832 | tf_op jit(solution)/shard_map/ppermute | solution.py:434
  25.0 8.5 %collective-permute-start.3 = (f32[384,128]{1,0:T(8,128)S(1)}, f32[384,128]{1,0:T(8,128)S(1)}, u32[]{:S(2)}, u32[]{:S(2)}) collective-permute-start(f32[384,128]{1,0:T(8,128)S(1)} %get-tuple-element.51), channel_id=1, source_target_pairs={{0,1},{1,0},{2,3},{3,2},{4,5},{5,4},{6,7},{7,6},{8,9},{9,8},{10,11... | collective-permute-start | bytes 589832 | tf_op jit(solution)/shard_map/ppermute | solution.py:435
  26.9 6.5 %copy-start = (s32[8,7]{1,0:T(8,128)S(1)}, s32[8,7]{1,0:T(8,128)}, u32[]{:S(2)}) copy-start(s32[8,7]{1,0:T(8,128)} %nbr.1) | copy-start | bytes 676
  26.9 6.5 %copy-start.1 = (s32[2]{0:T(128)S(1)}, s32[2]{0:T(128)}, u32[]{:S(2)}) copy-start(s32[2]{0:T(128)} %target.1) | copy-start | bytes 28
  34.2 19.2 %collective-permute-start.4 = (f32[41,8,128]{2,1,0:T(8,128)S(1)}, f32[41,8,128]{2,1,0:T(8,128)S(1)}, u32[]{:S(2)}, u32[]{:S(2)}) collective-permute-start(f32[41,8,128]{2,1,0:T(8,128)S(1)} %get-tuple-element.53), channel_id=1, source_target_pairs={{0,4},{1,5},{2,6},{3,7},{4,0},{5,1},{6,2},{7,3},{8,12},{9,13},{10,... | collective-permute-start | bytes 503816 | tf_op jit(solution)/shard_map/ppermute | solution.py:449
  36.5 24.7 %collective-permute-start.5 = (f32[41,8,128]{2,1,0:T(8,128)S(1)}, f32[41,8,128]{2,1,0:T(8,128)S(1)}, u32[]{:S(2)}, u32[]{:S(2)}) collective-permute-start(f32[41,8,128]{2,1,0:T(8,128)S(1)} %get-tuple-element.54), channel_id=1, source_target_pairs={{0,3},{1,4},{2,5},{3,6},{4,7},{5,0},{6,1},{7,2},{8,11},{9,12},{10,... | collective-permute-start | bytes 503816 | tf_op jit(solution)/shard_map/ppermute | solution.py:449
  43.3 19.8 %collective-permute-start.6 = (f32[41,8,128]{2,1,0:T(8,128)S(1)}, f32[41,8,128]{2,1,0:T(8,128)S(1)}, u32[]{:S(2)}, u32[]{:S(2)}) collective-permute-start(f32[41,8,128]{2,1,0:T(8,128)S(1)} %get-tuple-element.55), channel_id=1, source_target_pairs={{0,5},{1,6},{2,7},{3,0},{4,1},{5,2},{6,3},{7,4},{8,13},{9,14},{10,... | collective-permute-start | bytes 503816 | tf_op jit(solution)/shard_map/ppermute | solution.py:449
  45.2 17.9 %collective-permute-start.7 = (f32[41,8,128]{2,1,0:T(8,128)S(1)}, f32[41,8,128]{2,1,0:T(8,128)S(1)}, u32[]{:S(2)}, u32[]{:S(2)}) collective-permute-start(f32[41,8,128]{2,1,0:T(8,128)S(1)} %get-tuple-element.56), channel_id=1, source_target_pairs={{0,2},{1,3},{2,4},{3,5},{4,6},{5,7},{6,0},{7,1},{8,10},{9,11},{10,... | collective-permute-start | bytes 503816 | tf_op jit(solution)/shard_map/ppermute | solution.py:449
  51.4 16.2 %collective-permute-start.8 = (f32[41,8,128]{2,1,0:T(8,128)S(1)}, f32[41,8,128]{2,1,0:T(8,128)S(1)}, u32[]{:S(2)}, u32[]{:S(2)}) collective-permute-start(f32[41,8,128]{2,1,0:T(8,128)S(1)} %get-tuple-element.57), channel_id=1, source_target_pairs={{0,6},{1,7},{2,0},{3,1},{4,2},{5,3},{6,4},{7,5},{8,14},{9,15},{10,... | collective-permute-start | bytes 503816 | tf_op jit(solution)/shard_map/ppermute | solution.py:449
  53.4 16.4 %collective-permute-start.9 = (f32[41,8,128]{2,1,0:T(8,128)S(1)}, f32[41,8,128]{2,1,0:T(8,128)S(1)}, u32[]{:S(2)}, u32[]{:S(2)}) collective-permute-start(f32[41,8,128]{2,1,0:T(8,128)S(1)} %get-tuple-element.60), channel_id=1, source_target_pairs={{0,1},{1,2},{2,3},{3,4},{4,5},{5,6},{6,7},{7,0},{8,9},{9,10},{10,1... | collective-permute-start | bytes 503816 | tf_op jit(solution)/shard_map/ppermute | solution.py:449
  61.2 10.2 %collective-permute-start.10 = (f32[41,8,128]{2,1,0:T(8,128)S(1)}, f32[41,8,128]{2,1,0:T(8,128)S(1)}, u32[]{:S(2)}, u32[]{:S(2)}) collective-permute-start(f32[41,8,128]{2,1,0:T(8,128)S(1)} %get-tuple-element.61), channel_id=1, source_target_pairs={{0,7},{1,0},{2,1},{3,2},{4,3},{5,4},{6,5},{7,6},{8,15},{9,8},{10,9... | collective-permute-start | bytes 503816 | tf_op jit(solution)/shard_map/ppermute | solution.py:449

commit v5 on v4

--- a/solution.py
+++ b/solution.py
@@ -214,10 +214,35 @@
     crossed[...] = dot3(split(c_low), edge[0], 0)
 
 
+def above_kernel(a_high, a_low, factors, inner, outer, above, right, turned, late_terms):
+    placed = split(received_place(above, 2 * BS))
+    b_high = dot3(split(factors[1]), placed)
+    right[: 2 * HALF] = dot3((a_high[:, HALF:], a_low[:, HALF:]), split(b_high))
+    right[2 * HALF :] = dot3(split(inner[0, 1]), placed)
+    turned[...] = dot3(split(inner[1, 0]), placed, 0)
+    high = dot3(split(inner[1, 1]), placed)
+    late_terms[...] = dot3(placed, split(jnp.concatenate([outer[1], high], 1)), 0)
+
+
 def edge_kernel(
-    odd, inner, outer, cross, factors, near, own, below, above, side, far, moved, early, late
+    odd,
+    inner,
+    outer,
+    cross,
+    factors,
+    near,
+    own,
+    right,
+    turned,
+    late_terms,
+    below,
+    side,
+    far,
+    moved,
+    early,
+    late,
 ):
-    placed = [split(received_place(below, 9 * BS)), split(received_place(above, 2 * BS))]
+    placed = split(received_place(below, 9 * BS))
     low = lane_half(BS) == 0
     none = jnp.zeros((BS, 2 * BS), F32)
     seven = piece(below, 7)
@@ -237,7 +262,7 @@
     )
     inverse = split(block_diagonal(piece(below, 2), piece(below, 3)))
     b_below = -OMEGA * dot3(inverse, split(dot3(a_below, split(near[:HALF]))))
-    b_low = dot3(split(factors[0]), placed[0])
+    b_low = dot3(split(factors[0]), placed)
     image_low = dot3(a_below, split(jnp.concatenate([b_low, own[:HALF]], 1)))
     c_below = below[UP - HALF :]
     far_rows = jnp.concatenate([c_below, b_below], 1)
@@ -245,32 +270,31 @@
     far[...] = far_rows
     moved[...] = image_low
     across = dot3(split(cross[...]), split(far_rows))
-    terms = []
-    for s in range(2):
-        left, right = [dot3(split(inner[s, t]), placed[t]) for t in range(2)]
-        middle = outer[s]
-        if s == 0:
-            left = left + across[:, :AGG]
-            middle = middle + across[:, AGG:]
-        terms.append(dot3(placed[s], split(jnp.concatenate([left, middle, right], 1)), 0))
+    left = dot3(split(inner[0, 0]), placed) + across[:, :AGG]
+    middle = outer[0] + across[:, AGG:]
+    down_terms = dot3(
+        placed, split(jnp.concatenate([left, middle, right[2 * HALF :]], 1)), 0
+    )
     lower_terms = dot3(split(c_below), split(image_low), 0)
+    up_first = dot3(split(turned[...]), placed, 0)
     upward = odd[:1] == 1
     for c in range(3):
         columns = slice(c * AGG, (c + 1) * AGG)
-        down, up = terms[0][:, columns], terms[1][:, columns]
+        down = down_terms[:, columns]
         if c < 2:
             down = down + lower_terms[:, columns]
+        up = up_first if c == 0 else late_terms[:, (c - 1) * AGG : c * AGG]
         early[columns] = jnp.where(upward, up, down)
         late[columns] = jnp.where(upward, down, up)
 
 
 def middle_kernel(
-    a_high, a_low, factors, crossed, own, image, above, side, far, moved, part
+    a_high, a_low, crossed, own, image, right, side, far, moved, part
 ):
-    b_high = dot3(split(factors[1]), split(received_place(above, 2 * BS)))
     left = dot3((a_high[:, :HALF], a_low[:, :HALF]), split(side[...]))
-    right = dot3((a_high[:, HALF:], a_low[:, HALF:]), split(b_high))
-    middle = dot3(split(own[...]), split(jnp.concatenate([left, image[...], right], 1)), 0)
+    middle = dot3(
+        split(own[...]), split(jnp.concatenate([left, image[...], right[: 2 * HALF]], 1)), 0
+    )
     lower = dot3(split(far[:, AGG:]), split(moved[...]), 0) + dot3(
         split(crossed[...]), split(far[...])
     )
@@ -278,9 +302,9 @@
     part[:, 2 * AGG :] = middle[:, 2 * AGG :]
 
 
-def finish_kernel(nbr, target, odd, part, early, late, *outs):
-    first_id = nbr[0, 0] // 4
-    here = (nbr[0, 0] // RB) % RB
+def finish_kernel(target, odd, part, early, late, *outs):
+    here = lax.axis_index("gy")
+    first_id = (lax.axis_index("gx") * RB + here) * NA
     upward = odd[:1] == 1
     below = [
         jnp.where(upward, late[c * AGG : (c + 1) * AGG], early[c * AGG : (c + 1) * AGG])
@@ -345,7 +369,7 @@
         copy.wait()
 
 
-SHIFTS = (4, 3, 5, 2, 6, 1, 7)
+SHIFTS = (4, 2, 6, 3, 5, 1, 7)
 EARLY = (0,) + SHIFTS[:5]
 LATE = SHIFTS[5:]
 
@@ -424,9 +448,14 @@
             pltpu.SemaphoreType.DMA((3,)),
         ],
     )
+    right, turned, late_terms = call(
+        above_kernel,
+        on_chip(a_high, a_low, factors, inner, outer, above),
+        [(VMEM, (3 * HALF, AGG), F32), (VMEM, (HALF, AGG), F32), (VMEM, (AGG, 2 * AGG), F32)],
+    )
     side, far, moved, early, late = call(
         edge_kernel,
-        on_chip(odd, inner, outer, cross, factors, near, own, below, above),
+        on_chip(odd, inner, outer, cross, factors, near, own, right, turned, late_terms, below),
         [(VMEM, (HALF, AGG), F32), square, square] + [(VMEM, (3 * AGG, AGG), F32)] * 2,
     )
     odd_pairs = [(i, i + 1 if i % 2 else i - 1) for i in range(1, devices - 1)]
@@ -435,12 +464,12 @@
     late = lax.ppermute(late, axes, even_pairs)
     (part,) = call(
         middle_kernel,
-        on_chip(a_high, a_low, factors, crossed, own, image, above, side, far, moved),
+        on_chip(a_high, a_low, crossed, own, image, right, side, far, moved),
         [(VMEM, (AGG, 3 * AGG), F32)],
     )
     slots = call(
         finish_kernel,
-        [(SMEM, neighbors), (SMEM, target)] + on_chip(odd, part, early, late),
+        [(SMEM, target)] + on_chip(odd, part, early, late),
         [(VMEM, (SLOT, 8, 2 * BS), F32)] * RB,
     )
     got = {0: slots[0]}

time: 72.6 us -> 71.2 us (0.981)
  the two profiles are of different devices: /device:TPU:1 before, /device:TPU:259 now
where the time goes in v5:
time: 71.2 us; the launch traced here: 70.6 us
  starting transfers between devices  38.2 us (54%)
  waiting for transfers between devices  18.9 us (27%)
  Pallas kernels  12.7 us (18%)
  between operations  0.8 us (1%)
    ppermute x7, starting transfers between devices, body(): got[shift] = lax.ppermute(slots[shift], 'gy', pairs)  25.8 us
    pallas_call x8, Pallas kernels, call(): pl.pallas_call(kernel, in_specs=[memory for memory, _ in ins], out_specs=...  12.7 us
    ppermute x7, waiting for transfers between devices, body(): got[shift] = lax.ppermute(slots[shift], 'gy', pairs)  10 us
    ppermute x1, starting transfers between devices, body(): above = lax.ppermute(down, axes, downward)  4.37 us
    ppermute x1, waiting for transfers between devices, body(): early = lax.ppermute(early, axes, odd_pairs)  3.9 us
    ppermute x1, waiting for transfers between devices, body(): below = lax.ppermute(up, axes, upward)  3.24 us
    ppermute x1, starting transfers between devices, body(): below = lax.ppermute(up, axes, upward)  3.21 us
    ppermute x1, starting transfers between devices, body(): early = lax.ppermute(early, axes, odd_pairs)  2.92 us
  transfers between devices with their start and end apart: 11, of which 6 were waited for; matrix products, arithmetic and copies ran while one was open for 0% of the time, Pallas kernels for 11%

profile of v5, /device:TPU:259, one launch (start us, length us, event | category | flops | bytes accessed | tf_op | source)
XLA Modules:
  0.0 70.6 jit_solution(424696146391371361)
XLA Ops:
  0.6 2.2 %frame_kernel.1 = (f32[4,6,64,128]{3,2,1,0:T(8,128)S(1)}, f32[512,128]{1,0:T(8,128)S(1)}, s32[8,128]{1,0:T(8,128)S(1)}, f32[840,128]{1,0:T(8,128)S(1)}, f32[136,128]{1,0:T(8,128)S(1)}) custom-call(s32[8,7]{1,0:T(8,128)} %nbr_in.3, s32[8]{0:T(128)} %agg_in.1, f32[8,64,448]{2,1,0:T(8,128)} %blocks_in.3, f32[64,512]{1,0:T(8,128)} %tent_in.1, f32[64,512]{1,0:T(8,128)} %dinv_in.3), custom_call_target="tpu_custom_call" | custom-call | tf_op jit(solution)/shard_map/frame_kernel/pallas_call | solution.py:383
  2.9 3.2 %collective-permute-start.1 = (f32[840,128]{1,0:T(8,128)S(1)}, f32[840,128]{1,0:T(8,128)S(1)}, u32[]{:S(2)}, u32[]{:S(2)}) collective-permute-start(f32[840,128]{1,0:T(8,128)S(1)} %get-tuple-element.39.up), channel_id=1, source_target_pairs={{0,1},{1,2},{2,3},{3,4},{4,5},{5,6},{6,7},{7,8},{8,9},{9,10},{10,1... | collective-permute-start | bytes 1290248 | tf_op jit(solution)/shard_map/ppermute | solution.py:427
  6.1 4.4 %collective-permute-start = (f32[136,128]{1,0:T(8,128)S(1)}, f32[136,128]{1,0:T(8,128)S(1)}, u32[]{:S(2)}, u32[]{:S(2)}) collective-permute-start(f32[136,128]{1,0:T(8,128)S(1)} %get-tuple-element.48), channel_id=1, source_target_pairs={{1,0},{2,1},{3,2},{4,3},{5,4},{6,5},{7,6},{8,7},{9,8},{10,9},{11,1... | collective-permute-start | bytes 208904 | tf_op jit(solution)/shard_map/ppermute | solution.py:428
  10.5 4.2 %own_kernel.1 = (bf16[512,512]{1,0:T(8,128)(2,1)S(1)}, bf16[512,512]{1,0:T(8,128)(2,1)S(1)}, f32[2,256,256]{2,1,0:T(8,128)S(1)}, f32[2,2,256,256]{3,2,1,0:T(8,12...) custom-call(s32[8,7]{1,0:T(8,128)} %nbr_in.3, ...), custom_call_target="tpu_custom_call" | custom-call | tf_op jit(solution)/shard_map/own_kernel/pallas_call | solution.py:383
  14.7 1.2 %above_kernel.1 = (f32[768,128]{1,0:T(8,128)S(1)}, f32[256,128]{1,0:T(8,128)S(1)}, f32[128,256]{1,0:T(8,128)S(1)}) custom-call(bf16[512,512]{1,0:T(8,128)(2,1)S(1)} %get-tuple-element.40.a_high, bf16[512,512]{1,0:T(8,128)(2,1)S(1)} %get-tuple-element.41.a_low, f32[2,256,256]{2,1,0:T(8,128)S(1)} %get-tuple-element.45.factors, ...), custom_call_target="tpu_custom_call" | custom-call | tf_op jit(solution)/shard_map/above_kernel/pallas_call | solution.py:383
  15.9 3.2 %collective-permute-done.1.below = f32[840,128]{1,0:T(8,128)S(1)} collective-permute-done((f32[840,128]{1,0:T(8,128)S(1)}, f32[840,128]{1,0:T(8,128)S(1)}, u32[]{:S(2)}, u32[]{:S(2)}) %collective-permute-start.1) | collective-permute-done | bytes 430112 | tf_op jit(solution)/shard_map/ppermute | solution.py:427
  19.2 1.5 %edge_kernel.1 = (f32[256,128]{1,0:T(8,128)S(1)}, f32[256,256]{1,0:T(8,128)S(1)}, f32[256,256]{1,0:T(8,128)S(1)}, f32[384,128]{1,0:T(8,128)S(1)}, f32[384,128]{1,0:T(8,128)S(1)}) custom-call(s32[8,128]{1,0:T(8,128)S(1)} %get-tuple-element.36.odd, f32[2,2,256,256]{3,2,1,0:T(8,128)S(1)} %get-tuple-element.46.inner, ...), custom_call_target="tpu_custom_call" | custom-call | tf_op jit(solution)/shard_map/edge_kernel/pallas_call | solution.py:383
  20.7 2.9 %collective-permute-start.2 = (f32[384,128]{1,0:T(8,128)S(1)}, f32[384,128]{1,0:T(8,128)S(1)}, u32[]{:S(2)}, u32[]{:S(2)}) collective-permute-start(f32[384,128]{1,0:T(8,128)S(1)} %get-tuple-element.56), channel_id=1, source_target_pairs={{1,2},{2,1},{3,4},{4,3},{5,6},{6,5},{7,8},{8,7},{9,10},{10,9},{11,... | collective-permute-start | bytes 589832 | tf_op jit(solution)/shard_map/ppermute | solution.py:463
  23.6 1.9 %collective-permute-start.3 = (f32[384,128]{1,0:T(8,128)S(1)}, f32[384,128]{1,0:T(8,128)S(1)}, u32[]{:S(2)}, u32[]{:S(2)}) collective-permute-start(f32[384,128]{1,0:T(8,128)S(1)} %get-tuple-element.57), channel_id=1, source_target_pairs={{0,1},{1,0},{2,3},{3,2},{4,5},{5,4},{6,7},{7,6},{8,9},{9,8},{10,11... | collective-permute-start | bytes 589832 | tf_op jit(solution)/shard_map/ppermute | solution.py:464
  25.5 1.1 %middle_kernel.1.part = f32[128,384]{1,0:T(8,128)S(1)} custom-call(bf16[512,512]{1,0:T(8,128)(2,1)S(1)} %get-tuple-element.40.a_high, bf16[512,512]{1,0:T(8,128)(2,1)S(1)} %get-tuple-element.41.a_low, f32[128,256]{1,0:T(8,128)S(1)} %get-tuple-element.42.crossed, f32[512,128]{1,0:T(8,128)S(1)} %get-tuple-element.43.own, ...), custom_call_target="tpu_custom_call" | custom-call | tf_op jit(solution)/shard_map/middle_kernel/pallas_call | solution.py:383
  26.7 3.9 %collective-permute-done.2.early = f32[384,128]{1,0:T(8,128)S(1)} collective-permute-done((f32[384,128]{1,0:T(8,128)S(1)}, f32[384,128]{1,0:T(8,128)S(1)}, u32[]{:S(2)}, u32[]{:S(2)}) %collective-permute-start.2) | collective-permute-done | bytes 196640 | tf_op jit(solution)/shard_map/ppermute | solution.py:463
  30.6 1.7 %collective-permute-done.3.late = f32[384,128]{1,0:T(8,128)S(1)} collective-permute-done((f32[384,128]{1,0:T(8,128)S(1)}, f32[384,128]{1,0:T(8,128)S(1)}, u32[]{:S(2)}, u32[]{:S(2)}) %collective-permute-start.3) | collective-permute-done | bytes 196640 | tf_op jit(solution)/shard_map/ppermute | solution.py:464
  32.3 0.7 finish_kernel.1
  33.0 2.1 %collective-permute-start.4 = (f32[41,8,128]{2,1,0:T(8,128)S(1)}, f32[41,8,128]{2,1,0:T(8,128)S(1)}, u32[]{:S(2)}, u32[]{:S(2)}) collective-permute-start(f32[41,8,128]{2,1,0:T(8,128)S(1)} %get-tuple-element.59), channel_id=1, source_target_pairs={{0,4},{1,5},{2,6},{3,7},{4,0},{5,1},{6,2},{7,3},{8,12},{9,13},{10,... | collective-permute-start | bytes 503816 | tf_op jit(solution)/shard_map/ppermute | solution.py:478
  35.0 6.6 %collective-permute-start.5 = (f32[41,8,128]{2,1,0:T(8,128)S(1)}, f32[41,8,128]{2,1,0:T(8,128)S(1)}, u32[]{:S(2)}, u32[]{:S(2)}) collective-permute-start(f32[41,8,128]{2,1,0:T(8,128)S(1)} %get-tuple-element.60), channel_id=1, source_target_pairs={{0,2},{1,3},{2,4},{3,5},{4,6},{5,7},{6,0},{7,1},{8,10},{9,11},{10,... | collective-permute-start | bytes 503816 | tf_op jit(solution)/shard_map/ppermute | solution.py:478
  41.7 1.9 %collective-permute-start.6 = (f32[41,8,128]{2,1,0:T(8,128)S(1)}, f32[41,8,128]{2,1,0:T(8,128)S(1)}, u32[]{:S(2)}, u32[]{:S(2)}) collective-permute-start(f32[41,8,128]{2,1,0:T(8,128)S(1)} %get-tuple-element.61), channel_id=1, source_target_pairs={{0,6},{1,7},{2,0},{3,1},{4,2},{5,3},{6,4},{7,5},{8,14},{9,15},{10,... | collective-permute-start | bytes 503816 | tf_op jit(solution)/shard_map/ppermute | solution.py:478
  43.6 4.7 %collective-permute-start.7 = (f32[41,8,128]{2,1,0:T(8,128)S(1)}, f32[41,8,128]{2,1,0:T(8,128)S(1)}, u32[]{:S(2)}, u32[]{:S(2)}) collective-permute-start(f32[41,8,128]{2,1,0:T(8,128)S(1)} %get-tuple-element.62), channel_id=1, source_target_pairs={{0,3},{1,4},{2,5},{3,6},{4,7},{5,0},{6,1},{7,2},{8,11},{9,12},{10,... | collective-permute-start | bytes 503816 | tf_op jit(solution)/shard_map/ppermute | solution.py:478
  48.3 3.6 %collective-permute-start.8 = (f32[41,8,128]{2,1,0:T(8,128)S(1)}, f32[41,8,128]{2,1,0:T(8,128)S(1)}, u32[]{:S(2)}, u32[]{:S(2)}) collective-permute-start(f32[41,8,128]{2,1,0:T(8,128)S(1)} %get-tuple-element.63), channel_id=1, source_target_pairs={{0,5},{1,6},{2,7},{3,0},{4,1},{5,2},{6,3},{7,4},{8,13},{9,14},{10,... | collective-permute-start | bytes 503816 | tf_op jit(solution)/shard_map/ppermute | solution.py:478
  51.9 2.6 %collective-permute-start.9 = (f32[41,8,128]{2,1,0:T(8,128)S(1)}, f32[41,8,128]{2,1,0:T(8,128)S(1)}, u32[]{:S(2)}, u32[]{:S(2)}) collective-permute-start(f32[41,8,128]{2,1,0:T(8,128)S(1)} %get-tuple-element.66), channel_id=1, source_target_pairs={{0,1},{1,2},{2,3},{3,4},{4,5},{5,6},{6,7},{7,0},{8,9},{9,10},{10,1... | collective-permute-start | bytes 503816 | tf_op jit(solution)/shard_map/ppermute | solution.py:478
  54.6 4.3 %collective-permute-start.10 = (f32[41,8,128]{2,1,0:T(8,128)S(1)}, f32[41,8,128]{2,1,0:T(8,128)S(1)}, u32[]{:S(2)}, u32[]{:S(2)}) collective-permute-start(f32[41,8,128]{2,1,0:T(8,128)S(1)} %get-tuple-element.67), channel_id=1, source_target_pairs={{0,7},{1,0},{2,1},{3,2},{4,3},{5,4},{6,5},{7,6},{8,15},{9,8},{10,9... | collective-permute-start | bytes 503816 | tf_op jit(solution)/shard_map/ppermute | solution.py:478
  58.9 6.3 %collective-permute-done.7.refs_4_ = f32[41,8,128]{2,1,0:T(8,128)S(1)} collective-permute-done((f32[41,8,128]{2,1,0:T(8,128)S(1)}, f32[41,8,128]{2,1,0:T(8,128)S(1)}, u32[]{:S(2)}, u32[]{:S(2)}) %collective-permute-start.7) | collective-permute-done | bytes 167968 | tf_op jit(solution)/shard_map/ppermute | solution.py:478
  65.2 1.0 %unpack_first_kernel.1 = (f32[8,40,8,128]{3,2,1,0:T(8,128)}, f32[1,128]{1,0:T(1,128)S(1)}) custom-call(f32[41,8,128]{2,1,0:T(8,128)S(1)} %get-tuple-element.58.refs_0_, f32[41,8,128]{2,1,0:T(8,128)S(1)} %collective-permute-done.4.refs_1_, f32[41,8,128]{2,1,0:T(8,128)S(1)} %collective-permute-done.5.refs_2_, ...), custom_call_target="tpu_custom_call" | custom-call | tf_op jit(solution)/shard_map/unpack_first_kernel/pallas_call | solution.py:383
  66.8 3.1 %collective-permute-done.10.refs_1_ = f32[41,8,128]{2,1,0:T(8,128)S(1)} collective-permute-done((f32[41,8,128]{2,1,0:T(8,128)S(1)}, f32[41,8,128]{2,1,0:T(8,128)S(1)}, u32[]{:S(2)}, u32[]{:S(2)}) %collective-permute-start.10) | collective-permute-done | bytes 167968 | tf_op jit(solution)/shard_map/ppermute | solution.py:478
  69.9 0.8 %unpack_second_kernel.1 = (f32[8,40,8,128]{3,2,1,0:T(8,128)}, s32[8]{0:T(128)}) custom-call(f32[8,40,8,128]{3,2,1,0:T(8,128)} %get-tuple-element.64.begun, f32[1,128]{1,0:T(1,128)S(1)} %get-tuple-element.65.found, f32[41,8,128]{2,1,0:T(8,128)S(1)} %collective-permute-done.9.refs_0_, ...), custom_call_target="tpu_custom_call", output_to_operand_aliasing={{0}: (0, {})} | custom-call | tf_op jit(solution)/shard_map/unpack_second_kernel/pallas_call | solution.py:383
  (8 shorter events, 0.6 us)
Async XLA Ops:
  2.9 16.3 %collective-permute-start.1 = (f32[840,128]{1,0:T(8,128)S(1)}, f32[840,128]{1,0:T(8,128)S(1)}, u32[]{:S(2)}, u32[]{:S(2)}) collective-permute-start(f32[840,128]{1,0:T(8,128)S(1)} %get-tuple-element.39.up), channel_id=1, source_target_pairs={{0,1},{1,2},{2,3},{3,4},{4,5},{5,6},{6,7},{7,8},{8,9},{9,10},{10,1... | collective-permute-start | bytes 1290248 | tf_op jit(solution)/shard_map/ppermute | solution.py:427
  6.1 8.6 %collective-permute-start = (f32[136,128]{1,0:T(8,128)S(1)}, f32[136,128]{1,0:T(8,128)S(1)}, u32[]{:S(2)}, u32[]{:S(2)}) collective-permute-start(f32[136,128]{1,0:T(8,128)S(1)} %get-tuple-element.48), channel_id=1, source_target_pairs={{1,0},{2,1},{3,2},{4,3},{5,4},{6,5},{7,6},{8,7},{9,8},{10,9},{11,1... | collective-permute-start | bytes 208904 | tf_op jit(solution)/shard_map/ppermute | solution.py:428
  20.7 9.9 %collective-permute-start.2 = (f32[384,128]{1,0:T(8,128)S(1)}, f32[384,128]{1,0:T(8,128)S(1)}, u32[]{:S(2)}, u32[]{:S(2)}) collective-permute-start(f32[384,128]{1,0:T(8,128)S(1)} %get-tuple-element.56), channel_id=1, source_target_pairs={{1,2},{2,1},{3,4},{4,3},{5,6},{6,5},{7,8},{8,7},{9,10},{10,9},{11,... | collective-permute-start | bytes 589832 | tf_op jit(solution)/shard_map/ppermute | solution.py:463
  23.6 8.7 %collective-permute-start.3 = (f32[384,128]{1,0:T(8,128)S(1)}, f32[384,128]{1,0:T(8,128)S(1)}, u32[]{:S(2)}, u32[]{:S(2)}) collective-permute-start(f32[384,128]{1,0:T(8,128)S(1)} %get-tuple-element.57), channel_id=1, source_target_pairs={{0,1},{1,0},{2,3},{3,2},{4,5},{5,4},{6,7},{7,6},{8,9},{9,8},{10,11... | collective-permute-start | bytes 589832 | tf_op jit(solution)/shard_map/ppermute | solution.py:464
  25.5 6.8 %copy-start = (s32[2]{0:T(128)S(1)}, s32[2]{0:T(128)}, u32[]{:S(2)}) copy-start(s32[2]{0:T(128)} %target.1) | copy-start | bytes 28
  33.0 18.9 %collective-permute-start.4 = (f32[41,8,128]{2,1,0:T(8,128)S(1)}, f32[41,8,128]{2,1,0:T(8,128)S(1)}, u32[]{:S(2)}, u32[]{:S(2)}) collective-permute-start(f32[41,8,128]{2,1,0:T(8,128)S(1)} %get-tuple-element.59), channel_id=1, source_target_pairs={{0,4},{1,5},{2,6},{3,7},{4,0},{5,1},{6,2},{7,3},{8,12},{9,13},{10,... | collective-permute-start | bytes 503816 | tf_op jit(solution)/shard_map/ppermute | solution.py:478
  35.0 19.5 %collective-permute-start.5 = (f32[41,8,128]{2,1,0:T(8,128)S(1)}, f32[41,8,128]{2,1,0:T(8,128)S(1)}, u32[]{:S(2)}, u32[]{:S(2)}) collective-permute-start(f32[41,8,128]{2,1,0:T(8,128)S(1)} %get-tuple-element.60), channel_id=1, source_target_pairs={{0,2},{1,3},{2,4},{3,5},{4,6},{5,7},{6,0},{7,1},{8,10},{9,11},{10,... | collective-permute-start | bytes 503816 | tf_op jit(solution)/shard_map/ppermute | solution.py:478
  41.7 17.2 %collective-permute-start.6 = (f32[41,8,128]{2,1,0:T(8,128)S(1)}, f32[41,8,128]{2,1,0:T(8,128)S(1)}, u32[]{:S(2)}, u32[]{:S(2)}) collective-permute-start(f32[41,8,128]{2,1,0:T(8,128)S(1)} %get-tuple-element.61), channel_id=1, source_target_pairs={{0,6},{1,7},{2,0},{3,1},{4,2},{5,3},{6,4},{7,5},{8,14},{9,15},{10,... | collective-permute-start | bytes 503816 | tf_op jit(solution)/shard_map/ppermute | solution.py:478
  43.6 21.6 %collective-permute-start.7 = (f32[41,8,128]{2,1,0:T(8,128)S(1)}, f32[41,8,128]{2,1,0:T(8,128)S(1)}, u32[]{:S(2)}, u32[]{:S(2)}) collective-permute-start(f32[41,8,128]{2,1,0:T(8,128)S(1)} %get-tuple-element.62), channel_id=1, source_target_pairs={{0,3},{1,4},{2,5},{3,6},{4,7},{5,0},{6,1},{7,2},{8,11},{9,12},{10,... | collective-permute-start | bytes 503816 | tf_op jit(solution)/shard_map/ppermute | solution.py:478
  48.3 16.9 %collective-permute-start.8 = (f32[41,8,128]{2,1,0:T(8,128)S(1)}, f32[41,8,128]{2,1,0:T(8,128)S(1)}, u32[]{:S(2)}, u32[]{:S(2)}) collective-permute-start(f32[41,8,128]{2,1,0:T(8,128)S(1)} %get-tuple-element.63), channel_id=1, source_target_pairs={{0,5},{1,6},{2,7},{3,0},{4,1},{5,2},{6,3},{7,4},{8,13},{9,14},{10,... | collective-permute-start | bytes 503816 | tf_op jit(solution)/shard_map/ppermute | solution.py:478
  51.9 14.9 %collective-permute-start.9 = (f32[41,8,128]{2,1,0:T(8,128)S(1)}, f32[41,8,128]{2,1,0:T(8,128)S(1)}, u32[]{:S(2)}, u32[]{:S(2)}) collective-permute-start(f32[41,8,128]{2,1,0:T(8,128)S(1)} %get-tuple-element.66), channel_id=1, source_target_pairs={{0,1},{1,2},{2,3},{3,4},{4,5},{5,6},{6,7},{7,0},{8,9},{9,10},{10,1... | collective-permute-start | bytes 503816 | tf_op jit(solution)/shard_map/ppermute | solution.py:478
  54.6 15.3 %collective-permute-start.10 = (f32[41,8,128]{2,1,0:T(8,128)S(1)}, f32[41,8,128]{2,1,0:T(8,128)S(1)}, u32[]{:S(2)}, u32[]{:S(2)}) collective-permute-start(f32[41,8,128]{2,1,0:T(8,128)S(1)} %get-tuple-element.67), channel_id=1, source_target_pairs={{0,7},{1,0},{2,1},{3,2},{4,3},{5,4},{6,5},{7,6},{8,15},{9,8},{10,9... | collective-permute-start | bytes 503816 | tf_op jit(solution)/shard_map/ppermute | solution.py:478

commit v6 on v5

--- a/solution.py
+++ b/solution.py
@@ -29,7 +29,12 @@
     def dot(x, y):
         return lax.dot_general(x, y, (((side,), (0,)), ((), ())), preferred_element_type=F32)
 
-    return dot(a[0], b[0]) + (dot(a[0], b[1]) + dot(a[1], b[0]))
+    rows, columns = a[0].shape[1 - side], b[0].shape[1]
+    if columns == AGG:
+        both = dot(jnp.concatenate(a, 1 - side), jnp.concatenate(b, 1))
+        return both[:rows, :columns] + (both[:rows, columns:] + both[rows:, :columns])
+    both = dot(jnp.concatenate(a, 1 - side), b[0])
+    return both[:rows] + (dot(a[0], b[1]) + both[rows:])
 
 
 def lane_half(rows):

time: 71.2 us -> 70.8 us (level)
  the two profiles are of different devices: /device:TPU:259 before, /device:TPU:517 now
where the time goes in v6:
time: 70.8 us; the launch traced here: 70.3 us
  starting transfers between devices  37.6 us (53%)
  waiting for transfers between devices  19.8 us (28%)
  Pallas kernels  12.1 us (17%)
  between operations  0.82 us (1%)
    ppermute x7, starting transfers between devices, body(): got[shift] = lax.ppermute(slots[shift], 'gy', pairs)  25.2 us
    pallas_call x8, Pallas kernels, call(): pl.pallas_call(kernel, in_specs=[memory for memory, _ in ins], out_specs=...  12.1 us
    ppermute x7, waiting for transfers between devices, body(): got[shift] = lax.ppermute(slots[shift], 'gy', pairs)  10.6 us
    ppermute x1, starting transfers between devices, body(): above = lax.ppermute(down, axes, downward)  4.37 us
    ppermute x1, waiting for transfers between devices, body(): early = lax.ppermute(early, axes, odd_pairs)  4.35 us
    ppermute x1, waiting for transfers between devices, body(): below = lax.ppermute(up, axes, upward)  3.37 us
    ppermute x1, starting transfers between devices, body(): below = lax.ppermute(up, axes, upward)  3.2 us
    ppermute x1, starting transfers between devices, body(): early = lax.ppermute(early, axes, odd_pairs)  2.98 us
  transfers between devices with their start and end apart: 11, of which 5 were waited for; matrix products, arithmetic and copies ran while one was open for 0% of the time, Pallas kernels for 10%

profile of v6, /device:TPU:517, one launch (start us, length us, event | category | flops | bytes accessed | tf_op | source)
XLA Modules:
  0.0 70.3 jit_solution(11251234983036552513)
XLA Ops:
  0.6 2.2 %frame_kernel.1 = (f32[4,6,64,128]{3,2,1,0:T(8,128)S(1)}, f32[512,128]{1,0:T(8,128)S(1)}, s32[8,128]{1,0:T(8,128)S(1)}, f32[840,128]{1,0:T(8,128)S(1)}, f32[136,128]{1,0:T(8,128)S(1)}) custom-call(s32[8,7]{1,0:T(8,128)} %nbr_in.3, s32[8]{0:T(128)} %agg_in.1, f32[8,64,448]{2,1,0:T(8,128)} %blocks_in.3, f32[64,512]{1,0:T(8,128)} %tent_in.1, f32[64,512]{1,0:T(8,128)} %dinv_in.3), custom_call_target="tpu_custom_call" | custom-call | tf_op jit(solution)/shard_map/frame_kernel/pallas_call | solution.py:388
  2.8 3.2 %collective-permute-start.1 = (f32[840,128]{1,0:T(8,128)S(1)}, f32[840,128]{1,0:T(8,128)S(1)}, u32[]{:S(2)}, u32[]{:S(2)}) collective-permute-start(f32[840,128]{1,0:T(8,128)S(1)} %get-tuple-element.39.up), channel_id=1, source_target_pairs={{0,1},{1,2},{2,3},{3,4},{4,5},{5,6},{6,7},{7,8},{8,9},{9,10},{10,1... | collective-permute-start | bytes 1290248 | tf_op jit(solution)/shard_map/ppermute | solution.py:432
  6.0 4.4 %collective-permute-start = (f32[136,128]{1,0:T(8,128)S(1)}, f32[136,128]{1,0:T(8,128)S(1)}, u32[]{:S(2)}, u32[]{:S(2)}) collective-permute-start(f32[136,128]{1,0:T(8,128)S(1)} %get-tuple-element.48), channel_id=1, source_target_pairs={{1,0},{2,1},{3,2},{4,3},{5,4},{6,5},{7,6},{8,7},{9,8},{10,9},{11,1... | collective-permute-start | bytes 208904 | tf_op jit(solution)/shard_map/ppermute | solution.py:433
  10.4 4.1 %own_kernel.1 = (bf16[512,512]{1,0:T(8,128)(2,1)S(1)}, bf16[512,512]{1,0:T(8,128)(2,1)S(1)}, f32[2,256,256]{2,1,0:T(8,128)S(1)}, f32[2,2,256,256]{3,2,1,0:T(8,12...) custom-call(s32[8,7]{1,0:T(8,128)} %nbr_in.3, ...), custom_call_target="tpu_custom_call" | custom-call | tf_op jit(solution)/shard_map/own_kernel/pallas_call | solution.py:388
  14.5 1.1 %above_kernel.1 = (f32[768,128]{1,0:T(8,128)S(1)}, f32[256,128]{1,0:T(8,128)S(1)}, f32[128,256]{1,0:T(8,128)S(1)}) custom-call(bf16[512,512]{1,0:T(8,128)(2,1)S(1)} %get-tuple-element.40.a_high, bf16[512,512]{1,0:T(8,128)(2,1)S(1)} %get-tuple-element.41.a_low, f32[2,256,256]{2,1,0:T(8,128)S(1)} %get-tuple-element.45.factors, ...), custom_call_target="tpu_custom_call" | custom-call | tf_op jit(solution)/shard_map/above_kernel/pallas_call | solution.py:388
  15.7 3.4 %collective-permute-done.1.below = f32[840,128]{1,0:T(8,128)S(1)} collective-permute-done((f32[840,128]{1,0:T(8,128)S(1)}, f32[840,128]{1,0:T(8,128)S(1)}, u32[]{:S(2)}, u32[]{:S(2)}) %collective-permute-start.1) | collective-permute-done | bytes 430112 | tf_op jit(solution)/shard_map/ppermute | solution.py:432
  19.0 1.3 %edge_kernel.1 = (f32[256,128]{1,0:T(8,128)S(1)}, f32[256,256]{1,0:T(8,128)S(1)}, f32[256,256]{1,0:T(8,128)S(1)}, f32[384,128]{1,0:T(8,128)S(1)}, f32[384,128]{1,0:T(8,128)S(1)}) custom-call(s32[8,128]{1,0:T(8,128)S(1)} %get-tuple-element.36.odd, f32[2,2,256,256]{3,2,1,0:T(8,128)S(1)} %get-tuple-element.46.inner, ...), custom_call_target="tpu_custom_call" | custom-call | tf_op jit(solution)/shard_map/edge_kernel/pallas_call | solution.py:388
  20.3 3.0 %collective-permute-start.2 = (f32[384,128]{1,0:T(8,128)S(1)}, f32[384,128]{1,0:T(8,128)S(1)}, u32[]{:S(2)}, u32[]{:S(2)}) collective-permute-start(f32[384,128]{1,0:T(8,128)S(1)} %get-tuple-element.56), channel_id=1, source_target_pairs={{1,2},{2,1},{3,4},{4,3},{5,6},{6,5},{7,8},{8,7},{9,10},{10,9},{11,... | collective-permute-start | bytes 589832 | tf_op jit(solution)/shard_map/ppermute | solution.py:468
  23.3 1.9 %collective-permute-start.3 = (f32[384,128]{1,0:T(8,128)S(1)}, f32[384,128]{1,0:T(8,128)S(1)}, u32[]{:S(2)}, u32[]{:S(2)}) collective-permute-start(f32[384,128]{1,0:T(8,128)S(1)} %get-tuple-element.57), channel_id=1, source_target_pairs={{0,1},{1,0},{2,3},{3,2},{4,5},{5,4},{6,7},{7,6},{8,9},{9,8},{10,11... | collective-permute-start | bytes 589832 | tf_op jit(solution)/shard_map/ppermute | solution.py:469
  25.2 1.0 %middle_kernel.1.part = f32[128,384]{1,0:T(8,128)S(1)} custom-call(bf16[512,512]{1,0:T(8,128)(2,1)S(1)} %get-tuple-element.40.a_high, bf16[512,512]{1,0:T(8,128)(2,1)S(1)} %get-tuple-element.41.a_low, f32[128,256]{1,0:T(8,128)S(1)} %get-tuple-element.42.crossed, f32[512,128]{1,0:T(8,128)S(1)} %get-tuple-element.43.own, ...), custom_call_target="tpu_custom_call" | custom-call | tf_op jit(solution)/shard_map/middle_kernel/pallas_call | solution.py:388
  26.2 4.3 %collective-permute-done.2.early = f32[384,128]{1,0:T(8,128)S(1)} collective-permute-done((f32[384,128]{1,0:T(8,128)S(1)}, f32[384,128]{1,0:T(8,128)S(1)}, u32[]{:S(2)}, u32[]{:S(2)}) %collective-permute-start.2) | collective-permute-done | bytes 196640 | tf_op jit(solution)/shard_map/ppermute | solution.py:468
  30.6 1.4 %collective-permute-done.3.late = f32[384,128]{1,0:T(8,128)S(1)} collective-permute-done((f32[384,128]{1,0:T(8,128)S(1)}, f32[384,128]{1,0:T(8,128)S(1)}, u32[]{:S(2)}, u32[]{:S(2)}) %collective-permute-start.3) | collective-permute-done | bytes 196640 | tf_op jit(solution)/shard_map/ppermute | solution.py:469
  32.0 0.7 finish_kernel.1
  32.7 2.0 %collective-permute-start.4 = (f32[41,8,128]{2,1,0:T(8,128)S(1)}, f32[41,8,128]{2,1,0:T(8,128)S(1)}, u32[]{:S(2)}, u32[]{:S(2)}) collective-permute-start(f32[41,8,128]{2,1,0:T(8,128)S(1)} %get-tuple-element.59), channel_id=1, source_target_pairs={{0,4},{1,5},{2,6},{3,7},{4,0},{5,1},{6,2},{7,3},{8,12},{9,13},{10,... | collective-permute-start | bytes 503816 | tf_op jit(solution)/shard_map/ppermute | solution.py:483
  34.7 6.0 %collective-permute-start.5 = (f32[41,8,128]{2,1,0:T(8,128)S(1)}, f32[41,8,128]{2,1,0:T(8,128)S(1)}, u32[]{:S(2)}, u32[]{:S(2)}) collective-permute-start(f32[41,8,128]{2,1,0:T(8,128)S(1)} %get-tuple-element.60), channel_id=1, source_target_pairs={{0,2},{1,3},{2,4},{3,5},{4,6},{5,7},{6,0},{7,1},{8,10},{9,11},{10,... | collective-permute-start | bytes 503816 | tf_op jit(solution)/shard_map/ppermute | solution.py:483
  40.7 1.9 %collective-permute-start.6 = (f32[41,8,128]{2,1,0:T(8,128)S(1)}, f32[41,8,128]{2,1,0:T(8,128)S(1)}, u32[]{:S(2)}, u32[]{:S(2)}) collective-permute-start(f32[41,8,128]{2,1,0:T(8,128)S(1)} %get-tuple-element.61), channel_id=1, source_target_pairs={{0,6},{1,7},{2,0},{3,1},{4,2},{5,3},{6,4},{7,5},{8,14},{9,15},{10,... | collective-permute-start | bytes 503816 | tf_op jit(solution)/shard_map/ppermute | solution.py:483
  42.6 5.5 %collective-permute-start.7 = (f32[41,8,128]{2,1,0:T(8,128)S(1)}, f32[41,8,128]{2,1,0:T(8,128)S(1)}, u32[]{:S(2)}, u32[]{:S(2)}) collective-permute-start(f32[41,8,128]{2,1,0:T(8,128)S(1)} %get-tuple-element.62), channel_id=1, source_target_pairs={{0,3},{1,4},{2,5},{3,6},{4,7},{5,0},{6,1},{7,2},{8,11},{9,12},{10,... | collective-permute-start | bytes 503816 | tf_op jit(solution)/shard_map/ppermute | solution.py:483
  48.1 2.8 %collective-permute-start.8 = (f32[41,8,128]{2,1,0:T(8,128)S(1)}, f32[41,8,128]{2,1,0:T(8,128)S(1)}, u32[]{:S(2)}, u32[]{:S(2)}) collective-permute-start(f32[41,8,128]{2,1,0:T(8,128)S(1)} %get-tuple-element.63), channel_id=1, source_target_pairs={{0,5},{1,6},{2,7},{3,0},{4,1},{5,2},{6,3},{7,4},{8,13},{9,14},{10,... | collective-permute-start | bytes 503816 | tf_op jit(solution)/shard_map/ppermute | solution.py:483
  51.0 3.4 %collective-permute-start.9 = (f32[41,8,128]{2,1,0:T(8,128)S(1)}, f32[41,8,128]{2,1,0:T(8,128)S(1)}, u32[]{:S(2)}, u32[]{:S(2)}) collective-permute-start(f32[41,8,128]{2,1,0:T(8,128)S(1)} %get-tuple-element.66), channel_id=1, source_target_pairs={{0,1},{1,2},{2,3},{3,4},{4,5},{5,6},{6,7},{7,0},{8,9},{9,10},{10,1... | collective-permute-start | bytes 503816 | tf_op jit(solution)/shard_map/ppermute | solution.py:483
  54.4 3.5 %collective-permute-start.10 = (f32[41,8,128]{2,1,0:T(8,128)S(1)}, f32[41,8,128]{2,1,0:T(8,128)S(1)}, u32[]{:S(2)}, u32[]{:S(2)}) collective-permute-start(f32[41,8,128]{2,1,0:T(8,128)S(1)} %get-tuple-element.67), channel_id=1, source_target_pairs={{0,7},{1,0},{2,1},{3,2},{4,3},{5,4},{6,5},{7,6},{8,15},{9,8},{10,9... | collective-permute-start | bytes 503816 | tf_op jit(solution)/shard_map/ppermute | solution.py:483
  57.9 8.1 %collective-permute-done.7.refs_4_ = f32[41,8,128]{2,1,0:T(8,128)S(1)} collective-permute-done((f32[41,8,128]{2,1,0:T(8,128)S(1)}, f32[41,8,128]{2,1,0:T(8,128)S(1)}, u32[]{:S(2)}, u32[]{:S(2)}) %collective-permute-start.7) | collective-permute-done | bytes 167968 | tf_op jit(solution)/shard_map/ppermute | solution.py:483
  66.1 1.0 %unpack_first_kernel.1 = (f32[8,40,8,128]{3,2,1,0:T(8,128)}, f32[1,128]{1,0:T(1,128)S(1)}) custom-call(f32[41,8,128]{2,1,0:T(8,128)S(1)} %get-tuple-element.58.refs_0_, f32[41,8,128]{2,1,0:T(8,128)S(1)} %collective-permute-done.4.refs_1_, f32[41,8,128]{2,1,0:T(8,128)S(1)} %collective-permute-done.5.refs_2_, ...), custom_call_target="tpu_custom_call" | custom-call | tf_op jit(solution)/shard_map/unpack_first_kernel/pallas_call | solution.py:388
  67.1 2.5 %collective-permute-done.10.refs_1_ = f32[41,8,128]{2,1,0:T(8,128)S(1)} collective-permute-done((f32[41,8,128]{2,1,0:T(8,128)S(1)}, f32[41,8,128]{2,1,0:T(8,128)S(1)}, u32[]{:S(2)}, u32[]{:S(2)}) %collective-permute-start.10) | collective-permute-done | bytes 167968 | tf_op jit(solution)/shard_map/ppermute | solution.py:483
  69.6 0.8 %unpack_second_kernel.1 = (f32[8,40,8,128]{3,2,1,0:T(8,128)}, s32[8]{0:T(128)}) custom-call(f32[8,40,8,128]{3,2,1,0:T(8,128)} %get-tuple-element.64.begun, f32[1,128]{1,0:T(1,128)S(1)} %get-tuple-element.65.found, f32[41,8,128]{2,1,0:T(8,128)S(1)} %collective-permute-done.9.refs_0_, ...), custom_call_target="tpu_custom_call", output_to_operand_aliasing={{0}: (0, {})} | custom-call | tf_op jit(solution)/shard_map/unpack_second_kernel/pallas_call | solution.py:388
  (8 shorter events, 0.0 us)
Async XLA Ops:
  2.8 16.2 %collective-permute-start.1 = (f32[840,128]{1,0:T(8,128)S(1)}, f32[840,128]{1,0:T(8,128)S(1)}, u32[]{:S(2)}, u32[]{:S(2)}) collective-permute-start(f32[840,128]{1,0:T(8,128)S(1)} %get-tuple-element.39.up), channel_id=1, source_target_pairs={{0,1},{1,2},{2,3},{3,4},{4,5},{5,6},{6,7},{7,8},{8,9},{9,10},{10,1... | collective-permute-start | bytes 1290248 | tf_op jit(solution)/shard_map/ppermute | solution.py:432
  6.0 8.5 %collective-permute-start = (f32[136,128]{1,0:T(8,128)S(1)}, f32[136,128]{1,0:T(8,128)S(1)}, u32[]{:S(2)}, u32[]{:S(2)}) collective-permute-start(f32[136,128]{1,0:T(8,128)S(1)} %get-tuple-element.48), channel_id=1, source_target_pairs={{1,0},{2,1},{3,2},{4,3},{5,4},{6,5},{7,6},{8,7},{9,8},{10,9},{11,1... | collective-permute-start | bytes 208904 | tf_op jit(solution)/shard_map/ppermute | solution.py:433
  20.3 10.3 %collective-permute-start.2 = (f32[384,128]{1,0:T(8,128)S(1)}, f32[384,128]{1,0:T(8,128)S(1)}, u32[]{:S(2)}, u32[]{:S(2)}) collective-permute-start(f32[384,128]{1,0:T(8,128)S(1)} %get-tuple-element.56), channel_id=1, source_target_pairs={{1,2},{2,1},{3,4},{4,3},{5,6},{6,5},{7,8},{8,7},{9,10},{10,9},{11,... | collective-permute-start | bytes 589832 | tf_op jit(solution)/shard_map/ppermute | solution.py:468
  23.3 8.7 %collective-permute-start.3 = (f32[384,128]{1,0:T(8,128)S(1)}, f32[384,128]{1,0:T(8,128)S(1)}, u32[]{:S(2)}, u32[]{:S(2)}) collective-permute-start(f32[384,128]{1,0:T(8,128)S(1)} %get-tuple-element.57), channel_id=1, source_target_pairs={{0,1},{1,0},{2,3},{3,2},{4,5},{5,4},{6,7},{7,6},{8,9},{9,8},{10,11... | collective-permute-start | bytes 589832 | tf_op jit(solution)/shard_map/ppermute | solution.py:469
  25.2 6.8 %copy-start = (s32[2]{0:T(128)S(1)}, s32[2]{0:T(128)}, u32[]{:S(2)}) copy-start(s32[2]{0:T(128)} %target.1) | copy-start | bytes 28
  32.7 18.3 %collective-permute-start.4 = (f32[41,8,128]{2,1,0:T(8,128)S(1)}, f32[41,8,128]{2,1,0:T(8,128)S(1)}, u32[]{:S(2)}, u32[]{:S(2)}) collective-permute-start(f32[41,8,128]{2,1,0:T(8,128)S(1)} %get-tuple-element.59), channel_id=1, source_target_pairs={{0,4},{1,5},{2,6},{3,7},{4,0},{5,1},{6,2},{7,3},{8,12},{9,13},{10,... | collective-permute-start | bytes 503816 | tf_op jit(solution)/shard_map/ppermute | solution.py:483
  34.7 19.6 %collective-permute-start.5 = (f32[41,8,128]{2,1,0:T(8,128)S(1)}, f32[41,8,128]{2,1,0:T(8,128)S(1)}, u32[]{:S(2)}, u32[]{:S(2)}) collective-permute-start(f32[41,8,128]{2,1,0:T(8,128)S(1)} %get-tuple-element.60), channel_id=1, source_target_pairs={{0,2},{1,3},{2,4},{3,5},{4,6},{5,7},{6,0},{7,1},{8,10},{9,11},{10,... | collective-permute-start | bytes 503816 | tf_op jit(solution)/shard_map/ppermute | solution.py:483
  40.7 17.2 %collective-permute-start.6 = (f32[41,8,128]{2,1,0:T(8,128)S(1)}, f32[41,8,128]{2,1,0:T(8,128)S(1)}, u32[]{:S(2)}, u32[]{:S(2)}) collective-permute-start(f32[41,8,128]{2,1,0:T(8,128)S(1)} %get-tuple-element.61), channel_id=1, source_target_pairs={{0,6},{1,7},{2,0},{3,1},{4,2},{5,3},{6,4},{7,5},{8,14},{9,15},{10,... | collective-permute-start | bytes 503816 | tf_op jit(solution)/shard_map/ppermute | solution.py:483
  42.6 23.4 %collective-permute-start.7 = (f32[41,8,128]{2,1,0:T(8,128)S(1)}, f32[41,8,128]{2,1,0:T(8,128)S(1)}, u32[]{:S(2)}, u32[]{:S(2)}) collective-permute-start(f32[41,8,128]{2,1,0:T(8,128)S(1)} %get-tuple-element.62), channel_id=1, source_target_pairs={{0,3},{1,4},{2,5},{3,6},{4,7},{5,0},{6,1},{7,2},{8,11},{9,12},{10,... | collective-permute-start | bytes 503816 | tf_op jit(solution)/shard_map/ppermute | solution.py:483
  48.1 18.0 %collective-permute-start.8 = (f32[41,8,128]{2,1,0:T(8,128)S(1)}, f32[41,8,128]{2,1,0:T(8,128)S(1)}, u32[]{:S(2)}, u32[]{:S(2)}) collective-permute-start(f32[41,8,128]{2,1,0:T(8,128)S(1)} %get-tuple-element.63), channel_id=1, source_target_pairs={{0,5},{1,6},{2,7},{3,0},{4,1},{5,2},{6,3},{7,4},{8,13},{9,14},{10,... | collective-permute-start | bytes 503816 | tf_op jit(solution)/shard_map/ppermute | solution.py:483
  51.0 16.1 %collective-permute-start.9 = (f32[41,8,128]{2,1,0:T(8,128)S(1)}, f32[41,8,128]{2,1,0:T(8,128)S(1)}, u32[]{:S(2)}, u32[]{:S(2)}) collective-permute-start(f32[41,8,128]{2,1,0:T(8,128)S(1)} %get-tuple-element.66), channel_id=1, source_target_pairs={{0,1},{1,2},{2,3},{3,4},{4,5},{5,6},{6,7},{7,0},{8,9},{9,10},{10,1... | collective-permute-start | bytes 503816 | tf_op jit(solution)/shard_map/ppermute | solution.py:483
  54.4 15.2 %collective-permute-start.10 = (f32[41,8,128]{2,1,0:T(8,128)S(1)}, f32[41,8,128]{2,1,0:T(8,128)S(1)}, u32[]{:S(2)}, u32[]{:S(2)}) collective-permute-start(f32[41,8,128]{2,1,0:T(8,128)S(1)} %get-tuple-element.67), channel_id=1, source_target_pairs={{0,7},{1,0},{2,1},{3,2},{4,3},{5,4},{6,5},{7,6},{8,15},{9,8},{10,9... | collective-permute-start | bytes 503816 | tf_op jit(solution)/shard_map/ppermute | solution.py:483

commit v7 on v6

--- a/solution.py
+++ b/solution.py
@@ -307,7 +307,7 @@
     part[:, 2 * AGG :] = middle[:, 2 * AGG :]
 
 
-def finish_kernel(target, odd, part, early, late, *outs):
+def fill(shifts_out, target, odd, part, early, late, outs):
     here = lax.axis_index("gy")
     first_id = (lax.axis_index("gx") * RB + here) * NA
     upward = odd[:1] == 1
@@ -328,7 +328,7 @@
     ]
     numbers = [jnp.full((8, 2 * BS), first_id + (u + 1), jnp.int32).astype(F32) for u in range(NA)]
     shifts = [(target[u] - here) & (RB - 1) for u in range(NA)]
-    for shift, out in enumerate(outs):
+    for shift, out in zip(shifts_out, outs):
         used = [jnp.full((8, 2 * BS), shifts[u], jnp.int32) == shift for u in range(NA)]
 
         def chosen(first, second):
@@ -340,6 +340,14 @@
                     *[band[c][u * BS + 8 * r : u * BS + 8 * (r + 1)] for u in range(NA)]
                 )
         out[SLOT - 1] = chosen(*numbers)
+
+
+def finish_first_kernel(target, odd, part, early, late, *outs):
+    fill(SHIFTS[:1], target, odd, part, early, late, outs)
+
+
+def finish_rest_kernel(target, odd, part, early, late, *outs):
+    fill((0,) + SHIFTS[1:], target, odd, part, early, late, outs)
 
 
 def unpack(got, shifts, rows, sems, found):
@@ -472,15 +480,19 @@
         on_chip(a_high, a_low, crossed, own, image, right, side, far, moved),
         [(VMEM, (AGG, 3 * AGG), F32)],
     )
-    slots = call(
-        finish_kernel,
-        [(SMEM, target)] + on_chip(odd, part, early, late),
-        [(VMEM, (SLOT, 8, 2 * BS), F32)] * RB,
-    )
-    got = {0: slots[0]}
-    for shift in SHIFTS:
-        pairs = [(i, (i + shift) % RB) for i in range(RB)]
-        got[shift] = lax.ppermute(slots[shift], "gy", pairs)
+    got = {}
+    for kernel, filled in (
+        (finish_first_kernel, SHIFTS[:1]),
+        (finish_rest_kernel, (0,) + SHIFTS[1:]),
+    ):
+        slots = call(
+            kernel,
+            [(SMEM, target)] + on_chip(odd, part, early, late),
+            [(VMEM, (SLOT, 8, 2 * BS), F32)] * len(filled),
+        )
+        for shift, slot in zip(filled, slots):
+            pairs = [(i, (i + shift) % RB) for i in range(RB)]
+            got[shift] = lax.ppermute(slot, "gy", pairs) if shift else slot
     rows_out = (HBM, (RB, SLOT - 1, 8, 2 * BS), F32)
     begun, found = call(
         unpack_first_kernel,

time: 70.8 us -> 71.3 us (level)
  the two profiles are of different devices: /device:TPU:517 before, /device:TPU:199 now
where the time goes in v7:
time: 71.3 us; the launch traced here: 70.7 us
  starting transfers between devices  38.7 us (54%)
  waiting for transfers between devices  18.5 us (26%)
  Pallas kernels  12.7 us (18%)
  between operations  0.81 us (1%)
    ppermute x7, starting transfers between devices, body(): got[shift] = lax.ppermute(slot, 'gy', pairs) if shift else slot  26.4 us
    pallas_call x9, Pallas kernels, call(): pl.pallas_call(kernel, in_specs=[memory for memory, _ in ins], out_specs=...  12.7 us
    ppermute x7, waiting for transfers between devices, body(): got[shift] = lax.ppermute(slot, 'gy', pairs) if shift else slot  9.42 us
    ppermute x1, starting transfers between devices, body(): above = lax.ppermute(down, axes, downward)  4.37 us
    ppermute x1, waiting for transfers between devices, body(): early = lax.ppermute(early, axes, odd_pairs)  4.31 us
    ppermute x1, waiting for transfers between devices, body(): below = lax.ppermute(up, axes, upward)  3.45 us
    ppermute x1, starting transfers between devices, body(): below = lax.ppermute(up, axes, upward)  3.2 us
    ppermute x1, starting transfers between devices, body(): early = lax.ppermute(early, axes, odd_pairs)  2.9 us
  transfers between devices with their start and end apart: 11, of which 7 were waited for; matrix products, arithmetic and copies ran while one was open for 0% of the time, Pallas kernels for 11%

profile of v7, /device:TPU:199, one launch (start us, length us, event | category | flops | bytes accessed | tf_op | source)
XLA Modules:
  0.0 70.7 jit_solution(6130243785904366428)
XLA Ops:
  0.6 2.2 %frame_kernel.1 = (f32[4,6,64,128]{3,2,1,0:T(8,128)S(1)}, f32[512,128]{1,0:T(8,128)S(1)}, s32[8,128]{1,0:T(8,128)S(1)}, f32[840,128]{1,0:T(8,128)S(1)}, f32[136,128]{1,0:T(8,128)S(1)}) custom-call(s32[8,7]{1,0:T(8,128)} %nbr_in.3, s32[8]{0:T(128)} %agg_in.1, f32[8,64,448]{2,1,0:T(8,128)} %blocks_in.3, f32[64,512]{1,0:T(8,128)} %tent_in.1, f32[64,512]{1,0:T(8,128)} %dinv_in.3), custom_call_target="tpu_custom_call" | custom-call | tf_op jit(solution)/shard_map/frame_kernel/pallas_call | solution.py:396
  2.8 3.2 %collective-permute-start.1 = (f32[840,128]{1,0:T(8,128)S(1)}, f32[840,128]{1,0:T(8,128)S(1)}, u32[]{:S(2)}, u32[]{:S(2)}) collective-permute-start(f32[840,128]{1,0:T(8,128)S(1)} %get-tuple-element.38.up), channel_id=1, source_target_pairs={{0,1},{1,2},{2,3},{3,4},{4,5},{5,6},{6,7},{7,8},{8,9},{9,10},{10,1... | collective-permute-start | bytes 1290248 | tf_op jit(solution)/shard_map/ppermute | solution.py:440
  6.0 4.4 %collective-permute-start = (f32[136,128]{1,0:T(8,128)S(1)}, f32[136,128]{1,0:T(8,128)S(1)}, u32[]{:S(2)}, u32[]{:S(2)}) collective-permute-start(f32[136,128]{1,0:T(8,128)S(1)} %get-tuple-element.47), channel_id=1, source_target_pairs={{1,0},{2,1},{3,2},{4,3},{5,4},{6,5},{7,6},{8,7},{9,8},{10,9},{11,1... | collective-permute-start | bytes 208904 | tf_op jit(solution)/shard_map/ppermute | solution.py:441
  10.4 4.1 %own_kernel.1 = (bf16[512,512]{1,0:T(8,128)(2,1)S(1)}, bf16[512,512]{1,0:T(8,128)(2,1)S(1)}, f32[2,256,256]{2,1,0:T(8,128)S(1)}, f32[2,2,256,256]{3,2,1,0:T(8,12...) custom-call(s32[8,7]{1,0:T(8,128)} %nbr_in.3, ...), custom_call_target="tpu_custom_call" | custom-call | tf_op jit(solution)/shard_map/own_kernel/pallas_call | solution.py:396
  14.5 1.1 %above_kernel.1 = (f32[768,128]{1,0:T(8,128)S(1)}, f32[256,128]{1,0:T(8,128)S(1)}, f32[128,256]{1,0:T(8,128)S(1)}) custom-call(bf16[512,512]{1,0:T(8,128)(2,1)S(1)} %get-tuple-element.39.a_high, bf16[512,512]{1,0:T(8,128)(2,1)S(1)} %get-tuple-element.40.a_low, f32[2,256,256]{2,1,0:T(8,128)S(1)} %get-tuple-element.44.factors, ...), custom_call_target="tpu_custom_call" | custom-call | tf_op jit(solution)/shard_map/above_kernel/pallas_call | solution.py:396
  15.7 3.5 %collective-permute-done.1.below = f32[840,128]{1,0:T(8,128)S(1)} collective-permute-done((f32[840,128]{1,0:T(8,128)S(1)}, f32[840,128]{1,0:T(8,128)S(1)}, u32[]{:S(2)}, u32[]{:S(2)}) %collective-permute-start.1) | collective-permute-done | bytes 430112 | tf_op jit(solution)/shard_map/ppermute | solution.py:440
  19.1 1.3 %edge_kernel.1 = (f32[256,128]{1,0:T(8,128)S(1)}, f32[256,256]{1,0:T(8,128)S(1)}, f32[256,256]{1,0:T(8,128)S(1)}, f32[384,128]{1,0:T(8,128)S(1)}, f32[384,128]{1,0:T(8,128)S(1)}) custom-call(s32[8,128]{1,0:T(8,128)S(1)} %get-tuple-element.35.odd, f32[2,2,256,256]{3,2,1,0:T(8,128)S(1)} %get-tuple-element.45.inner, ...), custom_call_target="tpu_custom_call" | custom-call | tf_op jit(solution)/shard_map/edge_kernel/pallas_call | solution.py:396
  20.4 2.9 %collective-permute-start.2 = (f32[384,128]{1,0:T(8,128)S(1)}, f32[384,128]{1,0:T(8,128)S(1)}, u32[]{:S(2)}, u32[]{:S(2)}) collective-permute-start(f32[384,128]{1,0:T(8,128)S(1)} %get-tuple-element.55), channel_id=1, source_target_pairs={{1,2},{2,1},{3,4},{4,3},{5,6},{6,5},{7,8},{8,7},{9,10},{10,9},{11,... | collective-permute-start | bytes 589832 | tf_op jit(solution)/shard_map/ppermute | solution.py:476
  23.3 1.9 %collective-permute-start.3 = (f32[384,128]{1,0:T(8,128)S(1)}, f32[384,128]{1,0:T(8,128)S(1)}, u32[]{:S(2)}, u32[]{:S(2)}) collective-permute-start(f32[384,128]{1,0:T(8,128)S(1)} %get-tuple-element.56), channel_id=1, source_target_pairs={{0,1},{1,0},{2,3},{3,2},{4,5},{5,4},{6,7},{7,6},{8,9},{9,8},{10,11... | collective-permute-start | bytes 589832 | tf_op jit(solution)/shard_map/ppermute | solution.py:477
  25.2 1.0 %middle_kernel.1.part = f32[128,384]{1,0:T(8,128)S(1)} custom-call(bf16[512,512]{1,0:T(8,128)(2,1)S(1)} %get-tuple-element.39.a_high, bf16[512,512]{1,0:T(8,128)(2,1)S(1)} %get-tuple-element.40.a_low, f32[128,256]{1,0:T(8,128)S(1)} %get-tuple-element.41.crossed, f32[512,128]{1,0:T(8,128)S(1)} %get-tuple-element.42.own, ...), custom_call_target="tpu_custom_call" | custom-call | tf_op jit(solution)/shard_map/middle_kernel/pallas_call | solution.py:396
  26.2 4.3 %collective-permute-done.2.early = f32[384,128]{1,0:T(8,128)S(1)} collective-permute-done((f32[384,128]{1,0:T(8,128)S(1)}, f32[384,128]{1,0:T(8,128)S(1)}, u32[]{:S(2)}, u32[]{:S(2)}) %collective-permute-start.2) | collective-permute-done | bytes 196640 | tf_op jit(solution)/shard_map/ppermute | solution.py:476
  30.5 1.3 %collective-permute-done.3.late = f32[384,128]{1,0:T(8,128)S(1)} collective-permute-done((f32[384,128]{1,0:T(8,128)S(1)}, f32[384,128]{1,0:T(8,128)S(1)}, u32[]{:S(2)}, u32[]{:S(2)}) %collective-permute-start.3) | collective-permute-done | bytes 196640 | tf_op jit(solution)/shard_map/ppermute | solution.py:477
  32.5 2.2 %collective-permute-start.4 = (f32[41,8,128]{2,1,0:T(8,128)S(1)}, f32[41,8,128]{2,1,0:T(8,128)S(1)}, u32[]{:S(2)}, u32[]{:S(2)}) collective-permute-start(f32[41,8,128]{2,1,0:T(8,128)S(1)} %finish_first_kernel.1), channel_id=1, source_target_pairs={{0,4},{1,5},{2,6},{3,7},{4,0},{5,1},{6,2},{7,3},{8,12},{9,13},{10,... | collective-permute-start | bytes 503816 | tf_op jit(solution)/shard_map/ppermute | solution.py:495
  35.4 6.4 %collective-permute-start.5 = (f32[41,8,128]{2,1,0:T(8,128)S(1)}, f32[41,8,128]{2,1,0:T(8,128)S(1)}, u32[]{:S(2)}, u32[]{:S(2)}) collective-permute-start(f32[41,8,128]{2,1,0:T(8,128)S(1)} %get-tuple-element.58), channel_id=1, source_target_pairs={{0,2},{1,3},{2,4},{3,5},{4,6},{5,7},{6,0},{7,1},{8,10},{9,11},{10,... | collective-permute-start | bytes 503816 | tf_op jit(solution)/shard_map/ppermute | solution.py:495
  41.8 1.9 %collective-permute-start.6 = (f32[41,8,128]{2,1,0:T(8,128)S(1)}, f32[41,8,128]{2,1,0:T(8,128)S(1)}, u32[]{:S(2)}, u32[]{:S(2)}) collective-permute-start(f32[41,8,128]{2,1,0:T(8,128)S(1)} %get-tuple-element.59), channel_id=1, source_target_pairs={{0,6},{1,7},{2,0},{3,1},{4,2},{5,3},{6,4},{7,5},{8,14},{9,15},{10,... | collective-permute-start | bytes 503816 | tf_op jit(solution)/shard_map/ppermute | solution.py:495
  43.7 7.4 %collective-permute-start.7 = (f32[41,8,128]{2,1,0:T(8,128)S(1)}, f32[41,8,128]{2,1,0:T(8,128)S(1)}, u32[]{:S(2)}, u32[]{:S(2)}) collective-permute-start(f32[41,8,128]{2,1,0:T(8,128)S(1)} %get-tuple-element.60), channel_id=1, source_target_pairs={{0,3},{1,4},{2,5},{3,6},{4,7},{5,0},{6,1},{7,2},{8,11},{9,12},{10,... | collective-permute-start | bytes 503816 | tf_op jit(solution)/shard_map/ppermute | solution.py:495
  51.1 2.0 %collective-permute-start.8 = (f32[41,8,128]{2,1,0:T(8,128)S(1)}, f32[41,8,128]{2,1,0:T(8,128)S(1)}, u32[]{:S(2)}, u32[]{:S(2)}) collective-permute-start(f32[41,8,128]{2,1,0:T(8,128)S(1)} %get-tuple-element.61), channel_id=1, source_target_pairs={{0,5},{1,6},{2,7},{3,0},{4,1},{5,2},{6,3},{7,4},{8,13},{9,14},{10,... | collective-permute-start | bytes 503816 | tf_op jit(solution)/shard_map/ppermute | solution.py:495
  53.0 4.3 %collective-permute-start.9 = (f32[41,8,128]{2,1,0:T(8,128)S(1)}, f32[41,8,128]{2,1,0:T(8,128)S(1)}, u32[]{:S(2)}, u32[]{:S(2)}) collective-permute-start(f32[41,8,128]{2,1,0:T(8,128)S(1)} %get-tuple-element.64), channel_id=1, source_target_pairs={{0,1},{1,2},{2,3},{3,4},{4,5},{5,6},{6,7},{7,0},{8,9},{9,10},{10,1... | collective-permute-start | bytes 503816 | tf_op jit(solution)/shard_map/ppermute | solution.py:495
  57.3 2.2 %collective-permute-start.10 = (f32[41,8,128]{2,1,0:T(8,128)S(1)}, f32[41,8,128]{2,1,0:T(8,128)S(1)}, u32[]{:S(2)}, u32[]{:S(2)}) collective-permute-start(f32[41,8,128]{2,1,0:T(8,128)S(1)} %get-tuple-element.65), channel_id=1, source_target_pairs={{0,7},{1,0},{2,1},{3,2},{4,3},{5,4},{6,5},{7,6},{8,15},{9,8},{10,9... | collective-permute-start | bytes 503816 | tf_op jit(solution)/shard_map/ppermute | solution.py:495
  59.6 4.0 %collective-permute-done.7.refs_4_ = f32[41,8,128]{2,1,0:T(8,128)S(1)} collective-permute-done((f32[41,8,128]{2,1,0:T(8,128)S(1)}, f32[41,8,128]{2,1,0:T(8,128)S(1)}, u32[]{:S(2)}, u32[]{:S(2)}) %collective-permute-start.7) | collective-permute-done | bytes 167968 | tf_op jit(solution)/shard_map/ppermute | solution.py:495
  63.5 2.0 %collective-permute-done.8.refs_5_ = f32[41,8,128]{2,1,0:T(8,128)S(1)} collective-permute-done((f32[41,8,128]{2,1,0:T(8,128)S(1)}, f32[41,8,128]{2,1,0:T(8,128)S(1)}, u32[]{:S(2)}, u32[]{:S(2)}) %collective-permute-start.8) | collective-permute-done | bytes 167968 | tf_op jit(solution)/shard_map/ppermute | solution.py:495
  65.5 1.0 %unpack_first_kernel.1 = (f32[8,40,8,128]{3,2,1,0:T(8,128)}, f32[1,128]{1,0:T(1,128)S(1)}) custom-call(f32[41,8,128]{2,1,0:T(8,128)S(1)} %get-tuple-element.57.refs_0_, f32[41,8,128]{2,1,0:T(8,128)S(1)} %collective-permute-done.4.refs_1_, f32[41,8,128]{2,1,0:T(8,128)S(1)} %collective-permute-done.5.refs_2_, ...), custom_call_target="tpu_custom_call" | custom-call | tf_op jit(solution)/shard_map/unpack_first_kernel/pallas_call | solution.py:396
  66.5 1.2 %collective-permute-done.9.refs_0_ = f32[41,8,128]{2,1,0:T(8,128)S(1)} collective-permute-done((f32[41,8,128]{2,1,0:T(8,128)S(1)}, f32[41,8,128]{2,1,0:T(8,128)S(1)}, u32[]{:S(2)}, u32[]{:S(2)}) %collective-permute-start.9) | collective-permute-done | bytes 167968 | tf_op jit(solution)/shard_map/ppermute | solution.py:495
  67.7 2.3 %collective-permute-done.10.refs_1_ = f32[41,8,128]{2,1,0:T(8,128)S(1)} collective-permute-done((f32[41,8,128]{2,1,0:T(8,128)S(1)}, f32[41,8,128]{2,1,0:T(8,128)S(1)}, u32[]{:S(2)}, u32[]{:S(2)}) %collective-permute-start.10) | collective-permute-done | bytes 167968 | tf_op jit(solution)/shard_map/ppermute | solution.py:495
  (9 shorter events, 2.0 us)
Async XLA Ops:
  2.8 16.3 %collective-permute-start.1 = (f32[840,128]{1,0:T(8,128)S(1)}, f32[840,128]{1,0:T(8,128)S(1)}, u32[]{:S(2)}, u32[]{:S(2)}) collective-permute-start(f32[840,128]{1,0:T(8,128)S(1)} %get-tuple-element.38.up), channel_id=1, source_target_pairs={{0,1},{1,2},{2,3},{3,4},{4,5},{5,6},{6,7},{7,8},{8,9},{9,10},{10,1... | collective-permute-start | bytes 1290248 | tf_op jit(solution)/shard_map/ppermute | solution.py:440
  6.0 8.5 %collective-permute-start = (f32[136,128]{1,0:T(8,128)S(1)}, f32[136,128]{1,0:T(8,128)S(1)}, u32[]{:S(2)}, u32[]{:S(2)}) collective-permute-start(f32[136,128]{1,0:T(8,128)S(1)} %get-tuple-element.47), channel_id=1, source_target_pairs={{1,0},{2,1},{3,2},{4,3},{5,4},{6,5},{7,6},{8,7},{9,8},{10,9},{11,1... | collective-permute-start | bytes 208904 | tf_op jit(solution)/shard_map/ppermute | solution.py:441
  20.4 10.2 %collective-permute-start.2 = (f32[384,128]{1,0:T(8,128)S(1)}, f32[384,128]{1,0:T(8,128)S(1)}, u32[]{:S(2)}, u32[]{:S(2)}) collective-permute-start(f32[384,128]{1,0:T(8,128)S(1)} %get-tuple-element.55), channel_id=1, source_target_pairs={{1,2},{2,1},{3,4},{4,3},{5,6},{6,5},{7,8},{8,7},{9,10},{10,9},{11,... | collective-permute-start | bytes 589832 | tf_op jit(solution)/shard_map/ppermute | solution.py:476
  23.3 8.6 %collective-permute-start.3 = (f32[384,128]{1,0:T(8,128)S(1)}, f32[384,128]{1,0:T(8,128)S(1)}, u32[]{:S(2)}, u32[]{:S(2)}) collective-permute-start(f32[384,128]{1,0:T(8,128)S(1)} %get-tuple-element.56), channel_id=1, source_target_pairs={{0,1},{1,0},{2,3},{3,2},{4,5},{5,4},{6,7},{7,6},{8,9},{9,8},{10,11... | collective-permute-start | bytes 589832 | tf_op jit(solution)/shard_map/ppermute | solution.py:477
  25.2 6.6 %copy-start = (s32[2]{0:T(128)S(1)}, s32[2]{0:T(128)}, u32[]{:S(2)}) copy-start(s32[2]{0:T(128)} %target.3) | copy-start | bytes 28
  32.5 20.6 %collective-permute-start.4 = (f32[41,8,128]{2,1,0:T(8,128)S(1)}, f32[41,8,128]{2,1,0:T(8,128)S(1)}, u32[]{:S(2)}, u32[]{:S(2)}) collective-permute-start(f32[41,8,128]{2,1,0:T(8,128)S(1)} %finish_first_kernel.1), channel_id=1, source_target_pairs={{0,4},{1,5},{2,6},{3,7},{4,0},{5,1},{6,2},{7,3},{8,12},{9,13},{10,... | collective-permute-start | bytes 503816 | tf_op jit(solution)/shard_map/ppermute | solution.py:495
  35.4 22.0 %collective-permute-start.5 = (f32[41,8,128]{2,1,0:T(8,128)S(1)}, f32[41,8,128]{2,1,0:T(8,128)S(1)}, u32[]{:S(2)}, u32[]{:S(2)}) collective-permute-start(f32[41,8,128]{2,1,0:T(8,128)S(1)} %get-tuple-element.58), channel_id=1, source_target_pairs={{0,2},{1,3},{2,4},{3,5},{4,6},{5,7},{6,0},{7,1},{8,10},{9,11},{10,... | collective-permute-start | bytes 503816 | tf_op jit(solution)/shard_map/ppermute | solution.py:495
  41.8 17.8 %collective-permute-start.6 = (f32[41,8,128]{2,1,0:T(8,128)S(1)}, f32[41,8,128]{2,1,0:T(8,128)S(1)}, u32[]{:S(2)}, u32[]{:S(2)}) collective-permute-start(f32[41,8,128]{2,1,0:T(8,128)S(1)} %get-tuple-element.59), channel_id=1, source_target_pairs={{0,6},{1,7},{2,0},{3,1},{4,2},{5,3},{6,4},{7,5},{8,14},{9,15},{10,... | collective-permute-start | bytes 503816 | tf_op jit(solution)/shard_map/ppermute | solution.py:495
  43.7 19.8 %collective-permute-start.7 = (f32[41,8,128]{2,1,0:T(8,128)S(1)}, f32[41,8,128]{2,1,0:T(8,128)S(1)}, u32[]{:S(2)}, u32[]{:S(2)}) collective-permute-start(f32[41,8,128]{2,1,0:T(8,128)S(1)} %get-tuple-element.60), channel_id=1, source_target_pairs={{0,3},{1,4},{2,5},{3,6},{4,7},{5,0},{6,1},{7,2},{8,11},{9,12},{10,... | collective-permute-start | bytes 503816 | tf_op jit(solution)/shard_map/ppermute | solution.py:495
  51.1 14.5 %collective-permute-start.8 = (f32[41,8,128]{2,1,0:T(8,128)S(1)}, f32[41,8,128]{2,1,0:T(8,128)S(1)}, u32[]{:S(2)}, u32[]{:S(2)}) collective-permute-start(f32[41,8,128]{2,1,0:T(8,128)S(1)} %get-tuple-element.61), channel_id=1, source_target_pairs={{0,5},{1,6},{2,7},{3,0},{4,1},{5,2},{6,3},{7,4},{8,13},{9,14},{10,... | collective-permute-start | bytes 503816 | tf_op jit(solution)/shard_map/ppermute | solution.py:495
  53.0 14.7 %collective-permute-start.9 = (f32[41,8,128]{2,1,0:T(8,128)S(1)}, f32[41,8,128]{2,1,0:T(8,128)S(1)}, u32[]{:S(2)}, u32[]{:S(2)}) collective-permute-start(f32[41,8,128]{2,1,0:T(8,128)S(1)} %get-tuple-element.64), channel_id=1, source_target_pairs={{0,1},{1,2},{2,3},{3,4},{4,5},{5,6},{6,7},{7,0},{8,9},{9,10},{10,1... | collective-permute-start | bytes 503816 | tf_op jit(solution)/shard_map/ppermute | solution.py:495
  57.3 12.7 %collective-permute-start.10 = (f32[41,8,128]{2,1,0:T(8,128)S(1)}, f32[41,8,128]{2,1,0:T(8,128)S(1)}, u32[]{:S(2)}, u32[]{:S(2)}) collective-permute-start(f32[41,8,128]{2,1,0:T(8,128)S(1)} %get-tuple-element.65), channel_id=1, source_target_pairs={{0,7},{1,0},{2,1},{3,2},{4,3},{5,4},{6,5},{7,6},{8,15},{9,8},{10,9... | collective-permute-start | bytes 503816 | tf_op jit(solution)/shard_map/ppermute | solution.py:495
